TPU v7x, 128 devices: a whole 4x4x4 slice. The times are simulated.
128 devices in a mesh: grp: 8 (over x_hi, z), mem: 16 (over x_lo, y, core).
Axes of the slice: x: 4 (x_hi: 2, x_lo: 2; x = x_hi * 2 + x_lo), y: 4, z: 4, core: 2. Of those that a mesh axis runs over, the one named last changes fastest.
Arguments:
- tokens: bfloat16 [4096, 8192], P('grp', 'mem'), may hold values from -6 to 6
- base_weight: bfloat16 [8192, 14336], P(None, 'mem'), may hold values from -0.0625 to 0.0625
- adapt_down: bfloat16 [32, 8192, 64], P('grp', 'mem'), may hold values from -0.0625 to 0.0625
- adapt_up: bfloat16 [32, 64, 14336], P('grp', None, 'mem'), may hold values from -0.046875 to 0.046875
- cotangent: bfloat16 [4096, 14336], P('grp', 'mem'), may hold values from -6 to 6
- tenant: int32 [32], replicated, may hold values from 0 to 31
- adapter_slot: int32 [32], replicated, may hold values from 0 to 31, each once
Outputs:
- mixed: bfloat16 [4096, 14336], P('grp', 'mem')
- token_gradient: bfloat16 [4096, 8192], P('grp', 'mem')
- down_grad: bfloat16 [32, 8192, 64], P('grp', 'mem')
- up_grad: bfloat16 [32, 64, 14336], P('grp', None, 'mem')
Inputs may be any that keep to these rules, and one draw needn't show every extreme that they name: `adapter_slot`: each slot is held by exactly one adapter.
All inputs are finite; a program needn't handle non-finite values.
Results may differ from a plain program's by a relative error of at most 0.02.
Values may be sent and summed in bfloat16 or wider, within the bound.
No kernel may reach another device: no remote copies, remote signals or barrier semaphores. Data moves between devices by JAX's collectives and lax.ppermute only.
A program may use at most 128 MiB of HBM per device.

v0:
```python
import jax
import jax.numpy as jnp
from jax import lax
from jax.sharding import PartitionSpec as P

BLK_GRP = 4


adapter_scale = 8.0


def shards(tokens, base_weight, adapt_down, adapt_up, cotangent, tenant, adapter_slot):
    group_index = lax.axis_index("grp")
    blocks = BLK_GRP
    row_total = tokens.shape[0]
    block_length = row_total // blocks
    feature_total = tokens.shape[1]
    hidden_total = cotangent.shape[1]
    adapter_count = adapter_slot.shape[0]
    match_table = tenant[:, None] == jnp.arange(adapter_count, dtype=jnp.int32)[None, :]
    all_slots = jnp.sum(jnp.where(match_table, adapter_slot[None, :], 0), axis=1)
    own_slots = lax.dynamic_slice_in_dim(all_slots, group_index * blocks, blocks)
    stack_down, stack_up = (
        lax.all_gather(adapt_down, "grp", axis=0, tiled=True),
        lax.all_gather(adapt_up, "grp", axis=0, tiled=True),
    )
    down_blocks = jnp.take(stack_down, own_slots, axis=0)
    up_blocks = jnp.take(stack_up, own_slots, axis=0)
    token_blocks = tokens.reshape(blocks, block_length, feature_total)
    cot_blocks = cotangent.reshape(blocks, block_length, hidden_total)
    cot_part = jnp.einsum("kbf,krf->kbr", cot_blocks, up_blocks, preferred_element_type=jnp.float32)
    down_full = lax.all_gather(down_blocks, "mem", axis=1, tiled=True)
    shard_piece = lax.all_gather(tokens, "mem", axis=1, tiled=True)
    width_now = shard_piece.shape[1]
    base_running_sum = jnp.dot(shard_piece, base_weight, preferred_element_type=jnp.float32)
    piece_blocks = shard_piece.reshape(blocks, block_length, width_now)
    low_acc = jnp.einsum(
        "kbd,kdr->kbr", piece_blocks, down_full, preferred_element_type=jnp.float32
    )
    cot_sum = lax.psum(cot_part, "mem")
    low_rank = low_acc.astype(jnp.bfloat16)
    lowrank_output = jnp.einsum(
        "kbr,krf->kbf", low_rank, up_blocks, preferred_element_type=jnp.float32
    )
    mixed = (
        base_running_sum + adapter_scale * lowrank_output.reshape(row_total, hidden_total)
    ).astype(jnp.bfloat16)
    cot_rank = cot_sum.astype(jnp.bfloat16)
    input_terms = lax.dot_general(
        cotangent, base_weight, (((1,), (1,)), ((), ())), preferred_element_type=jnp.float32
    )
    input_portion = lax.psum_scatter(
        input_terms.astype(jnp.bfloat16), "mem", scatter_dimension=1, tiled=True
    ).astype(jnp.float32)
    lowrank_backward = jnp.einsum(
        "kbr,kdr->kbd", cot_rank, down_blocks, preferred_element_type=jnp.float32
    )
    token_gradient = (
        input_portion + adapter_scale * lowrank_backward.reshape(row_total, feature_total)
    ).astype(jnp.bfloat16)
    scaling_factor = adapter_scale / block_length
    grad_down = (
        jnp.einsum("kbd,kbr->kdr", token_blocks, cot_rank, preferred_element_type=jnp.float32)
        * scaling_factor
    )
    grad_up = (
        jnp.einsum("kbr,kbf->krf", low_rank, cot_blocks, preferred_element_type=jnp.float32)
        * scaling_factor
    )
    picker = (own_slots[None, :] == jnp.arange(adapter_count, dtype=jnp.int32)[:, None]).astype(
        jnp.float32
    )
    dense_down = jnp.einsum("nk,kdr->ndr", picker, grad_down, precision=lax.Precision.HIGHEST)
    dense_up = jnp.einsum("nk,krf->nrf", picker, grad_up, precision=lax.Precision.HIGHEST)
    down_grad, up_grad = (
        lax.psum_scatter(dense_down, "grp", scatter_dimension=0, tiled=True),
        lax.psum_scatter(dense_up, "grp", scatter_dimension=0, tiled=True),
    )
    return (mixed, token_gradient, down_grad.astype(jnp.bfloat16), up_grad.astype(jnp.bfloat16))


def solution(mesh):
    in_specs = (
        P("grp", "mem"),
        P(None, "mem"),
        P("grp", "mem", None),
        P("grp", None, "mem"),
        P("grp", "mem"),
        P(),
        P(),
    )
    out_specs = (P("grp", "mem"), P("grp", "mem"), P("grp", "mem", None), P("grp", None, "mem"))
    return jax.shard_map(shards, mesh=mesh, in_specs=in_specs, out_specs=out_specs, check_vma=False)
```

profile of v0, /device:TPU:1, one launch (start us, length us, event | category | flops | bytes accessed | tf_op | source)
XLA Modules:
  0.0 510.4 jit_solution(14840182347897437578)
XLA Ops:
  7.2 0.0 copy-start
  7.2 0.0 all-gather.7.cloned.1.call-start
  7.2 0.7 all-gather.7.cloned.1.call-update
  7.9 0.0 all-gather.11.cloned.1.call-start
  8.0 0.7 all-gather.11.cloned.1.call-update
  8.7 0.0 all-gather.9.cloned.1.call-start
  8.7 0.9 select_reduce_fusion
  9.6 0.1 compare_and_fusion
  9.7 57.7 %all-gather.7.cloned.1.call-done = bf16[32,512,64]{1,2,0:T(8,128)(2,1)} async-done(((bf16[4,512,64]{1,2,0:T(8,128)(2,1)}), bf16[32,512,64]{1,2,0:T(8,128)(2,1)}) %all-gather.7.cloned.1.call-update) | async-done | bytes 2097168 | tf_op jit(solution)/shard_map/all_gather | solution.py:24
  67.4 2.2 gather_fusion
  69.5 0.8 broadcast_select_fusion.1
  70.3 0.0 all-gather.9.cloned.1.call-update
  70.3 0.0 all-gather.5.cloned.1.call-start
  70.4 0.5 all-gather.5.cloned.1.call-update
  70.9 0.0 reduce-scatter.6.cloned.1.call-start
  71.0 63.7 %all-gather.11.cloned.1.call-done = bf16[32,64,896]{2,1,0:T(8,128)(2,1)} async-done(((bf16[4,64,896]{2,1,0:T(8,128)(2,1)}), bf16[32,64,896]{2,1,0:T(8,128)(2,1)}) %all-gather.11.cloned.1.call-update) | async-done | bytes 3670032 | tf_op jit(solution)/shard_map/all_gather | solution.py:25
  134.7 2.7 gather_fusion.1
  137.3 0.0 copy-done
  137.3 0.5 convolution_bitcast_fusion
  137.9 52.1 %all-reduce.1 = bf16[4,128,64]{1,2,0:T(8,128)(2,1)S(1)} all-reduce(f32[4,128,64]{1,2,0:T(8,128)S(1)} %convolution_bitcast_fusion), channel_id=1, replica_groups=mesh['grp'=8,'mem'=16] {'mem'}, use_global_device_ids=true, to_apply=%region_2.3 | all-reduce | flops 32768 | bytes 196608 | tf_op jit(solution)/shard_map/psum | solution.py:40
  190.0 1.3 fusion.1
  191.3 2.0 fusion.5
  193.3 4.5 copy.16
  197.8 0.0 reduce-scatter.6.cloned.1.call-update
  197.8 0.0 reduce-scatter.4.cloned.1.call-start
  197.8 22.0 %convolution_convert_fusion = bf16[512,8192]{1,0:T(8,128)(2,1)} fusion(bf16[512,896]{1,0:T(8,128)(2,1)S(1)} %copy-done, bf16[8192,896]{1,0:T(8,128)(2,1)} %param.8), kind=kOutput, calls=%fused_computation.2 | convolution fusion | flops 7520387072 | bytes 23986176 | tf_op jit(solution)/shard_map/dot_general | solution.py:49
  219.9 0.0 reduce-scatter.4.cloned.1.call-update
  219.9 0.2 reduce-scatter.8.cloned.1.call-start
  220.1 0.0 all-gather.9.cloned.1.call-done
  220.2 7.0 %all-gather.5.cloned.1.call-done = bf16[512,8192]{1,0:T(8,128)(2,1)} async-done(((bf16[512,512]{1,0:T(8,128)(2,1)}), bf16[512,8192]{1,0:T(8,128)(2,1)}) %all-gather.5.cloned.1.call-update) | async-done | bytes 8388624 | tf_op jit(solution)/shard_map/all_gather | solution.py:33
  227.2 7.7 %convolution_convert_fusion.1 = bf16[4,64,128]{2,1,0:T(8,128)(2,1)S(1)} fusion(bf16[4,8192,64]{1,2,0:T(8,128)(2,1)} %all-gather.9.cloned.1.call-done, bf16[4,128,8192]{2,1,0:T(8,128)(2,1)} %bitcast.35), kind=kOutput, calls=%fused_computation.11 | convolution fusion | flops 536903680 | bytes 12648448 | tf_op jit(solution)/shard_map/kbd,kdr->kbr/dot_general | solution.py:37
  234.8 0.3 convolution_multiply_fusion.2
  235.1 3.3 fusion.3
  238.4 7.2 %copy.18 = f32[32,64,896]{2,1,0:T(8,128)} copy(f32[32,64,896]{2,0,1:T(8,128)S(1)} %fusion.3) | data formatting | bytes 14680064 | tf_op jit(solution)/shard_map/nk,krf->nrf/dot_general | solution.py:74
  245.6 0.0 copy-start.2
  245.6 0.0 reduce-scatter.8.cloned.1.call-update
  245.6 0.9 copy-done.2
  246.6 0.3 convolution_multiply_fusion.1
  246.9 68.1 %reduce-scatter.6.cloned.1.call-done = f32[4,512,64]{1,2,0:T(8,128)} async-done(((f32[32,512,64]{1,2,0:T(8,128)}), f32[4,512,64]{1,2,0:T(8,128)}) %reduce-scatter.6.cloned.1.call-update) | async-done | bytes 524304 | tf_op jit(solution)/shard_map/reduce_scatter | solution.py:76
  315.0 1.8 convert_element_type.32
  316.7 0.5 convolution_multiply_fusion
  317.2 0.0 copy-start.1
  317.2 14.7 %fusion = bf16[512,896]{1,0:T(8,128)(2,1)} fusion(f32[4,128,896]{2,1,0:T(8,128)S(1)} %convolution_multiply_fusion, bf16[512,8192]{1,0:T(8,128)(2,1)} %all-gather.5.cloned.1.call-done, bf16[8192,896]{1,0:T(8,128)(2,1)} %param.8), kind=kOutput, calls=%fused_computation.4 | convolution fusion | flops 7517110272 | bytes 25821184 | tf_op jit(solution)/shard_map/dot_general | solution.py:35
  331.9 56.1 %reduce-scatter.4.cloned.1.call-done = bf16[512,512]{1,0:T(8,128)(2,1)} async-done(((bf16[512,8192]{1,0:T(8,128)(2,1)}), bf16[512,512]{1,0:T(8,128)(2,1)}) %reduce-scatter.4.cloned.1.call-update) | async-done | bytes 524304 | tf_op jit(solution)/shard_map/reduce_scatter | solution.py:52
  388.0 2.0 fusion.2
  390.0 111.5 %reduce-scatter.8.cloned.1.call-done = f32[4,64,896]{2,1,0:T(8,128)} async-done(((f32[32,64,896]{2,1,0:T(8,128)}), f32[4,64,896]{2,1,0:T(8,128)}) %reduce-scatter.8.cloned.1.call-update) | async-done | bytes 917520 | tf_op jit(solution)/shard_map/reduce_scatter | solution.py:77
  501.5 2.0 convert_element_type.33
  503.5 0.0 copy-done.1
  (2 shorter events, 0.0 us)
Async XLA Ops:
  7.2 130.2 %copy-start = (bf16[512,896]{1,0:T(8,128)(2,1)S(1)}, bf16[512,896]{1,0:T(8,128)(2,1)}, u32[]{:S(2)}) copy-start(bf16[512,896]{1,0:T(8,128)(2,1)} %param.11) | copy-start | bytes 2752516
  7.2 60.2 %all-gather.7.cloned.1.call-start = ((), (), s32[]{:S(2)}) async-start(), calls=%async_computation.4 | async-start | bytes 2359296 | tf_op jit(solution)/shard_map/all_gather | solution.py:24
  7.9 126.8 %all-gather.11.cloned.1.call-start = ((), (), s32[]{:S(2)}) async-start(), calls=%async_computation.6 | async-start | bytes 4128768 | tf_op jit(solution)/shard_map/all_gather | solution.py:25
  8.7 211.5 %all-gather.9.cloned.1.call-start = ((), (), s32[]{:S(2)}) async-start(), calls=%async_computation.5 | async-start | bytes 4456448 | tf_op jit(solution)/shard_map/all_gather | solution.py:32
  70.3 156.8 %all-gather.5.cloned.1.call-start = ((), (), s32[]{:S(2)}) async-start(), calls=%async_computation.3 | async-start | bytes 8912896 | tf_op jit(solution)/shard_map/all_gather | solution.py:33
  70.9 244.0 %reduce-scatter.6.cloned.1.call-start = ((), (), s32[]{:S(2)}) async-start(), calls=%async_computation.8 | async-start | bytes 4718592 | tf_op jit(solution)/shard_map/reduce_scatter | solution.py:76
  197.8 190.2 %reduce-scatter.4.cloned.1.call-start = ((), (), s32[]{:S(2)}) async-start(), calls=%async_computation.7 | async-start | bytes 8912896 | tf_op jit(solution)/shard_map/reduce_scatter | solution.py:52
  219.9 281.6 %reduce-scatter.8.cloned.1.call-start = ((), (), s32[]{:S(2)}) async-start(), calls=%async_computation.9 | async-start | bytes 8257536 | tf_op jit(solution)/shard_map/reduce_scatter | solution.py:77
  245.6 0.9 copy-start.2
  317.2 186.3 %copy-start.1 = (bf16[512,896]{1,0:T(8,128)(2,1)S(1)}, bf16[512,896]{1,0:T(8,128)(2,1)}, u32[]{:S(2)}) copy-start(bf16[512,896]{1,0:T(8,128)(2,1)} %param.11) | copy-start | bytes 2752516
Sparse Core Ops, SparseCore 0:
  10.4 56.9 all-gather.6
  69.7 64.9 all-gather.10
  136.9 36.3 all-gather.8
  174.9 52.2 all-gather.4
  230.8 84.0 reduce-scatter.5
  317.4 70.5 reduce-scatter.3
  392.3 109.1 reduce-scatter.7
where the time goes:
time: 511 us; the launch traced here: 510 us
  waiting for transfers between devices  366 us (72%)
  matrix products  52.5 us (10%)
  blocking collectives  52.1 us (10%)
  local copies, waits for them, and re-layouts  17.4 us (3%)
  between operations  14.3 us (3%)
  other arithmetic  7.54 us (1%)
    reduce_scatter x1, waiting for transfers between devices, shards(): lax.psum_scatter(dense_up, 'grp', scatter_dimension=0, tiled=True)  112 us
    reduce_scatter x1, waiting for transfers between devices, shards(): lax.psum_scatter(dense_down, 'grp', scatter_dimension=0, tiled=True)  68.1 us
    all_gather x1, waiting for transfers between devices, shards(): lax.all_gather(adapt_up, 'grp', axis=0, tiled=True)  63.7 us
    all_gather x1, waiting for transfers between devices, shards(): lax.all_gather(adapt_down, 'grp', axis=0, tiled=True)  57.7 us
    reduce_scatter x1, waiting for transfers between devices, shards(): lax.psum_scatter(input_terms.astype(jnp.bfloat16), 'mem', scatter_dimensi...  56.1 us
    psum x1, blocking collectives, shards(): cot_sum = lax.psum(cot_part, 'mem')  52.1 us
    dot_general x1, matrix products, shards(): lax.dot_general(cotangent, base_weight, (((1,), (1,)), ((), ())), preferr...  22 us
    dot_general x1, matrix products, shards(): jnp.dot(shard_piece, base_weight, preferred_element_type=jnp.float32)  14.7 us
  transfers between devices with their start and end apart: 7, of which 6 were waited for; matrix products, arithmetic and copies ran while one was open for 15% of the time, Pallas kernels for 0%

commit v1 on v0

v1 whole, which is shorter than its diff:
```python
import functools

import jax
import jax.numpy as jnp
from jax import lax
from jax.experimental import pallas as pl
from jax.experimental.pallas import tpu as pltpu
from jax.sharding import PartitionSpec as P

SCALE = 8.0
GRP, XL, YY, CORES = 8, 2, 4, 2
BLK = 4
F32, BF16 = jnp.float32, jnp.bfloat16
VMEM = pl.BlockSpec(memory_space=pltpu.VMEM)
SMEM = pl.BlockSpec(memory_space=pltpu.SMEM)
ANY = pl.BlockSpec(memory_space=pl.ANY)
LIMIT = 50 * 1024 * 1024


def mem_perm(move):
    pairs = []
    for x in range(XL):
        for y in range(YY):
            for c in range(CORES):
                tx, ty, tc = move(x, y, c)
                pairs.append(((x * YY + y) * CORES + c, (tx * YY + ty % YY) * CORES + tc))
    return pairs


def way(c):
    return 1 - 2 * c


MOVES = {
    "core": mem_perm(lambda x, y, c: (x, y, 1 - c)),
    "x": mem_perm(lambda x, y, c: (1 - x, y, c)),
    "fwd": mem_perm(lambda x, y, c: (x, y + way(c), c)),
    "back": mem_perm(lambda x, y, c: (x, y - way(c), c)),
    "far": mem_perm(lambda x, y, c: (x, y + 2, c)),
}


def send(value, move):
    return lax.ppermute(value, "mem", MOVES[move])


def exchange(pieces):
    return [pieces[0]] + [
        lax.ppermute(pieces[i], "grp", [(g, g ^ i) for g in range(GRP)]) for i in (2, 6, 4, 7, 5, 3, 1)
    ]


def ordered(received):
    order = (0, 2, 6, 4, 7, 5, 3, 1)
    return [received[order.index(i)] for i in range(GRP)]


def params(**kw):
    return pltpu.CompilerParams(vmem_limit_bytes=LIMIT, **kw)


def cut_kernel(group, down, up, *outs):
    width = down.shape[-1]
    for i in range(GRP):
        piece = group[0] ^ i
        for b in range(BLK):
            outs[i][b, :, :width] = down[b, piece]
            outs[i][b, :, width:] = up[b, piece]


def pick_kernel(index, *refs):
    ins, outs, held = refs[:GRP], refs[GRP : 2 * GRP], refs[2 * GRP]
    for i in range(GRP):
        held[BLK * i : BLK * (i + 1)] = ins[i][...]
    for i in range(GRP):
        for b in range(BLK):
            outs[i][b] = held[index[BLK * i + b]]


def rank_kernel(tokens, cot, *refs):
    ins, adapters, part = refs[:GRP], refs[GRP], refs[GRP + 1]
    width = tokens.shape[1]
    rows = tokens.shape[0] // BLK
    rank = adapters.shape[1]
    for b in range(BLK):
        whole = jnp.concatenate([ins[i][b].astype(F32) for i in range(GRP)], axis=0).astype(BF16)
        adapters[b] = whole
        span = slice(b * rows, (b + 1) * rows)
        dims = (((1,), (1,)), ((), ()))
        part[span, :rank] = lax.dot_general(tokens[span, :], whole[:, :width], dims, preferred_element_type=F32)
        part[span, rank:] = lax.dot_general(cot[span, :], whole[:, width:], dims, preferred_element_type=F32)


def grad_kernel(tokens, cot, ranks, *outs):
    width = tokens.shape[1]
    rows = tokens.shape[0] // BLK
    rank = ranks.shape[1] // 2
    piece = rank // GRP
    factor = SCALE / rows
    dims = (((0,), (0,)), ((), ()))
    for b in range(BLK):
        span = slice(b * rows, (b + 1) * rows)
        both = ranks[span, :]
        low, back = both[:, :rank], both[:, rank:]
        down = lax.dot_general(back, tokens[span, :], dims, preferred_element_type=F32) * factor
        up = lax.dot_general(low, cot[span, :], dims, preferred_element_type=F32) * factor
        for i in range(GRP):
            part = slice(i * piece, (i + 1) * piece)
            outs[i][b, :, :width] = down[part].astype(BF16)
            outs[i][b, :, width:] = up[part].astype(BF16)


def total_kernel(index, *refs):
    ins, outs, total = refs[:GRP], refs[GRP : 2 * GRP], refs[2 * GRP]
    total[...] = jnp.zeros_like(total)
    for i in range(GRP):
        for b in range(BLK):
            slot = index[BLK * i + b]
            total[slot] = total[slot] + ins[i][b].astype(F32)
    for i in range(GRP):
        outs[i][...] = total[BLK * i : BLK * (i + 1)].astype(BF16)


def join_kernel(group, *refs):
    ins, down, up = refs[:GRP], refs[GRP], refs[GRP + 1]
    width = down.shape[-1]
    for i in range(GRP):
        piece = group[0] ^ i
        for b in range(BLK):
            down[b, piece] = ins[i][b, :, :width]
            up[b, piece] = ins[i][b, :, width:]


def copy_kernel(order, source, out):
    out[...] = source[...]


def back_kernel(order, cot, cot_pair, own, pair, *outs):
    i = pl.program_id(0)
    dims = (((1,), (1,)), ((), ()))
    value = lax.dot_general(cot[...], own[0], dims, preferred_element_type=F32)
    value += lax.dot_general(cot_pair[...], pair[0], dims, preferred_element_type=F32)
    value = value.astype(BF16)
    for k in range(len(outs)):

        @pl.when(i == k)
        def _():
            outs[k][...] = value


def ahead_kernel(count, first, order, *refs):
    shards, refs = refs[:count], refs[count:]
    if first:
        own, pair, out_own, out_pair, held, sems = refs
    else:
        own, pair, start_own, start_pair, out_own, out_pair, held, sems = refs
    i = pl.program_id(0)
    copies = [pltpu.make_async_copy(shards[k], held.at[k], sems.at[k]) for k in range(count)]

    @pl.when(i == 0)
    def _():
        for copy in copies:
            copy.start()
        out_own[...] = jnp.zeros_like(out_own) if first else start_own[...]
        out_pair[...] = jnp.zeros_like(out_pair) if first else start_pair[...]

    for k in range(count):

        @pl.when(i == k)
        def _():
            copies[k].wait()

    shard = held[i]
    out_own[...] += jnp.dot(shard, own[0], preferred_element_type=F32)
    out_pair[...] += jnp.dot(shard, pair[0], preferred_element_type=F32)


def ahead(shards, weight, pair, order, start):
    count = len(shards)
    rows, depth = shards[0].shape
    wide = weight.shape[2]
    first = start is None
    total = pl.BlockSpec((rows, wide), lambda i, order: (0, 0))
    block = (1, depth, wide)
    specs = [ANY] * count + [
        pl.BlockSpec(block, lambda i, order: (order[i], 0, 0)),
        pl.BlockSpec(block, lambda i, order: (i, 0, 0)),
    ]
    if not first:
        specs += [total, total]
    return pl.pallas_call(
        functools.partial(ahead_kernel, count, first),
        grid_spec=pltpu.PrefetchScalarGridSpec(
            num_scalar_prefetch=1,
            grid=(count,),
            in_specs=specs,
            out_specs=[total, total],
            scratch_shapes=[pltpu.VMEM((count, rows, depth), BF16), pltpu.SemaphoreType.DMA((count,))],
        ),
        out_shape=[jax.ShapeDtypeStruct((rows, wide), F32)] * 2,
        compiler_params=params(),
        cost_estimate=pl.CostEstimate(
            flops=4 * count * rows * depth * wide, bytes_accessed=4 * count * depth * wide, transcendentals=0
        ),
        name="ahead",
    )(order, *shards, weight, pair, *(() if first else start))


def take_blocks(weight, order):
    count = order.shape[0]
    block = (1,) + weight.shape[1:]
    return pl.pallas_call(
        copy_kernel,
        grid_spec=pltpu.PrefetchScalarGridSpec(
            num_scalar_prefetch=1,
            grid=(count,),
            in_specs=[pl.BlockSpec(block, lambda i, order: (order[i], 0, 0))],
            out_specs=pl.BlockSpec(block, lambda i, order: (i, 0, 0)),
        ),
        out_shape=jax.ShapeDtypeStruct((count,) + weight.shape[1:], BF16),
        compiler_params=params(),
        name="take_blocks",
    )(order, weight)


def backward(cot, cot_pair, weight, pair, order):
    count = order.shape[0]
    rows, wide = cot.shape
    depth = weight.shape[1]
    block = (1, depth, wide)
    whole = pl.BlockSpec((rows, wide), lambda i, order: (0, 0))
    return pl.pallas_call(
        back_kernel,
        grid_spec=pltpu.PrefetchScalarGridSpec(
            num_scalar_prefetch=1,
            grid=(count,),
            in_specs=[
                whole,
                whole,
                pl.BlockSpec(block, lambda i, order: (order[i], 0, 0)),
                pl.BlockSpec(block, lambda i, order: (i, 0, 0)),
            ],
            out_specs=[pl.BlockSpec((rows, depth), lambda i, order: (0, 0))] * count,
        ),
        out_shape=[jax.ShapeDtypeStruct((rows, depth), BF16)] * count,
        compiler_params=params(),
        cost_estimate=pl.CostEstimate(
            flops=4 * count * rows * depth * wide, bytes_accessed=4 * count * depth * wide, transcendentals=0
        ),
        name="backward",
    )(order, cot, cot_pair, weight, pair)


def plus(*terms):
    total = terms[0].astype(F32)
    for term in terms[1:]:
        total = total + term.astype(F32)
    return total


def shards(tokens, base_weight, adapt_down, adapt_up, cotangent, tenant, adapter_slot):
    group = lax.axis_index("grp").astype(jnp.int32)
    member = lax.axis_index("mem").astype(jnp.int32)
    core, y, x = member % 2, (member // 2) % YY, member // (2 * YY)
    rows, feats = tokens.shape
    hidden = cotangent.shape[1]
    per_group, _, rank = adapt_down.shape
    piece = rank // GRP
    groups = jnp.arange(GRP, dtype=jnp.int32) ^ group

    match = tenant[:, None] == jnp.arange(adapter_slot.shape[0], dtype=jnp.int32)[None, :]
    slots = jnp.sum(jnp.where(match, adapter_slot[None, :], 0), axis=1)
    blocks = (groups[:, None] * BLK + jnp.arange(BLK, dtype=jnp.int32)[None, :]).reshape(-1)
    mine = jnp.sum(
        jnp.where(blocks[:, None] == jnp.arange(slots.shape[0], dtype=jnp.int32)[None, :], slots[None, :], 0), axis=1
    )
    index = ((mine // per_group) ^ group) * per_group + mine % per_group

    def block_order(c):
        d = 1 - 2 * c
        steps = ((0, 0), (1, 0), (0, -d), (0, d), (1, -d), (1, d), (0, 2), (1, 2))
        return jnp.stack([((x ^ dx) * YY + (y + dy + YY) % YY) * 2 + c for dx, dy in steps]).astype(jnp.int32)

    order, pair_order = block_order(core), block_order(1 - core)

    piece_shape = jax.ShapeDtypeStruct((per_group, piece, feats + hidden), BF16)
    down_t = jnp.swapaxes(adapt_down, 1, 2)
    group1 = group[None]

    cut = pl.pallas_call(
        cut_kernel,
        in_specs=[SMEM, VMEM, VMEM],
        out_specs=[VMEM] * GRP,
        out_shape=[piece_shape] * GRP,
        compiler_params=params(),
        name="cut",
    )(group1, down_t.reshape(per_group, GRP, piece, feats), adapt_up.reshape(per_group, GRP, piece, hidden))
    got = ordered(exchange(cut))

    t_x = send(tokens, "x")
    t_f = send(tokens, "fwd")
    t_b = send(tokens, "back")
    cot_pair = send(cotangent, "core")

    weight = base_weight.reshape(2 * XL * YY, feats, hidden)
    half = order.shape[0] // 2
    pair_w = [send(take_blocks(weight, pair_order[k : k + half]), "core") for k in (0, half)]

    t_ff = send(t_f, "fwd")
    t_xf = send(t_x, "fwd")
    t_xb = send(t_x, "back")
    t_xff = send(t_ff, "x")

    picked = pl.pallas_call(
        pick_kernel,
        in_specs=[SMEM] + [VMEM] * GRP,
        out_specs=[VMEM] * GRP,
        out_shape=[piece_shape] * GRP,
        scratch_shapes=[pltpu.VMEM((GRP * per_group, piece, feats + hidden), BF16)],
        compiler_params=params(),
        name="pick",
    )(index, *got)
    own_adapters = ordered(exchange(picked))
    adapters, part = pl.pallas_call(
        rank_kernel,
        in_specs=[VMEM] * (2 + GRP),
        out_specs=[VMEM] * 2,
        out_shape=[
            jax.ShapeDtypeStruct((BLK, rank, feats + hidden), BF16),
            jax.ShapeDtypeStruct((rows, 2 * rank), F32),
        ],
        compiler_params=params(),
        name="rank",
    )(tokens, cotangent, *own_adapters)

    parts = []
    for k in (0, half):
        parts += backward(cotangent, cot_pair, weight, pair_w[k // half], order[k : k + half])

    middle = rows // 2
    keep = jnp.where(core == 0, part[:middle], part[middle:])
    give = jnp.where(core == 0, part[middle:], part[:middle])
    chip = (keep + send(give, "core")).astype(BF16)
    two = plus(chip, send(chip, "x")).astype(BF16)
    half_sum = plus(two, send(two, "fwd"), send(two, "back"), send(two, "far")).astype(BF16)
    other = send(half_sum, "core")
    ranks = jnp.concatenate(
        [jnp.where(core == 0, half_sum, other), jnp.where(core == 0, other, half_sum)], axis=0
    )

    grads = pl.pallas_call(
        grad_kernel,
        in_specs=[VMEM] * 3,
        out_specs=[VMEM] * GRP,
        out_shape=[piece_shape] * GRP,
        compiler_params=params(),
        name="grads",
    )(tokens, cotangent, ranks)
    got = ordered(exchange(grads))
    totals = pl.pallas_call(
        total_kernel,
        in_specs=[SMEM] + [VMEM] * GRP,
        out_specs=[VMEM] * GRP,
        out_shape=[piece_shape] * GRP,
        scratch_shapes=[pltpu.VMEM((GRP * per_group, piece, feats + hidden), F32)],
        compiler_params=params(),
        name="total",
    )(index, *got)
    final = ordered(exchange(totals))
    down_grad, up_grad = pl.pallas_call(
        join_kernel,
        in_specs=[SMEM] + [VMEM] * GRP,
        out_specs=[VMEM] * 2,
        out_shape=[
            jax.ShapeDtypeStruct((per_group, GRP, piece, feats), BF16),
            jax.ShapeDtypeStruct((per_group, GRP, piece, hidden), BF16),
        ],
        compiler_params=params(),
        name="join",
    )(group1, *final)
    down_grad = jnp.swapaxes(down_grad.reshape(per_group, rank, feats), 1, 2)
    up_grad = up_grad.reshape(per_group, rank, hidden)

    g00, g10, g0b, g0f, g1b, g1f, g02, g12 = parts
    r_12 = send(g12, "x")
    r_1b = send(g1b, "back")
    r_1f = send(g1f, "fwd")
    r_0f = send(g0f, "fwd")
    r_02 = send(plus(g02, r_12).astype(BF16), "back")
    r_10 = send(plus(g10, r_1b, r_1f).astype(BF16), "x")
    r_0b = send(plus(g0b, r_02).astype(BF16), "back")
    cot_rank = ranks[:, rank:].reshape(BLK, rows // BLK, rank)
    low_rank = ranks[:, :rank].reshape(BLK, rows // BLK, rank)
    low_back = jnp.einsum("kbr,krd->kbd", cot_rank, adapters[:, :, :feats], preferred_element_type=F32)
    token_gradient = (plus(g00, r_0f, r_10, r_0b) + SCALE * low_back.reshape(rows, feats)).astype(BF16)

    first = ahead([tokens, t_x, t_f, t_b], weight, pair_w[0], order[:half], None)
    own_sum, pair_sum = ahead([t_xf, t_xb, t_ff, t_xff], weight, pair_w[1], order[half:], first)
    from_pair = send(pair_sum.astype(BF16), "core")
    low_out = jnp.einsum("kbr,krf->kbf", low_rank, adapters[:, :, feats:], preferred_element_type=F32)
    mixed = (own_sum + from_pair.astype(F32) + SCALE * low_out.reshape(rows, hidden)).astype(BF16)
    return mixed, token_gradient, down_grad, up_grad


def solution(mesh):
    in_specs = (
        P("grp", "mem"),
        P(None, "mem"),
        P("grp", "mem", None),
        P("grp", None, "mem"),
        P("grp", "mem"),
        P(),
        P(),
    )
    out_specs = (P("grp", "mem"), P("grp", "mem"), P("grp", "mem", None), P("grp", None, "mem"))
    return jax.shard_map(shards, mesh=mesh, in_specs=in_specs, out_specs=out_specs, check_vma=False)
```

time: 511 us -> 203 us (0.40)
  waiting for transfers between devices: 366 us -> 44.8 us
  starting transfers between devices: 0.46 us -> 92.3 us
  blocking collectives: 52.1 us -> 0 us
  matrix products: 52.5 us -> 0.65 us
  Pallas kernels: 0 us -> 49.1 us
  between operations: 14.3 us -> 1.07 us
  local copies, waits for them, and re-layouts: 17.4 us -> 5.96 us
    reduce_scatter x3 -> x0, waiting for transfers between devices: 236 us -> none  [the longest x1 112 us: shards(): lax.psum_scatter(dense_up, 'grp', scatter_dimension=0, tiled=True)]
    all_gather x4 -> x0, waiting for transfers between devices: 128 us -> none  [the longest x1 63.7 us: shards(): lax.all_gather(adapt_up, 'grp', axis=0, tiled=True)]
    ppermute x0 -> x52, starting transfers between devices: none -> 92.3 us  [the longest x28 51.9 us: exchange(): lax.ppermute(pieces[i], 'grp', [(g, g ^ i) for g in range(GRP)])]
    psum x1 -> x0, blocking collectives: 52.1 us -> none  [shards(): cot_sum = lax.psum(cot_part, 'mem')]
    dot_general x10 -> x2, matrix products: 52.5 us -> 0.65 us  [the longest x1 0.38 us: shards(): jnp.einsum('kbr,krf->kbf', low_rank, adapters[:, :, feats:], preferred_el...]
    pallas_call x0 -> x12, Pallas kernels: none -> 49.1 us  [the longest x2 19.2 us: ahead(): pl.pallas_call(functools.partial(ahead_kernel, count, first), grid_spec=p...]
    ppermute x0 -> x52, waiting for transfers between devices: none -> 44.8 us  [the longest x28 26.2 us: exchange(): lax.ppermute(pieces[i], 'grp', [(g, g ^ i) for g in range(GRP)])]
    dot_general x2 -> x0, local copies, waits for them, and re-layouts: 11.7 us -> none  [the longest x1 7.18 us: shards(): jnp.einsum('nk,krf->nrf', picker, grad_up, precision=lax.Precision.HIGHEST)]
  transfers between devices with their start and end apart: 7 -> 52, of which waited for: 6 -> 21; matrix products, arithmetic and copies ran while one was open for 15% -> 4% of each run, Pallas kernels for 0% -> 22%
where the time goes in v1:
time: 203 us
  starting transfers between devices  92.3 us (45%)
  Pallas kernels  49.1 us (24%)
  waiting for transfers between devices  44.8 us (22%)
  other arithmetic  8.76 us (4%)
  local copies, waits for them, and re-layouts  5.96 us (3%)
    ppermute x28, starting transfers between devices, exchange(): lax.ppermute(pieces[i], 'grp', [(g, g ^ i) for g in range(GRP)])  51.9 us
    ppermute x24, starting transfers between devices, send(): return lax.ppermute(value, 'mem', MOVES[move])  40.4 us
    ppermute x28, waiting for transfers between devices, exchange(): lax.ppermute(pieces[i], 'grp', [(g, g ^ i) for g in range(GRP)])  26.2 us
    pallas_call x2, Pallas kernels, ahead(): pl.pallas_call(functools.partial(ahead_kernel, count, first), grid_spec=p...  19.2 us
    ppermute x24, waiting for transfers between devices, send(): return lax.ppermute(value, 'mem', MOVES[move])  18.6 us
    pallas_call x2, Pallas kernels, backward(): pl.pallas_call(back_kernel, grid_spec=pltpu.PrefetchScalarGridSpec(num_sc...  15.1 us
    pallas_call x2, Pallas kernels, take_blocks(): pl.pallas_call(copy_kernel, grid_spec=pltpu.PrefetchScalarGridSpec(num_sc...  10.1 us
    unnamed x36, local copies, waits for them, and re-layouts  5.88 us
  transfers between devices with their start and end apart: 52, of which 21 were waited for; matrix products, arithmetic and copies ran while one was open for 4% of the time, Pallas kernels for 22%

profile of v1, /device:TPU:1, one launch (start us, length us, event | category | flops | bytes accessed | tf_op | source)
XLA Modules:
  0.0 202.6 jit_solution(6918037534149747447)
XLA Ops:
  0.8 5.0 %take_blocks.2 = bf16[4,512,896]{2,1,0:T(8,128)(2,1)} custom-call(s32[4]{0:T(128)S(1)} %pad_add_fusion.1.order, bf16[16,512,896]{2,1,0:T(8,128)(2,1)} %bitcast.40), custom_call_target="tpu_custom_call" | custom-call | tf_op jit(solution)/shard_map/take_blocks/pallas_call | solution.py:212
  5.9 1.4 collective-permute-start.6
  7.3 1.8 collective-permute-start.10
  9.1 3.3 %collective-permute-start.11 = (bf16[4,8,1408]{2,1,0:T(8,128)(2,1)S(1)}, bf16[4,8,1408]{2,1,0:T(8,128)(2,1)S(1)}, u32[]{:S(2)}, u32[]{:S(2)}) collective-permute-start(bf16[4,8,1408]{2,1,0:T(8,128)(2,1)S(1)} %get-tuple-element.58), channel_id=1, source_target_pairs={{0,32},{16,48},{32,0},{48,16},{64,96},{80,112},{96,64},{112,80},{1... | collective-permute-start | bytes 270344 | tf_op jit(solution)/shard_map/ppermute | solution.py:49
  12.5 5.0 %take_blocks.3 = bf16[4,512,896]{2,1,0:T(8,128)(2,1)} custom-call(s32[4]{0:T(128)S(1)} %pad_add_fusion.3.order, bf16[16,512,896]{2,1,0:T(8,128)(2,1)} %bitcast.41), custom_call_target="tpu_custom_call" | custom-call | tf_op jit(solution)/shard_map/take_blocks/pallas_call | solution.py:212
  18.5 2.8 %collective-permute-start.13 = (bf16[4,8,1408]{2,1,0:T(8,128)(2,1)S(1)}, bf16[4,8,1408]{2,1,0:T(8,128)(2,1)S(1)}, u32[]{:S(2)}, u32[]{:S(2)}) collective-permute-start(bf16[4,8,1408]{2,1,0:T(8,128)(2,1)S(1)} %get-tuple-element.60), channel_id=1, source_target_pairs={{0,64},{16,80},{32,96},{48,112},{64,0},{80,16},{96,32},{112,48},{1... | collective-permute-start | bytes 270344 | tf_op jit(solution)/shard_map/ppermute | solution.py:49
  21.6 6.5 %collective-permute-start.15 = (bf16[4,8,1408]{2,1,0:T(8,128)(2,1)S(1)}, bf16[4,8,1408]{2,1,0:T(8,128)(2,1)S(1)}, u32[]{:S(2)}, u32[]{:S(2)}) collective-permute-start(bf16[4,8,1408]{2,1,0:T(8,128)(2,1)S(1)} %get-tuple-element.62), channel_id=1, source_target_pairs={{0,96},{16,112},{32,64},{48,80},{64,32},{80,48},{96,0},{112,16},{1... | collective-permute-start | bytes 270344 | tf_op jit(solution)/shard_map/ppermute | solution.py:49
  28.1 1.6 collective-permute-start.16
  29.8 2.8 %collective-permute-done.15.refs_6_ = bf16[4,8,1408]{2,1,0:T(8,128)(2,1)S(1)} collective-permute-done((bf16[4,8,1408]{2,1,0:T(8,128)(2,1)S(1)}, bf16[4,8,1408]{2,1,0:T(8,128)(2,1)S(1)}, u32[]{:S(2)}, u32[]{:S(2)}) %collective-permute-start.15) | collective-permute-done | bytes 90144 | tf_op jit(solution)/shard_map/ppermute | solution.py:49
  32.5 2.6 %collective-permute-done.16.refs_7_ = bf16[4,8,1408]{2,1,0:T(8,128)(2,1)S(1)} collective-permute-done((bf16[4,8,1408]{2,1,0:T(8,128)(2,1)S(1)}, bf16[4,8,1408]{2,1,0:T(8,128)(2,1)S(1)}, u32[]{:S(2)}, u32[]{:S(2)}) %collective-permute-start.16) | collective-permute-done | bytes 90144 | tf_op jit(solution)/shard_map/ppermute | solution.py:49
  36.8 3.0 %collective-permute-start.19 = (bf16[4,8,1408]{2,1,0:T(8,128)(2,1)S(1)}, bf16[4,8,1408]{2,1,0:T(8,128)(2,1)S(1)}, u32[]{:S(2)}, u32[]{:S(2)}) collective-permute-start(bf16[4,8,1408]{2,1,0:T(8,128)(2,1)S(1)} %get-tuple-element.67), channel_id=1, source_target_pairs={{0,48},{16,32},{32,16},{48,0},{64,112},{80,96},{96,80},{112,64},{1... | collective-permute-start | bytes 270344 | tf_op jit(solution)/shard_map/ppermute | solution.py:49
  39.9 1.6 collective-permute-done.18.refs_2_
  41.5 1.3 collective-permute-start.21
  42.8 3.4 %collective-permute-start.22 = (bf16[4,8,1408]{2,1,0:T(8,128)(2,1)S(1)}, bf16[4,8,1408]{2,1,0:T(8,128)(2,1)S(1)}, u32[]{:S(2)}, u32[]{:S(2)}) collective-permute-start(bf16[4,8,1408]{2,1,0:T(8,128)(2,1)S(1)} %get-tuple-element.70), channel_id=1, source_target_pairs={{0,96},{16,112},{32,64},{48,80},{64,32},{80,48},{96,0},{112,16},{1... | collective-permute-start | bytes 270344 | tf_op jit(solution)/shard_map/ppermute | solution.py:49
  46.2 2.5 %collective-permute-start.23 = (bf16[4,8,1408]{2,1,0:T(8,128)(2,1)S(1)}, bf16[4,8,1408]{2,1,0:T(8,128)(2,1)S(1)}, u32[]{:S(2)}, u32[]{:S(2)}) collective-permute-start(bf16[4,8,1408]{2,1,0:T(8,128)(2,1)S(1)} %get-tuple-element.71), channel_id=1, source_target_pairs={{0,112},{16,96},{32,80},{48,64},{64,48},{80,32},{96,16},{112,0},{1... | collective-permute-start | bytes 270344 | tf_op jit(solution)/shard_map/ppermute | solution.py:49
  48.7 1.4 collective-permute-done.22.refs_6_
  50.1 3.5 %collective-permute-done.23.refs_7_ = bf16[4,8,1408]{2,1,0:T(8,128)(2,1)S(1)} collective-permute-done((bf16[4,8,1408]{2,1,0:T(8,128)(2,1)S(1)}, bf16[4,8,1408]{2,1,0:T(8,128)(2,1)S(1)}, u32[]{:S(2)}, u32[]{:S(2)}) %collective-permute-start.23) | collective-permute-done | bytes 90144 | tf_op jit(solution)/shard_map/ppermute | solution.py:49
  54.2 4.6 %collective-permute-start.24 = (f32[256,128]{1,0:T(8,128)S(1)}, f32[256,128]{1,0:T(8,128)S(1)}, u32[]{:S(2)}, u32[]{:S(2)}) collective-permute-start(f32[256,128]{1,0:T(8,128)S(1)} %slice_select_fusion), channel_id=1, source_target_pairs={{0,1},{1,0},{2,3},{3,2},{4,5},{5,4},{6,7},{7,6},{8,9},{9,8},{10,11... | collective-permute-start | bytes 393224 | tf_op jit(solution)/shard_map/ppermute | solution.py:44
  58.9 1.0 collective-permute-done.24
  60.3 2.8 %collective-permute-done.25 = bf16[256,128]{1,0:T(8,128)(2,1)S(1)} collective-permute-done((bf16[256,128]{1,0:T(8,128)(2,1)S(1)}, bf16[256,128]{1,0:T(8,128)(2,1)S(1)}, u32[]{:S(2)}, u32[]{:S(2)}) %collective-permute-start.25) | collective-permute-done | bytes 65568 | tf_op jit(solution)/shard_map/ppermute | solution.py:44
  63.1 2.8 %collective-permute-start.26 = (bf16[256,128]{1,0:T(8,128)(2,1)S(1)}, bf16[256,128]{1,0:T(8,128)(2,1)S(1)}, u32[]{:S(2)}, u32[]{:S(2)}) collective-permute-start(bf16[256,128]{1,0:T(8,128)(2,1)S(1)} %add_convert_fusion.4), channel_id=1, source_target_pairs={{0,2},{1,7},{2,4},{3,1},{4,6},{5,3},{6,0},{7,5},{8,10},{9,15},{10,... | collective-permute-start | bytes 196616 | tf_op jit(solution)/shard_map/ppermute | solution.py:44
  65.9 1.6 collective-permute-start.28
  67.9 2.9 %collective-permute-done.27 = bf16[256,128]{1,0:T(8,128)(2,1)S(1)} collective-permute-done((bf16[256,128]{1,0:T(8,128)(2,1)S(1)}, bf16[256,128]{1,0:T(8,128)(2,1)S(1)}, u32[]{:S(2)}, u32[]{:S(2)}) %collective-permute-start.27) | collective-permute-done | bytes 65568 | tf_op jit(solution)/shard_map/ppermute | solution.py:44
  71.1 2.7 %collective-permute-start.29 = (bf16[256,128]{1,0:T(8,128)(2,1)S(1)}, bf16[256,128]{1,0:T(8,128)(2,1)S(1)}, u32[]{:S(2)}, u32[]{:S(2)}) collective-permute-start(bf16[256,128]{1,0:T(8,128)(2,1)S(1)} %add_convert_fusion.3), channel_id=1, source_target_pairs={{0,1},{1,0},{2,3},{3,2},{4,5},{5,4},{6,7},{7,6},{8,9},{9,8},{10,11... | collective-permute-start | bytes 196616 | tf_op jit(solution)/shard_map/ppermute | solution.py:44
  75.7 1.2 grads.1
  80.4 1.2 collective-permute-start.39
  82.2 1.3 collective-permute-start.40
  83.5 1.8 collective-permute-done.39.refs_2_
  85.3 1.2 collective-permute-start.41
  87.0 2.2 %collective-permute-start.42 = (bf16[4,8,1408]{2,1,0:T(8,128)(2,1)}, bf16[4,8,1408]{2,1,0:T(8,128)(2,1)}, u32[]{:S(2)}, u32[]{:S(2)}) collective-permute-start(bf16[4,8,1408]{2,1,0:T(8,128)(2,1)} %copy-done.11), channel_id=1, source_target_pairs={{0,80},{16,64},{32,112},{48,96},{64,16},{80,0},{96,48},{112,32},{1... | collective-permute-start | bytes 270344 | tf_op jit(solution)/shard_map/ppermute | solution.py:49
  89.2 1.2 collective-permute-done.41.refs_4_
  90.4 3.1 %collective-permute-start.4 = (bf16[512,512]{1,0:T(8,128)(2,1)}, bf16[512,512]{1,0:T(8,128)(2,1)}, u32[]{:S(2)}, u32[]{:S(2)}) collective-permute-start(bf16[512,512]{1,0:T(8,128)(2,1)} %copy-done.5), channel_id=1, source_target_pairs={{0,2},{1,7},{2,4},{3,1},{4,6},{5,3},{6,0},{7,5},{8,10},{9,15},{10,... | collective-permute-start | bytes 1572872 | tf_op jit(solution)/shard_map/ppermute | solution.py:44
  93.5 3.2 %collective-permute-start.43 = (bf16[4,8,1408]{2,1,0:T(8,128)(2,1)}, bf16[4,8,1408]{2,1,0:T(8,128)(2,1)S(1)}, u32[]{:S(2)}, u32[]{:S(2)}) collective-permute-start(bf16[4,8,1408]{2,1,0:T(8,128)(2,1)} %copy-done.10), channel_id=1, source_target_pairs={{0,96},{16,112},{32,64},{48,80},{64,32},{80,48},{96,0},{112,16},{1... | collective-permute-start | bytes 270344 | tf_op jit(solution)/shard_map/ppermute | solution.py:49
  96.8 4.3 %collective-permute-done.43.refs_6_ = bf16[4,8,1408]{2,1,0:T(8,128)(2,1)S(1)} collective-permute-done((bf16[4,8,1408]{2,1,0:T(8,128)(2,1)}, bf16[4,8,1408]{2,1,0:T(8,128)(2,1)S(1)}, u32[]{:S(2)}, u32[]{:S(2)}) %collective-permute-start.43) | collective-permute-done | bytes 90144 | tf_op jit(solution)/shard_map/ppermute | solution.py:49
  101.1 2.1 %collective-permute-start.44 = (bf16[4,8,1408]{2,1,0:T(8,128)(2,1)}, bf16[4,8,1408]{2,1,0:T(8,128)(2,1)S(1)}, u32[]{:S(2)}, u32[]{:S(2)}) collective-permute-start(bf16[4,8,1408]{2,1,0:T(8,128)(2,1)} %copy-done.9), channel_id=1, source_target_pairs={{0,112},{16,96},{32,80},{48,64},{64,48},{80,32},{96,16},{112,0},{1... | collective-permute-start | bytes 270344 | tf_op jit(solution)/shard_map/ppermute | solution.py:49
  103.2 1.7 fusion.5
  104.9 3.8 %collective-permute-done.44.refs_7_ = bf16[4,8,1408]{2,1,0:T(8,128)(2,1)S(1)} collective-permute-done((bf16[4,8,1408]{2,1,0:T(8,128)(2,1)}, bf16[4,8,1408]{2,1,0:T(8,128)(2,1)S(1)}, u32[]{:S(2)}, u32[]{:S(2)}) %collective-permute-start.44) | collective-permute-done | bytes 90144 | tf_op jit(solution)/shard_map/ppermute | solution.py:49
  108.8 3.1 %collective-permute-start.7 = (bf16[512,512]{1,0:T(8,128)(2,1)S(1)}, bf16[512,512]{1,0:T(8,128)(2,1)S(1)}, u32[]{:S(2)}, u32[]{:S(2)}) collective-permute-start(bf16[512,512]{1,0:T(8,128)(2,1)S(1)} %copy-done.1), channel_id=1, source_target_pairs={{0,6},{1,3},{2,0},{3,5},{4,2},{5,7},{6,4},{7,1},{8,14},{9,11},{10,... | collective-permute-start | bytes 1572872 | tf_op jit(solution)/shard_map/ppermute | solution.py:44
  112.3 1.3 total.1
  113.7 1.4 collective-permute-start.2
  115.4 7.6 %backward.3 = (bf16[512,512]{1,0:T(8,128)(2,1)S(1)}, bf16[512,512]{1,0:T(8,128)(2,1)S(1)}, bf16[512,512]{1,0:T(8,128)(2,1)S(1)}, bf16[512,512]{1,0:T(8,128)(2,1)S(1)}) custom-call(s32[4]{0:T(128)S(1)} %pad_add_fusion.order, bf16[512,896]{1,0:T(8,128)(2,1)S(1)} %copy-done, bf16[512,896]{1,0:T(8,128)(2,1)S(1)} %collective-permute-done.30.cot_pair, ...), custom_call_target="tpu_custom_call" | custom-call | flops 3758096384 | bytes 7340032 | tf_op jit(solution)/shard_map/backward/pallas_call | solution.py:232
  123.1 1.2 collective-permute-start.35
  124.4 9.0 %ahead.2 = (f32[512,896]{1,0:T(8,128)S(1)}, f32[512,896]{1,0:T(8,128)}) custom-call(s32[4]{0:T(128)S(1)} %pad_add_fusion.2.order, bf16[512,512]{1,0:T(8,128)(2,1)S(1)} %copy-done.1, bf16[512,512]{1,0:T(8,128)(2,1)S(1)} %copy-done.4, bf16[512,512]{1,0:T(8,128)(2,1)S(1)} %copy-done.6, bf16[512,512]{1,0:T(8,128)(2,1)S(1)} %collective-permute-done.7.refs_3_, ...), custom_call_target="tpu_custom_call" | custom-call | flops 3758096384 | bytes 7340032 | tf_op jit(solution)/shard_map/ahead/pallas_call | solution.py:191
  133.4 1.2 copy-done.2
  134.7 2.6 %collective-permute-start.33 = (bf16[512,512]{1,0:T(8,128)(2,1)S(1)}, bf16[512,512]{1,0:T(8,128)(2,1)S(1)}, u32[]{:S(2)}, u32[]{:S(2)}) collective-permute-start(bf16[512,512]{1,0:T(8,128)(2,1)S(1)} %get-tuple-element.78), channel_id=1, source_target_pairs={{0,2},{1,7},{2,4},{3,1},{4,6},{5,3},{6,0},{7,5},{8,10},{9,15},{10,... | collective-permute-start | bytes 1572872 | tf_op jit(solution)/shard_map/ppermute | solution.py:44
  137.3 10.2 %ahead.3 = (f32[512,896]{1,0:T(8,128)S(1)}, f32[512,896]{1,0:T(8,128)}) custom-call(s32[4]{0:T(128)S(1)} %pad_add_fusion.order, bf16[512,512]{1,0:T(8,128)(2,1)S(1)} %collective-permute-done.1.refs_0_, bf16[512,512]{1,0:T(8,128)(2,1)S(1)} %collective-permute-done.2.refs_1_, bf16[512,512]{1,0:T(8,128)(2,1)} %collective-permute-done.4.refs_2_, ...), custom_call_target="tpu_custom_call" | custom-call | flops 3758096384 | bytes 7340032 | tf_op jit(solution)/shard_map/ahead/pallas_call | solution.py:191
  147.6 1.6 convert_element_type.81
  149.2 10.5 %collective-permute-start.9 = (bf16[512,896]{1,0:T(8,128)(2,1)S(1)}, bf16[512,896]{1,0:T(8,128)(2,1)S(1)}, u32[]{:S(2)}, u32[]{:S(2)}) collective-permute-start(bf16[512,896]{1,0:T(8,128)(2,1)S(1)} %convert_element_type.81), channel_id=1, source_target_pairs={{0,1},{1,0},{2,3},{3,2},{4,5},{5,4},{6,7},{7,6},{8,9},{9,8},{10,11... | collective-permute-start | bytes 2752520 | tf_op jit(solution)/shard_map/ppermute | solution.py:44
  160.5 1.2 add_convert_fusion.1
  161.7 7.6 %backward.2 = (bf16[512,512]{1,0:T(8,128)(2,1)S(1)}, bf16[512,512]{1,0:T(8,128)(2,1)S(1)}, bf16[512,512]{1,0:T(8,128)(2,1)S(1)}, bf16[512,512]{1,0:T(8,128)(2,1)S(1)}) custom-call(s32[4]{0:T(128)S(1)} %pad_add_fusion.2.order, bf16[512,896]{1,0:T(8,128)(2,1)S(1)} %copy-done, bf16[512,896]{1,0:T(8,128)(2,1)S(1)} %collective-permute-done.30.cot_pair, ...), custom_call_target="tpu_custom_call" | custom-call | flops 3758096384 | bytes 7340032 | tf_op jit(solution)/shard_map/backward/pallas_call | solution.py:232
  169.3 1.8 collective-permute-start.46
  171.2 2.3 %collective-permute-start.47 = (bf16[4,8,1408]{2,1,0:T(8,128)(2,1)S(1)}, bf16[4,8,1408]{2,1,0:T(8,128)(2,1)S(1)}, u32[]{:S(2)}, u32[]{:S(2)}) collective-permute-start(bf16[4,8,1408]{2,1,0:T(8,128)(2,1)S(1)} %get-tuple-element.93), channel_id=1, source_target_pairs={{0,48},{16,32},{32,16},{48,0},{64,112},{80,96},{96,80},{112,64},{1... | collective-permute-start | bytes 270344 | tf_op jit(solution)/shard_map/ppermute | solution.py:49
  173.5 1.0 add_convert_fusion.2
  174.6 1.3 collective-permute-start.49
  175.9 5.0 %collective-permute-start.50 = (bf16[4,8,1408]{2,1,0:T(8,128)(2,1)S(1)}, bf16[4,8,1408]{2,1,0:T(8,128)(2,1)S(1)}, u32[]{:S(2)}, u32[]{:S(2)}) collective-permute-start(bf16[4,8,1408]{2,1,0:T(8,128)(2,1)S(1)} %get-tuple-element.96), channel_id=1, source_target_pairs={{0,96},{16,112},{32,64},{48,80},{64,32},{80,48},{96,0},{112,16},{1... | collective-permute-start | bytes 270344 | tf_op jit(solution)/shard_map/ppermute | solution.py:49
  181.0 2.6 %collective-permute-start.51 = (bf16[4,8,1408]{2,1,0:T(8,128)(2,1)S(1)}, bf16[4,8,1408]{2,1,0:T(8,128)(2,1)S(1)}, u32[]{:S(2)}, u32[]{:S(2)}) collective-permute-start(bf16[4,8,1408]{2,1,0:T(8,128)(2,1)S(1)} %get-tuple-element.97), channel_id=1, source_target_pairs={{0,112},{16,96},{32,80},{48,64},{64,48},{80,32},{96,16},{112,0},{1... | collective-permute-start | bytes 270344 | tf_op jit(solution)/shard_map/ppermute | solution.py:49
  183.6 2.7 %collective-permute-start.31 = (bf16[512,512]{1,0:T(8,128)(2,1)S(1)}, bf16[512,512]{1,0:T(8,128)(2,1)S(1)}, u32[]{:S(2)}, u32[]{:S(2)}) collective-permute-start(bf16[512,512]{1,0:T(8,128)(2,1)S(1)} %get-tuple-element.75), channel_id=1, source_target_pairs={{0,2},{1,7},{2,4},{3,1},{4,6},{5,3},{6,0},{7,5},{8,10},{9,15},{10,... | collective-permute-start | bytes 1572872 | tf_op jit(solution)/shard_map/ppermute | solution.py:44
  186.9 2.1 %collective-permute-done.51.refs_7_ = bf16[4,8,1408]{2,1,0:T(8,128)(2,1)S(1)} collective-permute-done((bf16[4,8,1408]{2,1,0:T(8,128)(2,1)S(1)}, bf16[4,8,1408]{2,1,0:T(8,128)(2,1)S(1)}, u32[]{:S(2)}, u32[]{:S(2)}) %collective-permute-start.51) | collective-permute-done | bytes 90144 | tf_op jit(solution)/shard_map/ppermute | solution.py:49
  189.0 0.9 join.1
  189.9 1.2 fusion
  191.1 2.6 %collective-permute-done.31 = bf16[512,512]{1,0:T(8,128)(2,1)S(1)} collective-permute-done((bf16[512,512]{1,0:T(8,128)(2,1)S(1)}, bf16[512,512]{1,0:T(8,128)(2,1)S(1)}, u32[]{:S(2)}, u32[]{:S(2)}) %collective-permute-start.31) | collective-permute-done | bytes 524320 | tf_op jit(solution)/shard_map/ppermute | solution.py:44
  193.6 5.5 %collective-permute-done.34 = bf16[512,512]{1,0:T(8,128)(2,1)S(1)} collective-permute-done((bf16[512,512]{1,0:T(8,128)(2,1)}, bf16[512,512]{1,0:T(8,128)(2,1)S(1)}, u32[]{:S(2)}, u32[]{:S(2)}) %collective-permute-start.34) | collective-permute-done | bytes 524320 | tf_op jit(solution)/shard_map/ppermute | solution.py:44
  199.1 2.3 %collective-permute-done.37 = bf16[512,512]{1,0:T(8,128)(2,1)S(1)} collective-permute-done((bf16[512,512]{1,0:T(8,128)(2,1)S(1)}, bf16[512,512]{1,0:T(8,128)(2,1)S(1)}, u32[]{:S(2)}, u32[]{:S(2)}) %collective-permute-start.37) | collective-permute-done | bytes 524320 | tf_op jit(solution)/shard_map/ppermute | solution.py:44
  201.4 1.1 fusion.1
  (113 shorter events, 14.4 us)
Async XLA Ops:
  0.8 6.5 %copy-start.7 = (bf16[4,64,896]{2,1,0:T(8,128)(2,1)S(1)}, bf16[4,64,896]{2,1,0:T(8,128)(2,1)}, u32[]{:S(2)}) copy-start(bf16[4,64,896]{2,1,0:T(8,128)(2,1)} %param.10) | copy-start | bytes 1376260
  0.8 6.5 %copy-start.8 = (bf16[4,512,64]{1,2,0:T(8,128)(2,1)S(1)}, bf16[4,512,64]{1,2,0:T(8,128)(2,1)}, u32[]{:S(2)}) copy-start(bf16[4,512,64]{1,2,0:T(8,128)(2,1)} %param.9) | copy-start | bytes 786436
  5.9 109.3 %collective-permute-start.6 = (bf16[4,512,896]{2,1,0:T(8,128)(2,1)}, bf16[4,512,896]{2,1,0:T(8,128)(2,1)}, u32[]{:S(2)}, u32[]{:S(2)}) collective-permute-start(bf16[4,512,896]{2,1,0:T(8,128)(2,1)} %take_blocks.2), channel_id=1, source_target_pairs={{0,1},{1,0},{2,3},{3,2},{4,5},{5,4},{6,7},{7,6},{8,9},{9,8},{10,11... | collective-permute-start | bytes 11010056 | tf_op jit(solution)/shard_map/ppermute | solution.py:44
  7.3 11.1 %collective-permute-start.10 = (bf16[4,8,1408]{2,1,0:T(8,128)(2,1)S(1)}, bf16[4,8,1408]{2,1,0:T(8,128)(2,1)S(1)}, u32[]{:S(2)}, u32[]{:S(2)}) collective-permute-start(bf16[4,8,1408]{2,1,0:T(8,128)(2,1)S(1)} %get-tuple-element.57), channel_id=1, source_target_pairs={{0,16},{16,0},{32,48},{48,32},{64,80},{80,64},{96,112},{112,96},{1... | collective-permute-start | bytes 270344 | tf_op jit(solution)/shard_map/ppermute | solution.py:49
  9.1 12.3 %collective-permute-start.11 = (bf16[4,8,1408]{2,1,0:T(8,128)(2,1)S(1)}, bf16[4,8,1408]{2,1,0:T(8,128)(2,1)S(1)}, u32[]{:S(2)}, u32[]{:S(2)}) collective-permute-start(bf16[4,8,1408]{2,1,0:T(8,128)(2,1)S(1)} %get-tuple-element.58), channel_id=1, source_target_pairs={{0,32},{16,48},{32,0},{48,16},{64,96},{80,112},{96,64},{112,80},{1... | collective-permute-start | bytes 270344 | tf_op jit(solution)/shard_map/ppermute | solution.py:49
  12.4 9.1 %collective-permute-start.12 = (bf16[4,8,1408]{2,1,0:T(8,128)(2,1)S(1)}, bf16[4,8,1408]{2,1,0:T(8,128)(2,1)S(1)}, u32[]{:S(2)}, u32[]{:S(2)}) collective-permute-start(bf16[4,8,1408]{2,1,0:T(8,128)(2,1)S(1)} %get-tuple-element.59), channel_id=1, source_target_pairs={{0,48},{16,32},{32,16},{48,0},{64,112},{80,96},{96,80},{112,64},{1... | collective-permute-start | bytes 270344 | tf_op jit(solution)/shard_map/ppermute | solution.py:49
  12.5 5.8 %copy-start.16 = (s32[32]{0:T(128)S(1)}, s32[32]{0:T(128)}, u32[]{:S(2)}) copy-start(s32[32]{0:T(128)} %param.13) | copy-start | bytes 388
  12.5 5.8 %copy-start.17 = (s32[32]{0:T(128)S(1)}, s32[32]{0:T(128)}, u32[]{:S(2)}) copy-start(s32[32]{0:T(128)} %param.12) | copy-start | bytes 388
  12.5 41.1 %copy-start = (bf16[512,896]{1,0:T(8,128)(2,1)S(1)}, bf16[512,896]{1,0:T(8,128)(2,1)}, u32[]{:S(2)}) copy-start(bf16[512,896]{1,0:T(8,128)(2,1)} %cot.7) | copy-start | bytes 2752516
  12.5 41.1 %copy-start.1 = (bf16[512,512]{1,0:T(8,128)(2,1)S(1)}, bf16[512,512]{1,0:T(8,128)(2,1)}, u32[]{:S(2)}) copy-start(bf16[512,512]{1,0:T(8,128)(2,1)} %tokens.3) | copy-start | bytes 1572868
  17.6 105.6 %collective-permute-start.8 = (bf16[4,512,896]{2,1,0:T(8,128)(2,1)}, bf16[4,512,896]{2,1,0:T(8,128)(2,1)}, u32[]{:S(2)}, u32[]{:S(2)}) collective-permute-start(bf16[4,512,896]{2,1,0:T(8,128)(2,1)} %take_blocks.3), channel_id=1, source_target_pairs={{0,1},{1,0},{2,3},{3,2},{4,5},{5,4},{6,7},{7,6},{8,9},{9,8},{10,11... | collective-permute-start | bytes 11010056 | tf_op jit(solution)/shard_map/ppermute | solution.py:44
  18.5 9.6 %collective-permute-start.13 = (bf16[4,8,1408]{2,1,0:T(8,128)(2,1)S(1)}, bf16[4,8,1408]{2,1,0:T(8,128)(2,1)S(1)}, u32[]{:S(2)}, u32[]{:S(2)}) collective-permute-start(bf16[4,8,1408]{2,1,0:T(8,128)(2,1)S(1)} %get-tuple-element.60), channel_id=1, source_target_pairs={{0,64},{16,80},{32,96},{48,112},{64,0},{80,16},{96,32},{112,48},{1... | collective-permute-start | bytes 270344 | tf_op jit(solution)/shard_map/ppermute | solution.py:49
  21.5 8.3 %collective-permute-start.14 = (bf16[4,8,1408]{2,1,0:T(8,128)(2,1)S(1)}, bf16[4,8,1408]{2,1,0:T(8,128)(2,1)S(1)}, u32[]{:S(2)}, u32[]{:S(2)}) collective-permute-start(bf16[4,8,1408]{2,1,0:T(8,128)(2,1)S(1)} %get-tuple-element.61), channel_id=1, source_target_pairs={{0,80},{16,64},{32,112},{48,96},{64,16},{80,0},{96,48},{112,32},{1... | collective-permute-start | bytes 270344 | tf_op jit(solution)/shard_map/ppermute | solution.py:49
  21.6 10.9 %collective-permute-start.15 = (bf16[4,8,1408]{2,1,0:T(8,128)(2,1)S(1)}, bf16[4,8,1408]{2,1,0:T(8,128)(2,1)S(1)}, u32[]{:S(2)}, u32[]{:S(2)}) collective-permute-start(bf16[4,8,1408]{2,1,0:T(8,128)(2,1)S(1)} %get-tuple-element.62), channel_id=1, source_target_pairs={{0,96},{16,112},{32,64},{48,80},{64,32},{80,48},{96,0},{112,16},{1... | collective-permute-start | bytes 270344 | tf_op jit(solution)/shard_map/ppermute | solution.py:49
  28.1 7.0 %collective-permute-start.16 = (bf16[4,8,1408]{2,1,0:T(8,128)(2,1)S(1)}, bf16[4,8,1408]{2,1,0:T(8,128)(2,1)S(1)}, u32[]{:S(2)}, u32[]{:S(2)}) collective-permute-start(bf16[4,8,1408]{2,1,0:T(8,128)(2,1)S(1)} %get-tuple-element.63), channel_id=1, source_target_pairs={{0,112},{16,96},{32,80},{48,64},{64,48},{80,32},{96,16},{112,0},{1... | collective-permute-start | bytes 270344 | tf_op jit(solution)/shard_map/ppermute | solution.py:49
  35.8 3.9 %collective-permute-start.17 = (bf16[4,8,1408]{2,1,0:T(8,128)(2,1)S(1)}, bf16[4,8,1408]{2,1,0:T(8,128)(2,1)S(1)}, u32[]{:S(2)}, u32[]{:S(2)}) collective-permute-start(bf16[4,8,1408]{2,1,0:T(8,128)(2,1)S(1)} %get-tuple-element.65), channel_id=1, source_target_pairs={{0,16},{16,0},{32,48},{48,32},{64,80},{80,64},{96,112},{112,96},{1... | collective-permute-start | bytes 270344 | tf_op jit(solution)/shard_map/ppermute | solution.py:49
  35.9 5.6 %collective-permute-start.18 = (bf16[4,8,1408]{2,1,0:T(8,128)(2,1)S(1)}, bf16[4,8,1408]{2,1,0:T(8,128)(2,1)S(1)}, u32[]{:S(2)}, u32[]{:S(2)}) collective-permute-start(bf16[4,8,1408]{2,1,0:T(8,128)(2,1)S(1)} %get-tuple-element.66), channel_id=1, source_target_pairs={{0,32},{16,48},{32,0},{48,16},{64,96},{80,112},{96,64},{112,80},{1... | collective-permute-start | bytes 270344 | tf_op jit(solution)/shard_map/ppermute | solution.py:49
  36.8 6.0 %collective-permute-start.19 = (bf16[4,8,1408]{2,1,0:T(8,128)(2,1)S(1)}, bf16[4,8,1408]{2,1,0:T(8,128)(2,1)S(1)}, u32[]{:S(2)}, u32[]{:S(2)}) collective-permute-start(bf16[4,8,1408]{2,1,0:T(8,128)(2,1)S(1)} %get-tuple-element.67), channel_id=1, source_target_pairs={{0,48},{16,32},{32,16},{48,0},{64,112},{80,96},{96,80},{112,64},{1... | collective-permute-start | bytes 270344 | tf_op jit(solution)/shard_map/ppermute | solution.py:49
  39.7 6.5 %collective-permute-start.20 = (bf16[4,8,1408]{2,1,0:T(8,128)(2,1)S(1)}, bf16[4,8,1408]{2,1,0:T(8,128)(2,1)S(1)}, u32[]{:S(2)}, u32[]{:S(2)}) collective-permute-start(bf16[4,8,1408]{2,1,0:T(8,128)(2,1)S(1)} %get-tuple-element.68), channel_id=1, source_target_pairs={{0,64},{16,80},{32,96},{48,112},{64,0},{80,16},{96,32},{112,48},{1... | collective-permute-start | bytes 270344 | tf_op jit(solution)/shard_map/ppermute | solution.py:49
  41.5 7.2 %collective-permute-start.21 = (bf16[4,8,1408]{2,1,0:T(8,128)(2,1)S(1)}, bf16[4,8,1408]{2,1,0:T(8,128)(2,1)S(1)}, u32[]{:S(2)}, u32[]{:S(2)}) collective-permute-start(bf16[4,8,1408]{2,1,0:T(8,128)(2,1)S(1)} %get-tuple-element.69), channel_id=1, source_target_pairs={{0,80},{16,64},{32,112},{48,96},{64,16},{80,0},{96,48},{112,32},{1... | collective-permute-start | bytes 270344 | tf_op jit(solution)/shard_map/ppermute | solution.py:49
  42.8 7.3 %collective-permute-start.22 = (bf16[4,8,1408]{2,1,0:T(8,128)(2,1)S(1)}, bf16[4,8,1408]{2,1,0:T(8,128)(2,1)S(1)}, u32[]{:S(2)}, u32[]{:S(2)}) collective-permute-start(bf16[4,8,1408]{2,1,0:T(8,128)(2,1)S(1)} %get-tuple-element.70), channel_id=1, source_target_pairs={{0,96},{16,112},{32,64},{48,80},{64,32},{80,48},{96,0},{112,16},{1... | collective-permute-start | bytes 270344 | tf_op jit(solution)/shard_map/ppermute | solution.py:49
  46.2 7.4 %collective-permute-start.23 = (bf16[4,8,1408]{2,1,0:T(8,128)(2,1)S(1)}, bf16[4,8,1408]{2,1,0:T(8,128)(2,1)S(1)}, u32[]{:S(2)}, u32[]{:S(2)}) collective-permute-start(bf16[4,8,1408]{2,1,0:T(8,128)(2,1)S(1)} %get-tuple-element.71), channel_id=1, source_target_pairs={{0,112},{16,96},{32,80},{48,64},{64,48},{80,32},{96,16},{112,0},{1... | collective-permute-start | bytes 270344 | tf_op jit(solution)/shard_map/ppermute | solution.py:49
  54.2 5.6 %collective-permute-start.24 = (f32[256,128]{1,0:T(8,128)S(1)}, f32[256,128]{1,0:T(8,128)S(1)}, u32[]{:S(2)}, u32[]{:S(2)}) collective-permute-start(f32[256,128]{1,0:T(8,128)S(1)} %slice_select_fusion), channel_id=1, source_target_pairs={{0,1},{1,0},{2,3},{3,2},{4,5},{5,4},{6,7},{7,6},{8,9},{9,8},{10,11... | collective-permute-start | bytes 393224 | tf_op jit(solution)/shard_map/ppermute | solution.py:44
  59.9 3.2 %collective-permute-start.25 = (bf16[256,128]{1,0:T(8,128)(2,1)S(1)}, bf16[256,128]{1,0:T(8,128)(2,1)S(1)}, u32[]{:S(2)}, u32[]{:S(2)}) collective-permute-start(bf16[256,128]{1,0:T(8,128)(2,1)S(1)} %add_convert_fusion.5), channel_id=1, source_target_pairs={{0,8},{1,9},{2,10},{3,11},{4,12},{5,13},{6,14},{7,15},{8,0},{9,1},... | collective-permute-start | bytes 196616 | tf_op jit(solution)/shard_map/ppermute | solution.py:44
  63.1 4.5 %collective-permute-start.26 = (bf16[256,128]{1,0:T(8,128)(2,1)S(1)}, bf16[256,128]{1,0:T(8,128)(2,1)S(1)}, u32[]{:S(2)}, u32[]{:S(2)}) collective-permute-start(bf16[256,128]{1,0:T(8,128)(2,1)S(1)} %add_convert_fusion.4), channel_id=1, source_target_pairs={{0,2},{1,7},{2,4},{3,1},{4,6},{5,3},{6,0},{7,5},{8,10},{9,15},{10,... | collective-permute-start | bytes 196616 | tf_op jit(solution)/shard_map/ppermute | solution.py:44
  65.9 4.9 %collective-permute-start.27 = (bf16[256,128]{1,0:T(8,128)(2,1)S(1)}, bf16[256,128]{1,0:T(8,128)(2,1)S(1)}, u32[]{:S(2)}, u32[]{:S(2)}) collective-permute-start(bf16[256,128]{1,0:T(8,128)(2,1)S(1)} %add_convert_fusion.4), channel_id=1, source_target_pairs={{0,6},{1,3},{2,0},{3,5},{4,2},{5,7},{6,4},{7,1},{8,14},{9,11},{10,... | collective-permute-start | bytes 196616 | tf_op jit(solution)/shard_map/ppermute | solution.py:44
  65.9 5.1 %collective-permute-start.28 = (bf16[256,128]{1,0:T(8,128)(2,1)S(1)}, bf16[256,128]{1,0:T(8,128)(2,1)S(1)}, u32[]{:S(2)}, u32[]{:S(2)}) collective-permute-start(bf16[256,128]{1,0:T(8,128)(2,1)S(1)} %add_convert_fusion.4), channel_id=1, source_target_pairs={{0,4},{1,5},{2,6},{3,7},{4,0},{5,1},{6,2},{7,3},{8,12},{9,13},{10,... | collective-permute-start | bytes 196616 | tf_op jit(solution)/shard_map/ppermute | solution.py:44
  67.5 11.3 %collective-permute-start = (bf16[512,512]{1,0:T(8,128)(2,1)S(1)}, bf16[512,512]{1,0:T(8,128)(2,1)S(1)}, u32[]{:S(2)}, u32[]{:S(2)}) collective-permute-start(bf16[512,512]{1,0:T(8,128)(2,1)S(1)} %copy-done.1), channel_id=1, source_target_pairs={{0,8},{1,9},{2,10},{3,11},{4,12},{5,13},{6,14},{7,15},{8,0},{9,1},... | collective-permute-start | bytes 1572872 | tf_op jit(solution)/shard_map/ppermute | solution.py:44
  70.8 8.3 %collective-permute-start.3 = (bf16[512,512]{1,0:T(8,128)(2,1)S(1)}, bf16[512,512]{1,0:T(8,128)(2,1)S(1)}, u32[]{:S(2)}, u32[]{:S(2)}) collective-permute-start(bf16[512,512]{1,0:T(8,128)(2,1)S(1)} %copy-done.1), channel_id=1, source_target_pairs={{0,2},{1,7},{2,4},{3,1},{4,6},{5,3},{6,0},{7,5},{8,10},{9,15},{10,... | collective-permute-start | bytes 1572872 | tf_op jit(solution)/shard_map/ppermute | solution.py:44
  71.1 3.6 %collective-permute-start.29 = (bf16[256,128]{1,0:T(8,128)(2,1)S(1)}, bf16[256,128]{1,0:T(8,128)(2,1)S(1)}, u32[]{:S(2)}, u32[]{:S(2)}) collective-permute-start(bf16[256,128]{1,0:T(8,128)(2,1)S(1)} %add_convert_fusion.3), channel_id=1, source_target_pairs={{0,1},{1,0},{2,3},{3,2},{4,5},{5,4},{6,7},{7,6},{8,9},{9,8},{10,11... | collective-permute-start | bytes 196616 | tf_op jit(solution)/shard_map/ppermute | solution.py:44
  74.7 38.9 %collective-permute-start.30 = (bf16[512,896]{1,0:T(8,128)(2,1)S(1)}, bf16[512,896]{1,0:T(8,128)(2,1)S(1)}, u32[]{:S(2)}, u32[]{:S(2)}) collective-permute-start(bf16[512,896]{1,0:T(8,128)(2,1)S(1)} %copy-done), channel_id=1, source_target_pairs={{0,1},{1,0},{2,3},{3,2},{4,5},{5,4},{6,7},{7,6},{8,9},{9,8},{10,11... | collective-permute-start | bytes 2752520 | tf_op jit(solution)/shard_map/ppermute | solution.py:44
  78.8 0.8 copy-start.3
  78.8 3.4 %collective-permute-start.38 = (bf16[4,8,1408]{2,1,0:T(8,128)(2,1)S(1)}, bf16[4,8,1408]{2,1,0:T(8,128)(2,1)S(1)}, u32[]{:S(2)}, u32[]{:S(2)}) collective-permute-start(bf16[4,8,1408]{2,1,0:T(8,128)(2,1)S(1)} %get-tuple-element.83), channel_id=1, source_target_pairs={{0,16},{16,0},{32,48},{48,32},{64,80},{80,64},{96,112},{112,96},{1... | collective-permute-start | bytes 270344 | tf_op jit(solution)/shard_map/ppermute | solution.py:49
  80.4 4.9 %collective-permute-start.39 = (bf16[4,8,1408]{2,1,0:T(8,128)(2,1)S(1)}, bf16[4,8,1408]{2,1,0:T(8,128)(2,1)S(1)}, u32[]{:S(2)}, u32[]{:S(2)}) collective-permute-start(bf16[4,8,1408]{2,1,0:T(8,128)(2,1)S(1)} %get-tuple-element.84), channel_id=1, source_target_pairs={{0,32},{16,48},{32,0},{48,16},{64,96},{80,112},{96,64},{112,80},{1... | collective-permute-start | bytes 270344 | tf_op jit(solution)/shard_map/ppermute | solution.py:49
  82.2 4.8 %collective-permute-start.40 = (bf16[4,8,1408]{2,1,0:T(8,128)(2,1)}, bf16[4,8,1408]{2,1,0:T(8,128)(2,1)S(1)}, u32[]{:S(2)}, u32[]{:S(2)}) collective-permute-start(bf16[4,8,1408]{2,1,0:T(8,128)(2,1)} %get-tuple-element.85), channel_id=1, source_target_pairs={{0,48},{16,32},{32,16},{48,0},{64,112},{80,96},{96,80},{112,64},{1... | collective-permute-start | bytes 270344 | tf_op jit(solution)/shard_map/ppermute | solution.py:49
  85.3 5.1 %collective-permute-start.41 = (bf16[4,8,1408]{2,1,0:T(8,128)(2,1)}, bf16[4,8,1408]{2,1,0:T(8,128)(2,1)S(1)}, u32[]{:S(2)}, u32[]{:S(2)}) collective-permute-start(bf16[4,8,1408]{2,1,0:T(8,128)(2,1)} %get-tuple-element.86), channel_id=1, source_target_pairs={{0,64},{16,80},{32,96},{48,112},{64,0},{80,16},{96,32},{112,48},{1... | collective-permute-start | bytes 270344 | tf_op jit(solution)/shard_map/ppermute | solution.py:49
  87.0 6.5 %collective-permute-start.42 = (bf16[4,8,1408]{2,1,0:T(8,128)(2,1)}, bf16[4,8,1408]{2,1,0:T(8,128)(2,1)}, u32[]{:S(2)}, u32[]{:S(2)}) collective-permute-start(bf16[4,8,1408]{2,1,0:T(8,128)(2,1)} %copy-done.11), channel_id=1, source_target_pairs={{0,80},{16,64},{32,112},{48,96},{64,16},{80,0},{96,48},{112,32},{1... | collective-permute-start | bytes 270344 | tf_op jit(solution)/shard_map/ppermute | solution.py:49
  90.4 23.3 %collective-permute-start.4 = (bf16[512,512]{1,0:T(8,128)(2,1)}, bf16[512,512]{1,0:T(8,128)(2,1)}, u32[]{:S(2)}, u32[]{:S(2)}) collective-permute-start(bf16[512,512]{1,0:T(8,128)(2,1)} %copy-done.5), channel_id=1, source_target_pairs={{0,2},{1,7},{2,4},{3,1},{4,6},{5,3},{6,0},{7,5},{8,10},{9,15},{10,... | collective-permute-start | bytes 1572872 | tf_op jit(solution)/shard_map/ppermute | solution.py:44
  93.5 20.1 %copy-start.4 = (bf16[512,512]{1,0:T(8,128)(2,1)S(1)}, bf16[512,512]{1,0:T(8,128)(2,1)}, u32[]{:S(2)}) copy-start(bf16[512,512]{1,0:T(8,128)(2,1)} %copy-done.3) | copy-start | bytes 1572868
  93.5 7.6 %collective-permute-start.43 = (bf16[4,8,1408]{2,1,0:T(8,128)(2,1)}, bf16[4,8,1408]{2,1,0:T(8,128)(2,1)S(1)}, u32[]{:S(2)}, u32[]{:S(2)}) collective-permute-start(bf16[4,8,1408]{2,1,0:T(8,128)(2,1)} %copy-done.10), channel_id=1, source_target_pairs={{0,96},{16,112},{32,64},{48,80},{64,32},{80,48},{96,0},{112,16},{1... | collective-permute-start | bytes 270344 | tf_op jit(solution)/shard_map/ppermute | solution.py:49
  101.1 7.7 %collective-permute-start.44 = (bf16[4,8,1408]{2,1,0:T(8,128)(2,1)}, bf16[4,8,1408]{2,1,0:T(8,128)(2,1)S(1)}, u32[]{:S(2)}, u32[]{:S(2)}) collective-permute-start(bf16[4,8,1408]{2,1,0:T(8,128)(2,1)} %copy-done.9), channel_id=1, source_target_pairs={{0,112},{16,96},{32,80},{48,64},{64,48},{80,32},{96,16},{112,0},{1... | collective-permute-start | bytes 270344 | tf_op jit(solution)/shard_map/ppermute | solution.py:49
  108.8 14.3 %collective-permute-start.7 = (bf16[512,512]{1,0:T(8,128)(2,1)S(1)}, bf16[512,512]{1,0:T(8,128)(2,1)S(1)}, u32[]{:S(2)}, u32[]{:S(2)}) collective-permute-start(bf16[512,512]{1,0:T(8,128)(2,1)S(1)} %copy-done.1), channel_id=1, source_target_pairs={{0,6},{1,3},{2,0},{3,5},{4,2},{5,7},{6,4},{7,1},{8,14},{9,11},{10,... | collective-permute-start | bytes 1572872 | tf_op jit(solution)/shard_map/ppermute | solution.py:44
  113.6 10.8 %copy-start.6 = (bf16[512,512]{1,0:T(8,128)(2,1)S(1)}, bf16[512,512]{1,0:T(8,128)(2,1)}, u32[]{:S(2)}) copy-start(bf16[512,512]{1,0:T(8,128)(2,1)} %copy-done.5) | copy-start | bytes 1572868
  113.6 21.1 %collective-permute-start.1 = (bf16[512,512]{1,0:T(8,128)(2,1)S(1)}, bf16[512,512]{1,0:T(8,128)(2,1)S(1)}, u32[]{:S(2)}, u32[]{:S(2)}) collective-permute-start(bf16[512,512]{1,0:T(8,128)(2,1)S(1)} %copy-done.4), channel_id=1, source_target_pairs={{0,2},{1,7},{2,4},{3,1},{4,6},{5,3},{6,0},{7,5},{8,10},{9,15},{10,... | collective-permute-start | bytes 1572872 | tf_op jit(solution)/shard_map/ppermute | solution.py:44
  113.7 21.1 %collective-permute-start.2 = (bf16[512,512]{1,0:T(8,128)(2,1)S(1)}, bf16[512,512]{1,0:T(8,128)(2,1)S(1)}, u32[]{:S(2)}, u32[]{:S(2)}) collective-permute-start(bf16[512,512]{1,0:T(8,128)(2,1)S(1)} %copy-done.4), channel_id=1, source_target_pairs={{0,6},{1,3},{2,0},{3,5},{4,2},{5,7},{6,4},{7,1},{8,14},{9,11},{10,... | collective-permute-start | bytes 1572872 | tf_op jit(solution)/shard_map/ppermute | solution.py:44
  115.1 22.2 %collective-permute-start.5 = (bf16[512,512]{1,0:T(8,128)(2,1)}, bf16[512,512]{1,0:T(8,128)(2,1)S(1)}, u32[]{:S(2)}, u32[]{:S(2)}) collective-permute-start(bf16[512,512]{1,0:T(8,128)(2,1)} %collective-permute-done.4.refs_2_), channel_id=1, source_target_pairs={{0,8},{1,9},{2,10},{3,11},{4,12},{5,13},{6,14},{7,15},{8,0},{9,1},... | collective-permute-start | bytes 1572872 | tf_op jit(solution)/shard_map/ppermute | solution.py:44
  123.0 51.4 %collective-permute-start.45 = (bf16[4,8,1408]{2,1,0:T(8,128)(2,1)S(1)}, bf16[4,8,1408]{2,1,0:T(8,128)(2,1)S(1)}, u32[]{:S(2)}, u32[]{:S(2)}) collective-permute-start(bf16[4,8,1408]{2,1,0:T(8,128)(2,1)S(1)} %get-tuple-element.91), channel_id=1, source_target_pairs={{0,16},{16,0},{32,48},{48,32},{64,80},{80,64},{96,112},{112,96},{1... | collective-permute-start | bytes 270344 | tf_op jit(solution)/shard_map/ppermute | solution.py:49
  123.1 36.6 %collective-permute-start.35 = (bf16[512,512]{1,0:T(8,128)(2,1)S(1)}, bf16[512,512]{1,0:T(8,128)(2,1)S(1)}, u32[]{:S(2)}, u32[]{:S(2)}) collective-permute-start(bf16[512,512]{1,0:T(8,128)(2,1)S(1)} %get-tuple-element.81), channel_id=1, source_target_pairs={{0,8},{1,9},{2,10},{3,11},{4,12},{5,13},{6,14},{7,15},{8,0},{9,1},... | collective-permute-start | bytes 1572872 | tf_op jit(solution)/shard_map/ppermute | solution.py:44
  133.4 1.2 copy-start.2
  134.7 34.7 %collective-permute-start.32 = (bf16[512,512]{1,0:T(8,128)(2,1)S(1)}, bf16[512,512]{1,0:T(8,128)(2,1)S(1)}, u32[]{:S(2)}, u32[]{:S(2)}) collective-permute-start(bf16[512,512]{1,0:T(8,128)(2,1)S(1)} %get-tuple-element.77), channel_id=1, source_target_pairs={{0,6},{1,3},{2,0},{3,5},{4,2},{5,7},{6,4},{7,1},{8,14},{9,11},{10,... | collective-permute-start | bytes 1572872 | tf_op jit(solution)/shard_map/ppermute | solution.py:44
  134.7 36.4 %collective-permute-start.33 = (bf16[512,512]{1,0:T(8,128)(2,1)S(1)}, bf16[512,512]{1,0:T(8,128)(2,1)S(1)}, u32[]{:S(2)}, u32[]{:S(2)}) collective-permute-start(bf16[512,512]{1,0:T(8,128)(2,1)S(1)} %get-tuple-element.78), channel_id=1, source_target_pairs={{0,2},{1,7},{2,4},{3,1},{4,6},{5,3},{6,0},{7,5},{8,10},{9,15},{10,... | collective-permute-start | bytes 1572872 | tf_op jit(solution)/shard_map/ppermute | solution.py:44
  149.2 40.8 %collective-permute-start.9 = (bf16[512,896]{1,0:T(8,128)(2,1)S(1)}, bf16[512,896]{1,0:T(8,128)(2,1)S(1)}, u32[]{:S(2)}, u32[]{:S(2)}) collective-permute-start(bf16[512,896]{1,0:T(8,128)(2,1)S(1)} %convert_element_type.81), channel_id=1, source_target_pairs={{0,1},{1,0},{2,3},{3,2},{4,5},{5,4},{6,7},{7,6},{8,9},{9,8},{10,11... | collective-permute-start | bytes 2752520 | tf_op jit(solution)/shard_map/ppermute | solution.py:44
  159.7 0.8 copy-start.14
  161.7 14.2 %collective-permute-start.36 = (bf16[512,512]{1,0:T(8,128)(2,1)S(1)}, bf16[512,512]{1,0:T(8,128)(2,1)S(1)}, u32[]{:S(2)}, u32[]{:S(2)}) collective-permute-start(bf16[512,512]{1,0:T(8,128)(2,1)S(1)} %add_convert_fusion.1), channel_id=1, source_target_pairs={{0,6},{1,3},{2,0},{3,5},{4,2},{5,7},{6,4},{7,1},{8,14},{9,11},{10,... | collective-permute-start | bytes 1572872 | tf_op jit(solution)/shard_map/ppermute | solution.py:44
  169.3 5.3 %collective-permute-start.46 = (bf16[4,8,1408]{2,1,0:T(8,128)(2,1)S(1)}, bf16[4,8,1408]{2,1,0:T(8,128)(2,1)S(1)}, u32[]{:S(2)}, u32[]{:S(2)}) collective-permute-start(bf16[4,8,1408]{2,1,0:T(8,128)(2,1)S(1)} %get-tuple-element.92), channel_id=1, source_target_pairs={{0,32},{16,48},{32,0},{48,16},{64,96},{80,112},{96,64},{112,80},{1... | collective-permute-start | bytes 270344 | tf_op jit(solution)/shard_map/ppermute | solution.py:49
  171.2 9.9 %collective-permute-start.47 = (bf16[4,8,1408]{2,1,0:T(8,128)(2,1)S(1)}, bf16[4,8,1408]{2,1,0:T(8,128)(2,1)S(1)}, u32[]{:S(2)}, u32[]{:S(2)}) collective-permute-start(bf16[4,8,1408]{2,1,0:T(8,128)(2,1)S(1)} %get-tuple-element.93), channel_id=1, source_target_pairs={{0,48},{16,32},{32,16},{48,0},{64,112},{80,96},{96,80},{112,64},{1... | collective-permute-start | bytes 270344 | tf_op jit(solution)/shard_map/ppermute | solution.py:49
  173.5 13.2 %copy-start.15 = (bf16[512,64]{1,0:T(8,128)(2,1)S(1)}, bf16[512,64]{1,0:T(8,128)(2,1)}, u32[]{:S(2)}) copy-start(bf16[512,64]{1,0:T(8,128)(2,1)} %get-tuple-element.100) | copy-start | bytes 196612
  174.5 9.2 %collective-permute-start.48 = (bf16[4,8,1408]{2,1,0:T(8,128)(2,1)S(1)}, bf16[4,8,1408]{2,1,0:T(8,128)(2,1)S(1)}, u32[]{:S(2)}, u32[]{:S(2)}) collective-permute-start(bf16[4,8,1408]{2,1,0:T(8,128)(2,1)S(1)} %get-tuple-element.94), channel_id=1, source_target_pairs={{0,64},{16,80},{32,96},{48,112},{64,0},{80,16},{96,32},{112,48},{1... | collective-permute-start | bytes 270344 | tf_op jit(solution)/shard_map/ppermute | solution.py:49
  174.6 11.7 %collective-permute-start.49 = (bf16[4,8,1408]{2,1,0:T(8,128)(2,1)S(1)}, bf16[4,8,1408]{2,1,0:T(8,128)(2,1)S(1)}, u32[]{:S(2)}, u32[]{:S(2)}) collective-permute-start(bf16[4,8,1408]{2,1,0:T(8,128)(2,1)S(1)} %get-tuple-element.95), channel_id=1, source_target_pairs={{0,80},{16,64},{32,112},{48,96},{64,16},{80,0},{96,48},{112,32},{1... | collective-permute-start | bytes 270344 | tf_op jit(solution)/shard_map/ppermute | solution.py:49
  175.9 10.7 %collective-permute-start.50 = (bf16[4,8,1408]{2,1,0:T(8,128)(2,1)S(1)}, bf16[4,8,1408]{2,1,0:T(8,128)(2,1)S(1)}, u32[]{:S(2)}, u32[]{:S(2)}) collective-permute-start(bf16[4,8,1408]{2,1,0:T(8,128)(2,1)S(1)} %get-tuple-element.96), channel_id=1, source_target_pairs={{0,96},{16,112},{32,64},{48,80},{64,32},{80,48},{96,0},{112,16},{1... | collective-permute-start | bytes 270344 | tf_op jit(solution)/shard_map/ppermute | solution.py:49
  181.0 7.9 %collective-permute-start.51 = (bf16[4,8,1408]{2,1,0:T(8,128)(2,1)S(1)}, bf16[4,8,1408]{2,1,0:T(8,128)(2,1)S(1)}, u32[]{:S(2)}, u32[]{:S(2)}) collective-permute-start(bf16[4,8,1408]{2,1,0:T(8,128)(2,1)S(1)} %get-tuple-element.97), channel_id=1, source_target_pairs={{0,112},{16,96},{32,80},{48,64},{64,48},{80,32},{96,16},{112,0},{1... | collective-permute-start | bytes 270344 | tf_op jit(solution)/shard_map/ppermute | solution.py:49
  183.6 10.0 %collective-permute-start.31 = (bf16[512,512]{1,0:T(8,128)(2,1)S(1)}, bf16[512,512]{1,0:T(8,128)(2,1)S(1)}, u32[]{:S(2)}, u32[]{:S(2)}) collective-permute-start(bf16[512,512]{1,0:T(8,128)(2,1)S(1)} %get-tuple-element.75), channel_id=1, source_target_pairs={{0,2},{1,7},{2,4},{3,1},{4,6},{5,3},{6,0},{7,5},{8,10},{9,15},{10,... | collective-permute-start | bytes 1572872 | tf_op jit(solution)/shard_map/ppermute | solution.py:44
  186.3 12.8 %collective-permute-start.34 = (bf16[512,512]{1,0:T(8,128)(2,1)}, bf16[512,512]{1,0:T(8,128)(2,1)S(1)}, u32[]{:S(2)}, u32[]{:S(2)}) collective-permute-start(bf16[512,512]{1,0:T(8,128)(2,1)} %add_convert_fusion.2), channel_id=1, source_target_pairs={{0,8},{1,9},{2,10},{3,11},{4,12},{5,13},{6,14},{7,15},{8,0},{9,1},... | collective-permute-start | bytes 1572872 | tf_op jit(solution)/shard_map/ppermute | solution.py:44
  186.6 14.8 %collective-permute-start.37 = (bf16[512,512]{1,0:T(8,128)(2,1)S(1)}, bf16[512,512]{1,0:T(8,128)(2,1)S(1)}, u32[]{:S(2)}, u32[]{:S(2)}) collective-permute-start(bf16[512,512]{1,0:T(8,128)(2,1)S(1)} %add_convert_fusion), channel_id=1, source_target_pairs={{0,6},{1,3},{2,0},{3,5},{4,2},{5,7},{6,4},{7,1},{8,14},{9,11},{10,... | collective-permute-start | bytes 1572872 | tf_op jit(solution)/shard_map/ppermute | solution.py:44
  (6 other events, 4.0 us)

commit v2 on v0

v2 whole, which is shorter than its diff:
```python
import functools

import jax
import jax.numpy as jnp
from jax import lax
from jax.experimental import pallas as pl
from jax.experimental.pallas import tpu as pltpu
from jax.sharding import PartitionSpec as P

SCALE = 8.0
GRP, XL, YY, CORES = 8, 2, 4, 2
BLK = 4
F32, BF16 = jnp.float32, jnp.bfloat16
VMEM = pl.BlockSpec(memory_space=pltpu.VMEM)
SMEM = pl.BlockSpec(memory_space=pltpu.SMEM)
HBM = pl.BlockSpec(memory_space=pltpu.HBM)
ANY = pl.BlockSpec(memory_space=pl.ANY)
WIDE = 56
COST = pl.CostEstimate(flops=1, bytes_accessed=1, transcendentals=0)
NT = (((1,), (1,)), ((), ()))
TN = (((0,), (0,)), ((), ()))


def mem_perm(move):
    pairs = []
    for x in range(XL):
        for y in range(YY):
            for c in range(CORES):
                tx, ty, tc = move(x, y, c)
                pairs.append(((x * YY + y) * CORES + c, (tx * YY + ty % YY) * CORES + tc))
    return pairs


def way(c):
    return 1 - 2 * c


MOVES = {
    "core": mem_perm(lambda x, y, c: (x, y, 1 - c)),
    "x": mem_perm(lambda x, y, c: (1 - x, y, c)),
    "fwd": mem_perm(lambda x, y, c: (x, y + way(c), c)),
    "back": mem_perm(lambda x, y, c: (x, y - way(c), c)),
    "far": mem_perm(lambda x, y, c: (x, y + 2, c)),
}


def send(value, move, name):
    with jax.named_scope(name):
        return lax.ppermute(value, "mem", MOVES[move])


def stay(value):
    return pltpu.with_memory_space_constraint(value, pltpu.HBM)


def exchange(pieces):
    return lax.all_to_all(pieces, "grp", 0, 0, tiled=True)


def params(mib):
    return pltpu.CompilerParams(vmem_limit_bytes=mib * 1024 * 1024)


def cut_kernel(down, up, out):
    width = down.shape[-1]
    out[:, 0, :, :width] = down[0]
    out[:, 0, :, width:] = up[0]


def pick_kernel(slots, got, out):
    for i in range(GRP):
        for b in range(BLK):
            slot = slots[BLK * i + b]
            out[i, b] = got[slot // BLK, slot % BLK]


def rank_kernel(tokens, cot, got, adapters, part):
    width = tokens.shape[1]
    rank = adapters.shape[1]
    whole = jnp.concatenate([got[i, 0].astype(F32) for i in range(GRP)], axis=0).astype(BF16)
    adapters[0] = whole
    part[:, :rank] = lax.dot_general(tokens[...], whole[:, :width], NT, preferred_element_type=F32)
    part[:, rank:] = lax.dot_general(cot[...], whole[:, width:], NT, preferred_element_type=F32)


def grad_kernel(tokens, cot, ranks, out):
    width = tokens.shape[1]
    rows = tokens.shape[0]
    rank = ranks.shape[1] // 2
    piece = rank // GRP
    factor = SCALE / rows
    both = ranks[...]
    down = lax.dot_general(both[:, rank:], tokens[...], TN, preferred_element_type=F32) * factor
    up = lax.dot_general(both[:, :rank], cot[...], TN, preferred_element_type=F32) * factor
    for i in range(GRP):
        part = slice(i * piece, (i + 1) * piece)
        out[i, 0, :, :width] = down[part].astype(BF16)
        out[i, 0, :, width:] = up[part].astype(BF16)


def total_kernel(slots, got, out, total):
    total[...] = jnp.zeros_like(total)
    for i in range(GRP):
        for b in range(BLK):
            slot = slots[BLK * i + b]
            total[slot] = total[slot] + got[i, b].astype(F32)
    for i in range(GRP):
        out[i] = total[BLK * i : BLK * (i + 1)].astype(BF16)


def join_kernel(got, down, up):
    width = down.shape[-1]
    down[0] = got[:, 0, :, :width]
    up[0] = got[:, 0, :, width:]


def back_kernel(count, order, cot, cot_pair, own, pair, *refs):
    outs, (ready, out_sems) = refs[:count], refs[count:]
    i = pl.program_id(0)
    copies = [pltpu.make_async_copy(ready.at[k % 2], outs[k], out_sems.at[k % 2]) for k in range(count)]
    for k in range(2, count):

        @pl.when(i == k)
        def _():
            copies[k - 2].wait()

    value = lax.dot_general(cot[...], own[0], NT, preferred_element_type=F32)
    value += lax.dot_general(cot_pair[...], pair[0], NT, preferred_element_type=F32)
    ready[lax.rem(i, 2)] = value.astype(BF16)
    for k in range(count):

        @pl.when(i == k)
        def _():
            copies[k].start()

    @pl.when(i == count - 1)
    def _():
        copies[-2].wait()
        copies[-1].wait()


def backward(cot, cot_pair, weight, pair, order):
    count = order.shape[0]
    rows, wide = cot.shape
    depth = weight.shape[1]
    whole = pl.BlockSpec((rows, wide), lambda i, order: (0, 0))
    block = pl.BlockSpec((1, depth, wide), lambda i, order: (order[i], 0, 0))
    return pl.pallas_call(
        functools.partial(back_kernel, count),
        grid_spec=pltpu.PrefetchScalarGridSpec(
            num_scalar_prefetch=1,
            grid=(count,),
            in_specs=[whole, whole, block, block],
            out_specs=[HBM] * count,
            scratch_shapes=[pltpu.VMEM((2, rows, depth), BF16), pltpu.SemaphoreType.DMA((2,))],
        ),
        out_shape=[pltpu.HBM((rows, depth), BF16)] * count,
        compiler_params=params(30),
        cost_estimate=COST,
        name="backward",
    )(order, cot, cot_pair, weight, pair)


def ahead_kernel(count, order, *refs):
    pieces, (own, pair, ranks, adapters, out, out_pair) = refs[:count], refs[count : count + 6]
    held, total, sems = refs[count + 6 :]
    i = pl.program_id(0)
    copies = [pltpu.make_async_copy(s, held.at[k], sems.at[k]) for k, s in enumerate(pieces)]

    @pl.when(i == 0)
    def _():
        for copy in copies:
            copy.start()
        rank = adapters.shape[1]
        rows = ranks.shape[0] // BLK
        width = adapters.shape[2] - out.shape[1]
        for b in range(BLK):
            span = slice(b * rows, (b + 1) * rows)
            out[span, :] = SCALE * jnp.dot(ranks[span, :rank], adapters[b, :, width:], preferred_element_type=F32)
        total[...] = jnp.zeros_like(total)

    for k in range(count):

        @pl.when(i == k)
        def _():
            copies[k].wait()

    out[...] += jnp.dot(held[i], own[0], preferred_element_type=F32)
    total[...] += jnp.dot(held[i], pair[0], preferred_element_type=F32)

    @pl.when(i == count - 1)
    def _():
        out_pair[...] = total[...].astype(BF16)


def ahead(pieces, weight, pair, ranks, adapters, order):
    count = len(pieces)
    rows, depth = pieces[0].shape
    wide = weight.shape[2]
    block = pl.BlockSpec((1, depth, wide), lambda i, order: (order[i], 0, 0))
    total = pl.BlockSpec((rows, wide), lambda i, order: (0, 0))
    return pl.pallas_call(
        functools.partial(ahead_kernel, count),
        grid_spec=pltpu.PrefetchScalarGridSpec(
            num_scalar_prefetch=1,
            grid=(count,),
            in_specs=[HBM] * count
            + [
                block,
                block,
                pl.BlockSpec(ranks.shape, lambda i, order: (0, 0)),
                pl.BlockSpec(adapters.shape, lambda i, order: (0, 0, 0)),
            ],
            out_specs=[total, total],
            scratch_shapes=[
                pltpu.VMEM((count, rows, depth), BF16),
                pltpu.VMEM((rows, wide), F32),
                pltpu.SemaphoreType.DMA((count,)),
            ],
        ),
        out_shape=[jax.ShapeDtypeStruct((rows, wide), F32), jax.ShapeDtypeStruct((rows, wide), BF16)],
        compiler_params=params(30),
        cost_estimate=COST,
        name="ahead",
    )(order, *pieces, weight, pair, ranks, adapters)


def close_kernel(here, back, fwd, across, ranks, adapters, out):
    rank = adapters.shape[1]
    width = out.shape[1]
    value = here[...].astype(F32) + back[...].astype(F32) + fwd[...].astype(F32) + across[...].astype(F32)
    low = jnp.dot(ranks[:, rank:], adapters[0, :, :width], preferred_element_type=F32)
    out[...] = (value + SCALE * low).astype(BF16)


def add_kernel(a0, a1, b0, b1, b2, out_a, out_b):
    out_a[...] = (a0[...].astype(F32) + a1[...].astype(F32)).astype(BF16)
    out_b[...] = (b0[...].astype(F32) + b1[...].astype(F32) + b2[...].astype(F32)).astype(BF16)


def add_both(*terms):
    rows, wide = terms[0].shape
    spec = pl.BlockSpec((rows // 2, wide), lambda i: (i, 0))
    return pl.pallas_call(
        add_kernel,
        grid=(2,),
        in_specs=[spec] * len(terms),
        out_specs=[spec] * 2,
        out_shape=[jax.ShapeDtypeStruct((rows, wide), BF16)] * 2,
        compiler_params=params(WIDE),
        cost_estimate=COST,
        name="add_both",
    )(*terms)


def one_kernel(a0, a1, out):
    out[...] = (a0[...].astype(F32) + a1[...].astype(F32)).astype(BF16)


def add(*terms):
    rows, wide = terms[0].shape
    spec = pl.BlockSpec((rows // 2, wide), lambda i: (i, 0))
    return pl.pallas_call(
        one_kernel,
        grid=(2,),
        in_specs=[spec] * 2,
        out_specs=spec,
        out_shape=jax.ShapeDtypeStruct((rows, wide), BF16),
        compiler_params=params(WIDE),
        cost_estimate=COST,
        name="add",
    )(*terms)


def plus(*terms):
    total = terms[0].astype(F32)
    for term in terms[1:]:
        total = total + term.astype(F32)
    return total


def shards(tokens, base_weight, adapt_down, adapt_up, cotangent, tenant, adapter_slot):
    member = lax.axis_index("mem").astype(jnp.int32)
    core, y, x = member % 2, (member // 2) % YY, member // (2 * YY)
    rows, feats = tokens.shape
    hidden = cotangent.shape[1]
    both = feats + hidden
    per_group, _, rank = adapt_down.shape
    piece = rank // GRP
    block_rows = rows // BLK

    match = tenant[:, None] == jnp.arange(adapter_slot.shape[0], dtype=jnp.int32)[None, :]
    slots = jnp.sum(jnp.where(match, adapter_slot[None, :], 0), axis=1)

    def block_order(c):
        d = 1 - 2 * c
        steps = ((0, 0), (1, 0), (0, -d), (0, d), (1, -d), (1, d), (0, 2), (1, 2))
        return jnp.stack([((x ^ dx) * YY + (y + dy + YY) % YY) * 2 + c for dx, dy in steps]).astype(jnp.int32)

    order = block_order(core)
    piece_shape = pltpu.HBM((GRP, per_group, piece, both), BF16)
    all_pieces = pl.BlockSpec(piece_shape.shape, lambda i: (0, 0, 0, 0))
    weight = stay(base_weight.reshape(2 * XL * YY, feats, hidden))

    pair_w = stay(send(base_weight, "core", "w_all").reshape(weight.shape))
    t_x = stay(send(tokens, "x", "t_x"))
    t_f = stay(send(tokens, "fwd", "t_f"))
    t_b = stay(send(tokens, "back", "t_b"))
    cot_pair = send(cotangent, "core", "c_cot")
    cut = pl.pallas_call(
        cut_kernel,
        grid=(per_group,),
        in_specs=[
            pl.BlockSpec((1, GRP, piece, feats), lambda b: (b, 0, 0, 0)),
            pl.BlockSpec((1, GRP, piece, hidden), lambda b: (b, 0, 0, 0)),
        ],
        out_specs=pl.BlockSpec((GRP, 1, piece, both), lambda b: (0, b, 0, 0)),
        out_shape=piece_shape,
        compiler_params=params(WIDE),
        cost_estimate=COST,
        name="cut",
    )(
        stay(jnp.swapaxes(adapt_down, 1, 2).reshape(per_group, GRP, piece, feats)),
        stay(adapt_up.reshape(per_group, GRP, piece, hidden)),
    )
    got = exchange(cut)
    got, t_x, t_f, t_b = lax.optimization_barrier((got, t_x, t_f, t_b))

    t_ff = stay(send(t_f, "fwd", "t_ff"))
    t_xf = stay(send(t_x, "fwd", "t_xf"))
    t_xb = stay(send(t_x, "back", "t_xb"))
    picked = pl.pallas_call(
        pick_kernel,
        grid=(1,),
        in_specs=[SMEM, all_pieces],
        out_specs=all_pieces,
        out_shape=piece_shape,
        compiler_params=params(4),
        cost_estimate=COST,
        name="pick",
    )(slots, got)
    own = exchange(picked)
    parts = backward(cotangent, cot_pair, weight, pair_w, order)
    own, parts, t_ff, t_xf, t_xb = lax.optimization_barrier((own, parts, t_ff, t_xf, t_xb))
    g00, g10, g0b, g0f, g1b, g1f, g02, g12 = parts

    r_12 = send(g12, "x", "r_12")
    t_xff = stay(send(t_xf, "fwd", "t_xff"))
    adapters, part = pl.pallas_call(
        rank_kernel,
        grid=(BLK,),
        in_specs=[
            pl.BlockSpec((block_rows, feats), lambda b: (b, 0)),
            pl.BlockSpec((block_rows, hidden), lambda b: (b, 0)),
            pl.BlockSpec((GRP, 1, piece, both), lambda b: (0, b, 0, 0)),
        ],
        out_specs=[
            pl.BlockSpec((1, rank, both), lambda b: (b, 0, 0)),
            pl.BlockSpec((block_rows, 2 * rank), lambda b: (b, 0)),
        ],
        out_shape=[
            jax.ShapeDtypeStruct((BLK, rank, both), BF16),
            jax.ShapeDtypeStruct((rows, 2 * rank), F32),
        ],
        compiler_params=params(6),
        cost_estimate=COST,
        name="rank",
    )(tokens, cotangent, own)
    chip = (part + send(part, "core", "k_core")).astype(BF16)
    two = plus(chip, send(chip, "x", "k_x")).astype(BF16)
    ranks = plus(two, send(two, "fwd", "k_f"), send(two, "back", "k_b"), send(two, "far", "k_far")).astype(BF16)
    ranks, r_12, t_xff = lax.optimization_barrier((ranks, r_12, t_xff))

    grads = pl.pallas_call(
        grad_kernel,
        grid=(BLK,),
        in_specs=[
            pl.BlockSpec((block_rows, feats), lambda b: (b, 0)),
            pl.BlockSpec((block_rows, hidden), lambda b: (b, 0)),
            pl.BlockSpec((block_rows, 2 * rank), lambda b: (b, 0)),
        ],
        out_specs=pl.BlockSpec((GRP, 1, piece, both), lambda b: (0, b, 0, 0)),
        out_shape=piece_shape,
        compiler_params=params(6),
        cost_estimate=COST,
        name="grads",
    )(tokens, cotangent, ranks)
    got = exchange(grads)
    r_1b = send(g1b, "back", "r_1b")
    r_1f = send(g1f, "fwd", "r_1f")
    r_02 = send(add(g02, r_12), "back", "r_02")
    sum_0b, sum_10 = add_both(g0b, r_02, g10, r_1b, r_1f)
    r_0f = send(g0f, "fwd", "r_0f")
    r_0b = send(sum_0b, "back", "r_0b")
    r_10 = send(sum_10, "x", "r_10")
    t_xff, sum_0b, sum_10 = lax.optimization_barrier((t_xff, sum_0b, sum_10))
    pieces = (tokens, t_x, t_f, t_b, t_xf, t_xb, t_ff, t_xff)
    own_sum, pair_sum = ahead(pieces, weight, pair_w, ranks, adapters, order)
    got, own_sum, pair_sum, r_0b, r_0f, r_10 = lax.optimization_barrier((got, own_sum, pair_sum, r_0b, r_0f, r_10))

    totals = pl.pallas_call(
        total_kernel,
        grid=(1,),
        in_specs=[SMEM, all_pieces],
        out_specs=all_pieces,
        out_shape=piece_shape,
        scratch_shapes=[pltpu.VMEM((GRP * per_group, piece, both), F32)],
        compiler_params=params(6),
        cost_estimate=COST,
        name="total",
    )(slots, got)
    final = exchange(totals)
    mixed = (own_sum + send(pair_sum, "core", "c_sum").astype(F32)).astype(BF16)
    step = pl.BlockSpec((block_rows, feats), lambda b: (b, 0))
    token_gradient = pl.pallas_call(
        close_kernel,
        grid=(BLK,),
        in_specs=[
            step,
            step,
            step,
            step,
            pl.BlockSpec((block_rows, 2 * rank), lambda b: (b, 0)),
            pl.BlockSpec((1, rank, both), lambda b: (b, 0, 0)),
        ],
        out_specs=pl.BlockSpec((block_rows, feats), lambda b: (b, 0)),
        out_shape=jax.ShapeDtypeStruct((rows, feats), BF16),
        compiler_params=params(WIDE),
        cost_estimate=COST,
        name="close",
    )(g00, r_0b, r_0f, r_10, ranks, adapters)
    final, mixed, token_gradient = lax.optimization_barrier((final, mixed, token_gradient))
    down_grad, up_grad = pl.pallas_call(
        join_kernel,
        grid=(per_group,),
        in_specs=[pl.BlockSpec((GRP, 1, piece, both), lambda b: (0, b, 0, 0))],
        out_specs=[
            pl.BlockSpec((1, GRP, piece, feats), lambda b: (b, 0, 0, 0)),
            pl.BlockSpec((1, GRP, piece, hidden), lambda b: (b, 0, 0, 0)),
        ],
        out_shape=[
            jax.ShapeDtypeStruct((per_group, GRP, piece, feats), BF16),
            jax.ShapeDtypeStruct((per_group, GRP, piece, hidden), BF16),
        ],
        compiler_params=params(4),
        cost_estimate=COST,
        name="join",
    )(final)
    down_grad = jnp.swapaxes(down_grad.reshape(per_group, rank, feats), 1, 2)
    return mixed, token_gradient, down_grad, up_grad.reshape(per_group, rank, hidden)


def solution(mesh):
    in_specs = (
        P("grp", "mem"),
        P(None, "mem"),
        P("grp", "mem", None),
        P("grp", None, "mem"),
        P("grp", "mem"),
        P(),
        P(),
    )
    out_specs = (P("grp", "mem"), P("grp", "mem"), P("grp", "mem", None), P("grp", None, "mem"))
    return jax.shard_map(shards, mesh=mesh, in_specs=in_specs, out_specs=out_specs, check_vma=False)
```

time: 511 us -> 150 us (0.29)
  waiting for transfers between devices: 366 us -> 33.5 us
  starting transfers between devices: 0.46 us -> 59.1 us
  matrix products: 52.5 us -> 0 us
  blocking collectives: 52.1 us -> 0 us
  Pallas kernels: 0 us -> 49.1 us
  local copies, waits for them, and re-layouts: 17.4 us -> 3.88 us
  between operations: 14.3 us -> 0.85 us
    reduce_scatter x3 -> x0, waiting for transfers between devices: 236 us -> none  [the longest x1 112 us: shards(): lax.psum_scatter(dense_up, 'grp', scatter_dimension=0, tiled=True)]
    all_gather x4 -> x0, waiting for transfers between devices: 128 us -> none  [the longest x1 63.7 us: shards(): lax.all_gather(adapt_up, 'grp', axis=0, tiled=True)]
    dot_general x10 -> x0, matrix products: 52.5 us -> none  [the longest x1 22 us: shards(): lax.dot_general(cotangent, base_weight, (((1,), (1,)), ((), ())), preferr...]
    psum x1 -> x0, blocking collectives: 52.1 us -> none  [shards(): cot_sum = lax.psum(cot_part, 'mem')]
    pallas_call x0 -> x11, Pallas kernels: none -> 49.1 us  [the longest x1 14.5 us: backward(): pl.pallas_call(functools.partial(back_kernel, count), grid_spec=pltpu.Pre...]
    ppermute x0 -> x22, starting transfers between devices: none -> 29.9 us  [send(): return lax.ppermute(value, 'mem', MOVES[move])]
    all_to_all x0 -> x4, starting transfers between devices: none -> 29.2 us  [exchange(): return lax.all_to_all(pieces, 'grp', 0, 0, tiled=True)]
    ppermute x0 -> x22, waiting for transfers between devices: none -> 28.4 us  [send(): return lax.ppermute(value, 'mem', MOVES[move])]
  transfers between devices with their start and end apart: 7 -> 26, of which waited for: 6 -> 12; matrix products, arithmetic and copies ran while one was open for 15% -> 2% of each run, Pallas kernels for 0% -> 31%
where the time goes in v2:
time: 150 us; the launch traced here: 149 us
  starting transfers between devices  59.1 us (39%)
  Pallas kernels  49.1 us (33%)
  waiting for transfers between devices  33.5 us (22%)
  local copies, waits for them, and re-layouts  3.88 us (3%)
  other arithmetic  2.58 us (2%)
    ppermute x22, starting transfers between devices, send(): return lax.ppermute(value, 'mem', MOVES[move])  29.9 us
    all_to_all x4, starting transfers between devices, exchange(): return lax.all_to_all(pieces, 'grp', 0, 0, tiled=True)  29.2 us
    ppermute x22, waiting for transfers between devices, send(): return lax.ppermute(value, 'mem', MOVES[move])  28.4 us
    pallas_call x1, Pallas kernels, backward(): pl.pallas_call(functools.partial(back_kernel, count), grid_spec=pltpu.Pre...  14.5 us
    pallas_call x1, Pallas kernels, ahead(): pl.pallas_call(functools.partial(ahead_kernel, count), grid_spec=pltpu.Pr...  13.8 us
    all_to_all x4, waiting for transfers between devices, exchange(): return lax.all_to_all(pieces, 'grp', 0, 0, tiled=True)  5.06 us
    pallas_call x1, Pallas kernels, shards(): pl.pallas_call(close_kernel, grid=(BLK,), in_specs=[step, step, step, ste...  4.27 us
    unnamed x28, local copies, waits for them, and re-layouts  3.79 us
  transfers between devices with their start and end apart: 26, of which 12 were waited for; matrix products, arithmetic and copies ran while one was open for 2% of the time, Pallas kernels for 31%

profile of v2, /device:TPU:1, one launch (start us, length us, event | category | flops | bytes accessed | tf_op | source)
XLA Modules:
  0.0 149.0 jit_solution(16572820032937240041)
XLA Ops:
  0.7 1.5 %collective-permute-start.4 = (bf16[8192,896]{1,0:T(8,128)(2,1)}, bf16[8192,896]{1,0:T(8,128)(2,1)}, u32[]{:S(2)}, u32[]{:S(2)}) collective-permute-start(bf16[8192,896]{1,0:T(8,128)(2,1)} %param.8), channel_id=1, source_target_pairs={{0,1},{1,0},{2,3},{3,2},{4,5},{5,4},{6,7},{7,6},{8,9},{9,8},{10,11... | collective-permute-start | bytes 44040200 | tf_op jit(solution)/shard_map/w_all/ppermute | solution.py:49
  2.2 3.3 %cut.1 = bf16[8,4,8,1408]{3,2,1,0:T(8,128)(2,1)} custom-call(bf16[4,8,8,512]{3,2,1,0:T(8,128)(2,1)} %bitcast.21, bf16[4,8,8,896]{3,2,1,0:T(8,128)(2,1)} %bitcast.20), custom_call_target="tpu_custom_call" | custom-call | flops 1 | bytes 1 | tf_op jit(solution)/shard_map/cut/pallas_call | solution.py:310
  5.4 7.6 %all-to-all-start = ((bf16[8,4,8,1408]{3,2,1,0:T(8,128)(2,1)}), bf16[8,4,8,1408]{3,2,1,0:T(8,128)(2,1)S(1)}, u32[]{:S(2)}, u32[]{:S(2)}) async-start(bf16[8,4,8,1408]{3,2,1,0:T(8,128)(2,1)} %cut.1), calls=%async_computation | async-start | bytes 1441792 | tf_op jit(solution)/shard_map/all_to_all | solution.py:57
  13.0 1.4 collective-permute-start.2
  14.4 1.5 %collective-permute-start.1 = (bf16[512,512]{1,0:T(8,128)(2,1)S(1)}, bf16[512,512]{1,0:T(8,128)(2,1)S(1)}, u32[]{:S(2)}, u32[]{:S(2)}) collective-permute-start(bf16[512,512]{1,0:T(8,128)(2,1)S(1)} %copy-done.1), channel_id=1, source_target_pairs={{0,2},{1,7},{2,4},{3,1},{4,6},{5,3},{6,0},{7,5},{8,10},{9,15},{10,... | collective-permute-start | bytes 1572872 | tf_op jit(solution)/shard_map/t_f/ppermute | solution.py:49
  15.9 0.3 collective-permute-start
  16.2 0.8 collective-permute-start.3
  17.1 0.2 select_reduce_fusion.slots
  17.3 7.2 %collective-permute-done.2.refs_3_ = bf16[512,512]{1,0:T(8,128)(2,1)S(1)} collective-permute-done((bf16[512,512]{1,0:T(8,128)(2,1)S(1)}, bf16[512,512]{1,0:T(8,128)(2,1)S(1)}, u32[]{:S(2)}, u32[]{:S(2)}) %collective-permute-start.2) | collective-permute-done | bytes 524320 | tf_op jit(solution)/shard_map/t_b/ppermute | solution.py:49
  24.5 3.5 %collective-permute-done.1.refs_2_ = bf16[512,512]{1,0:T(8,128)(2,1)S(1)} collective-permute-done((bf16[512,512]{1,0:T(8,128)(2,1)S(1)}, bf16[512,512]{1,0:T(8,128)(2,1)S(1)}, u32[]{:S(2)}, u32[]{:S(2)}) %collective-permute-start.1) | collective-permute-done | bytes 524320 | tf_op jit(solution)/shard_map/t_f/ppermute | solution.py:49
  28.0 0.8 copy-done.8
  28.8 4.6 %collective-permute-done.refs_1_ = bf16[512,512]{1,0:T(8,128)(2,1)} collective-permute-done((bf16[512,512]{1,0:T(8,128)(2,1)S(1)}, bf16[512,512]{1,0:T(8,128)(2,1)}, u32[]{:S(2)}, u32[]{:S(2)}) %collective-permute-start) | collective-permute-done | bytes 524320 | tf_op jit(solution)/shard_map/t_x/ppermute | solution.py:49
  33.4 0.0 all-to-all-done.got
  33.4 1.6 %pick.1 = bf16[8,4,8,1408]{3,2,1,0:T(8,128)(2,1)} custom-call(s32[32]{0:T(128)S(1)} %select_reduce_fusion.slots, bf16[8,4,8,1408]{3,2,1,0:T(8,128)(2,1)S(1)} %all-to-all-done.got), custom_call_target="tpu_custom_call" | custom-call | flops 1 | bytes 1 | tf_op jit(solution)/shard_map/pick/pallas_call | solution.py:332
  35.0 6.9 %all-to-all-start.1 = ((bf16[8,4,8,1408]{3,2,1,0:T(8,128)(2,1)}), bf16[8,4,8,1408]{3,2,1,0:T(8,128)(2,1)S(1)}, u32[]{:S(2)}, u32[]{:S(2)}) async-start(bf16[8,4,8,1408]{3,2,1,0:T(8,128)(2,1)} %pick.1), calls=%async_computation.1 | async-start | bytes 1441792 | tf_op jit(solution)/shard_map/all_to_all | solution.py:57
  41.9 2.7 %collective-permute-start.5 = (bf16[512,512]{1,0:T(8,128)(2,1)}, bf16[512,512]{1,0:T(8,128)(2,1)}, u32[]{:S(2)}, u32[]{:S(2)}) collective-permute-start(bf16[512,512]{1,0:T(8,128)(2,1)} %copy-done.8), channel_id=1, source_target_pairs={{0,2},{1,7},{2,4},{3,1},{4,6},{5,3},{6,0},{7,5},{8,10},{9,15},{10,... | collective-permute-start | bytes 1572872 | tf_op jit(solution)/shard_map/t_ff/ppermute | solution.py:49
  44.7 0.0 collective-permute-start.7
  44.7 2.7 %collective-permute-start.6 = (bf16[512,512]{1,0:T(8,128)(2,1)}, bf16[512,512]{1,0:T(8,128)(2,1)}, u32[]{:S(2)}, u32[]{:S(2)}) collective-permute-start(bf16[512,512]{1,0:T(8,128)(2,1)} %collective-permute-done.refs_1_), channel_id=1, source_target_pairs={{0,2},{1,7},{2,4},{3,1},{4,6},{5,3},{6,0},{7,5},{8,10},{9,15},{10,... | collective-permute-start | bytes 1572872 | tf_op jit(solution)/shard_map/t_xf/ppermute | solution.py:49
  47.3 0.1 stack.35.order
  47.4 0.0 collective-permute-done.3.cot_pair
  47.4 0.0 collective-permute-done.4
  47.4 14.5 %backward.1 = (bf16[512,512]{1,0:T(8,128)(2,1)}, bf16[512,512]{1,0:T(8,128)(2,1)}, bf16[512,512]{1,0:T(8,128)(2,1)}, bf16[512,512]{1,0:T(8,128)(2,1)}, bf16[512,...) custom-call(s32[8]{0:T(128)S(1)} %stack.35.order, ...), custom_call_target="tpu_custom_call" | custom-call | flops 1 | bytes 1 | tf_op jit(solution)/shard_map/backward/pallas_call | solution.py:148
  61.9 0.0 collective-permute-done.5.refs_6_
  62.0 0.4 collective-permute-done.6.refs_4_
  62.3 0.0 all-to-all-done.1.got
  62.4 1.4 rank.1
  63.7 3.1 %collective-permute-start.8 = (f32[512,128]{1,0:T(8,128)S(1)}, f32[512,128]{1,0:T(8,128)S(1)}, u32[]{:S(2)}, u32[]{:S(2)}) collective-permute-start(f32[512,128]{1,0:T(8,128)S(1)} %get-tuple-element.61), channel_id=1, source_target_pairs={{0,1},{1,0},{2,3},{3,2},{4,5},{5,4},{6,7},{7,6},{8,9},{9,8},{10,11... | collective-permute-start | bytes 786440 | tf_op jit(solution)/shard_map/k_core/ppermute | solution.py:49
  66.8 1.2 collective-permute-done.8
  68.0 0.1 collective-permute-start.9
  68.1 1.4 collective-permute-start.13
  69.6 0.5 collective-permute-start.14
  70.1 2.8 %collective-permute-done.9 = bf16[512,128]{1,0:T(8,128)(2,1)S(1)} collective-permute-done((bf16[512,128]{1,0:T(8,128)(2,1)S(1)}, bf16[512,128]{1,0:T(8,128)(2,1)S(1)}, u32[]{:S(2)}, u32[]{:S(2)}) %collective-permute-start.9) | collective-permute-done | bytes 131104 | tf_op jit(solution)/shard_map/k_x/ppermute | solution.py:49
  72.9 0.1 collective-permute-start.12
  73.0 1.3 collective-permute-start.11
  74.2 1.5 collective-permute-start.10
  75.7 4.0 %collective-permute-done.12 = bf16[512,128]{1,0:T(8,128)(2,1)S(1)} collective-permute-done((bf16[512,128]{1,0:T(8,128)(2,1)S(1)}, bf16[512,128]{1,0:T(8,128)(2,1)S(1)}, u32[]{:S(2)}, u32[]{:S(2)}) %collective-permute-start.12) | collective-permute-done | bytes 131104 | tf_op jit(solution)/shard_map/k_far/ppermute | solution.py:49
  79.7 1.1 collective-permute-start.16
  80.8 0.4 collective-permute-done.11
  81.2 2.4 %collective-permute-start.17 = (bf16[512,512]{1,0:T(8,128)(2,1)}, bf16[512,512]{1,0:T(8,128)(2,1)}, u32[]{:S(2)}, u32[]{:S(2)}) collective-permute-start(bf16[512,512]{1,0:T(8,128)(2,1)} %get-tuple-element.74), channel_id=1, source_target_pairs={{0,2},{1,7},{2,4},{3,1},{4,6},{5,3},{6,0},{7,5},{8,10},{9,15},{10,... | collective-permute-start | bytes 1572872 | tf_op jit(solution)/shard_map/r_1f/ppermute | solution.py:49
  83.7 0.1 collective-permute-done.10
  83.8 0.1 add_convert_fusion.1.ranks.refs_10_
  83.9 0.0 copy-start.3
  83.9 0.2 collective-permute-done.13.a1
  84.1 0.8 copy-done.10
  84.8 2.2 %add.160 = bf16[512,512]{1,0:T(8,128)(2,1)} custom-call(bf16[512,512]{1,0:T(8,128)(2,1)} %get-tuple-element.70.a0, bf16[512,512]{1,0:T(8,128)(2,1)} %copy-done.10), custom_call_target="tpu_custom_call" | custom-call | flops 1 | bytes 1 | tf_op jit(solution)/shard_map/add/pallas_call | solution.py:263
  87.0 0.0 collective-permute-start.15
  87.0 2.3 %grads.1 = bf16[8,4,8,1408]{3,2,1,0:T(8,128)(2,1)} custom-call(bf16[512,512]{1,0:T(8,128)(2,1)S(1)} %copy-done.1, bf16[512,896]{1,0:T(8,128)(2,1)S(1)} %copy-done, bf16[512,128]{1,0:T(8,128)(2,1)S(1)} %add_convert_fusion.1.ranks.refs_10_), custom_call_target="tpu_custom_call" | custom-call | flops 1 | bytes 1 | tf_op jit(solution)/shard_map/grads/pallas_call | solution.py:374
  89.3 6.9 %all-to-all-start.2 = ((bf16[8,4,8,1408]{3,2,1,0:T(8,128)(2,1)}), bf16[8,4,8,1408]{3,2,1,0:T(8,128)(2,1)S(1)}, u32[]{:S(2)}, u32[]{:S(2)}) async-start(bf16[8,4,8,1408]{3,2,1,0:T(8,128)(2,1)} %grads.1), calls=%async_computation.2 | async-start | bytes 1441792 | tf_op jit(solution)/shard_map/all_to_all | solution.py:57
  96.3 2.7 %collective-permute-start.19 = (bf16[512,512]{1,0:T(8,128)(2,1)}, bf16[512,512]{1,0:T(8,128)(2,1)}, u32[]{:S(2)}, u32[]{:S(2)}) collective-permute-start(bf16[512,512]{1,0:T(8,128)(2,1)} %get-tuple-element.81), channel_id=1, source_target_pairs={{0,2},{1,7},{2,4},{3,1},{4,6},{5,3},{6,0},{7,5},{8,10},{9,15},{10,... | collective-permute-start | bytes 1572872 | tf_op jit(solution)/shard_map/r_0f/ppermute | solution.py:49
  99.0 0.0 collective-permute-done.17.b2
  99.0 4.0 %collective-permute-done.15.a1 = bf16[512,512]{1,0:T(8,128)(2,1)} collective-permute-done((bf16[512,512]{1,0:T(8,128)(2,1)}, bf16[512,512]{1,0:T(8,128)(2,1)}, u32[]{:S(2)}, u32[]{:S(2)}) %collective-permute-start.15) | collective-permute-done | bytes 524320 | tf_op jit(solution)/shard_map/r_02/ppermute | solution.py:49
  103.0 2.5 %add_both.1 = (bf16[512,512]{1,0:T(8,128)(2,1)}, bf16[512,512]{1,0:T(8,128)(2,1)}) custom-call(bf16[512,512]{1,0:T(8,128)(2,1)} %get-tuple-element.69.a0, bf16[512,512]{1,0:T(8,128)(2,1)} %collective-permute-done.15.a1, bf16[512,512]{1,0:T(8,128)(2,1)} %get-tuple-element.72.b0, bf16[512,512]{1,0:T(8,128)(2,1)} %collective-permute-done.16.b1, ...), custom_call_target="tpu_custom_call" | custom-call | flops 1 | bytes 1 | tf_op jit(solution)/shard_map/add_both/pallas_call | solution.py:244
  105.5 0.1 collective-permute-start.20
  105.6 13.8 %ahead.1 = (f32[512,896]{1,0:T(8,128)S(1)}, bf16[512,896]{1,0:T(8,128)(2,1)S(1)}) custom-call(s32[8]{0:T(128)S(1)} %stack.35.order, bf16[512,512]{1,0:T(8,128)(2,1)S(1)} %copy-done.1, bf16[512,512]{1,0:T(8,128)(2,1)} %collective-permute-done.refs_1_, bf16[512,512]{1,0:T(8,128)(2,1)} %copy-done.8, bf16[512,512]{1,0:T(8,128)(2,1)} %copy-done.7, ...), custom_call_target="tpu_custom_call" | custom-call | flops 1 | bytes 1 | tf_op jit(solution)/shard_map/ahead/pallas_call | solution.py:202
  119.5 1.3 copy-done.4
  120.7 0.9 copy-done.6
  121.7 0.0 collective-permute-done.20.across
  121.7 4.8 %collective-permute-start.21 = (bf16[512,896]{1,0:T(8,128)(2,1)}, bf16[512,896]{1,0:T(8,128)(2,1)}, u32[]{:S(2)}, u32[]{:S(2)}) collective-permute-start(bf16[512,896]{1,0:T(8,128)(2,1)} %copy-done.6), channel_id=1, source_target_pairs={{0,1},{1,0},{2,3},{3,2},{4,5},{5,4},{6,7},{7,6},{8,9},{9,8},{10,11... | collective-permute-start | bytes 2752520 | tf_op jit(solution)/shard_map/c_sum/ppermute | solution.py:49
  126.4 1.8 %total.1 = bf16[8,4,8,1408]{3,2,1,0:T(8,128)(2,1)} custom-call(s32[32]{0:T(128)S(1)} %select_reduce_fusion.slots, bf16[8,4,8,1408]{3,2,1,0:T(8,128)(2,1)S(1)} %all-to-all-done.2.got), custom_call_target="tpu_custom_call" | custom-call | flops 1 | bytes 1 | tf_op jit(solution)/shard_map/total/pallas_call | solution.py:401
  128.2 7.7 %all-to-all-start.3 = ((bf16[8,4,8,1408]{3,2,1,0:T(8,128)(2,1)}), bf16[8,4,8,1408]{3,2,1,0:T(8,128)(2,1)S(1)}, u32[]{:S(2)}, u32[]{:S(2)}) async-start(bf16[8,4,8,1408]{3,2,1,0:T(8,128)(2,1)} %total.1), calls=%async_computation.3 | async-start | bytes 1441792 | tf_op jit(solution)/shard_map/all_to_all | solution.py:57
  135.9 4.3 %close.1 = bf16[512,512]{1,0:T(8,128)(2,1)} custom-call(bf16[512,512]{1,0:T(8,128)(2,1)} %get-tuple-element.85.here, bf16[512,512]{1,0:T(8,128)(2,1)} %collective-permute-done.18.back, bf16[512,512]{1,0:T(8,128)(2,1)} %collective-permute-done.19.fwd, bf16[512,512]{1,0:T(8,128)(2,1)} %collective-permute-done.20.across, bf16[512,128]{1,0:T(8,128)(2,1)} %copy-done.3, ...), custom_call_target="tpu_custom_call" | custom-call | flops 1 | bytes 1 | tf_op jit(solution)/shard_map/close/pallas_call | solution.py:415
  140.2 2.3 %add_convert_fusion = bf16[512,896]{1,0:T(8,128)(2,1)} fusion(f32[512,896]{1,0:T(8,128)S(1)} %copy-done.5, bf16[512,896]{1,0:T(8,128)(2,1)} %collective-permute-done.21), kind=kLoop, calls=%fused_computation | loop fusion | flops 1376256 | bytes 3670016 | tf_op jit(solution)/shard_map/convert_element_type | solution.py:413
  142.4 5.1 %all-to-all-done.3.got = bf16[8,4,8,1408]{3,2,1,0:T(8,128)(2,1)S(1)} async-done(((bf16[8,4,8,1408]{3,2,1,0:T(8,128)(2,1)}), bf16[8,4,8,1408]{3,2,1,0:T(8,128)(2,1)S(1)}, u32[]{:S(2)}, u32[]{:S(2)}) %all-to-all-start.3) | async-done | bytes 720928 | tf_op jit(solution)/shard_map/all_to_all | solution.py:57
  147.5 1.5 join.1
  (33 shorter events, 0.1 us)
Async XLA Ops:
  0.6 12.4 %copy-start.1 = (bf16[512,512]{1,0:T(8,128)(2,1)S(1)}, bf16[512,512]{1,0:T(8,128)(2,1)}, u32[]{:S(2)}) copy-start(bf16[512,512]{1,0:T(8,128)(2,1)} %refs_0_.1) | copy-start | bytes 1572868
  0.6 15.6 %copy-start = (bf16[512,896]{1,0:T(8,128)(2,1)S(1)}, bf16[512,896]{1,0:T(8,128)(2,1)}, u32[]{:S(2)}) copy-start(bf16[512,896]{1,0:T(8,128)(2,1)} %cot.5) | copy-start | bytes 2752516
  0.7 16.4 %copy-start.12 = (s32[32]{0:T(128)S(1)}, s32[32]{0:T(128)}, u32[]{:S(2)}) copy-start(s32[32]{0:T(128)} %param.13) | copy-start | bytes 388
  0.7 16.4 %copy-start.13 = (s32[32]{0:T(128)S(1)}, s32[32]{0:T(128)}, u32[]{:S(2)}) copy-start(s32[32]{0:T(128)} %param.12) | copy-start | bytes 388
  0.7 46.8 %collective-permute-start.4 = (bf16[8192,896]{1,0:T(8,128)(2,1)}, bf16[8192,896]{1,0:T(8,128)(2,1)}, u32[]{:S(2)}, u32[]{:S(2)}) collective-permute-start(bf16[8192,896]{1,0:T(8,128)(2,1)} %param.8), channel_id=1, source_target_pairs={{0,1},{1,0},{2,3},{3,2},{4,5},{5,4},{6,7},{7,6},{8,9},{9,8},{10,11... | collective-permute-start | bytes 44040200 | tf_op jit(solution)/shard_map/w_all/ppermute | solution.py:49
  5.4 28.0 %all-to-all-start = ((bf16[8,4,8,1408]{3,2,1,0:T(8,128)(2,1)}), bf16[8,4,8,1408]{3,2,1,0:T(8,128)(2,1)S(1)}, u32[]{:S(2)}, u32[]{:S(2)}) async-start(bf16[8,4,8,1408]{3,2,1,0:T(8,128)(2,1)} %cut.1), calls=%async_computation | async-start | bytes 1441792 | tf_op jit(solution)/shard_map/all_to_all | solution.py:57
  13.0 11.4 %collective-permute-start.2 = (bf16[512,512]{1,0:T(8,128)(2,1)S(1)}, bf16[512,512]{1,0:T(8,128)(2,1)S(1)}, u32[]{:S(2)}, u32[]{:S(2)}) collective-permute-start(bf16[512,512]{1,0:T(8,128)(2,1)S(1)} %copy-done.1), channel_id=1, source_target_pairs={{0,6},{1,3},{2,0},{3,5},{4,2},{5,7},{6,4},{7,1},{8,14},{9,11},{10,... | collective-permute-start | bytes 1572872 | tf_op jit(solution)/shard_map/t_b/ppermute | solution.py:49
  14.4 13.6 %collective-permute-start.1 = (bf16[512,512]{1,0:T(8,128)(2,1)S(1)}, bf16[512,512]{1,0:T(8,128)(2,1)S(1)}, u32[]{:S(2)}, u32[]{:S(2)}) collective-permute-start(bf16[512,512]{1,0:T(8,128)(2,1)S(1)} %copy-done.1), channel_id=1, source_target_pairs={{0,2},{1,7},{2,4},{3,1},{4,6},{5,3},{6,0},{7,5},{8,10},{9,15},{10,... | collective-permute-start | bytes 1572872 | tf_op jit(solution)/shard_map/t_f/ppermute | solution.py:49
  15.9 17.5 %collective-permute-start = (bf16[512,512]{1,0:T(8,128)(2,1)S(1)}, bf16[512,512]{1,0:T(8,128)(2,1)}, u32[]{:S(2)}, u32[]{:S(2)}) collective-permute-start(bf16[512,512]{1,0:T(8,128)(2,1)S(1)} %copy-done.1), channel_id=1, source_target_pairs={{0,8},{1,9},{2,10},{3,11},{4,12},{5,13},{6,14},{7,15},{8,0},{9,1},... | collective-permute-start | bytes 1572872 | tf_op jit(solution)/shard_map/t_x/ppermute | solution.py:49
  16.2 31.2 %collective-permute-start.3 = (bf16[512,896]{1,0:T(8,128)(2,1)S(1)}, bf16[512,896]{1,0:T(8,128)(2,1)S(1)}, u32[]{:S(2)}, u32[]{:S(2)}) collective-permute-start(bf16[512,896]{1,0:T(8,128)(2,1)S(1)} %copy-done), channel_id=1, source_target_pairs={{0,1},{1,0},{2,3},{3,2},{4,5},{5,4},{6,7},{7,6},{8,9},{9,8},{10,11... | collective-permute-start | bytes 2752520 | tf_op jit(solution)/shard_map/c_cot/ppermute | solution.py:49
  24.5 3.5 %copy-start.7 = (bf16[512,512]{1,0:T(8,128)(2,1)}, bf16[512,512]{1,0:T(8,128)(2,1)S(1)}, u32[]{:S(2)}) copy-start(bf16[512,512]{1,0:T(8,128)(2,1)S(1)} %collective-permute-done.2.refs_3_) | copy-start | bytes 1572868
  28.0 0.8 copy-start.8
  35.0 27.4 %all-to-all-start.1 = ((bf16[8,4,8,1408]{3,2,1,0:T(8,128)(2,1)}), bf16[8,4,8,1408]{3,2,1,0:T(8,128)(2,1)S(1)}, u32[]{:S(2)}, u32[]{:S(2)}) async-start(bf16[8,4,8,1408]{3,2,1,0:T(8,128)(2,1)} %pick.1), calls=%async_computation.1 | async-start | bytes 1441792 | tf_op jit(solution)/shard_map/all_to_all | solution.py:57
  41.9 20.0 %collective-permute-start.5 = (bf16[512,512]{1,0:T(8,128)(2,1)}, bf16[512,512]{1,0:T(8,128)(2,1)}, u32[]{:S(2)}, u32[]{:S(2)}) collective-permute-start(bf16[512,512]{1,0:T(8,128)(2,1)} %copy-done.8), channel_id=1, source_target_pairs={{0,2},{1,7},{2,4},{3,1},{4,6},{5,3},{6,0},{7,5},{8,10},{9,15},{10,... | collective-permute-start | bytes 1572872 | tf_op jit(solution)/shard_map/t_ff/ppermute | solution.py:49
  44.7 17.3 %collective-permute-start.7 = (bf16[512,512]{1,0:T(8,128)(2,1)}, bf16[512,512]{1,0:T(8,128)(2,1)}, u32[]{:S(2)}, u32[]{:S(2)}) collective-permute-start(bf16[512,512]{1,0:T(8,128)(2,1)} %collective-permute-done.refs_1_), channel_id=1, source_target_pairs={{0,6},{1,3},{2,0},{3,5},{4,2},{5,7},{6,4},{7,1},{8,14},{9,11},{10,... | collective-permute-start | bytes 1572872 | tf_op jit(solution)/shard_map/t_xb/ppermute | solution.py:49
  44.7 17.7 %collective-permute-start.6 = (bf16[512,512]{1,0:T(8,128)(2,1)}, bf16[512,512]{1,0:T(8,128)(2,1)}, u32[]{:S(2)}, u32[]{:S(2)}) collective-permute-start(bf16[512,512]{1,0:T(8,128)(2,1)} %collective-permute-done.refs_1_), channel_id=1, source_target_pairs={{0,2},{1,7},{2,4},{3,1},{4,6},{5,3},{6,0},{7,5},{8,10},{9,15},{10,... | collective-permute-start | bytes 1572872 | tf_op jit(solution)/shard_map/t_xf/ppermute | solution.py:49
  62.4 5.8 %copy-start.11 = (bf16[512,512]{1,0:T(8,128)(2,1)S(1)}, bf16[512,512]{1,0:T(8,128)(2,1)}, u32[]{:S(2)}) copy-start(bf16[512,512]{1,0:T(8,128)(2,1)} %get-tuple-element.62) | copy-start | bytes 1572868
  63.7 41.9 %copy-start.2 = (bf16[4,64,1408]{2,1,0:T(8,128)(2,1)}, bf16[4,64,1408]{2,1,0:T(8,128)(2,1)S(1)}, u32[]{:S(2)}) copy-start(bf16[4,64,1408]{2,1,0:T(8,128)(2,1)S(1)} %get-tuple-element.78.refs_11_.adapters) | copy-start | bytes 2162692
  63.7 4.2 %collective-permute-start.8 = (f32[512,128]{1,0:T(8,128)S(1)}, f32[512,128]{1,0:T(8,128)S(1)}, u32[]{:S(2)}, u32[]{:S(2)}) collective-permute-start(f32[512,128]{1,0:T(8,128)S(1)} %get-tuple-element.61), channel_id=1, source_target_pairs={{0,1},{1,0},{2,3},{3,2},{4,5},{5,4},{6,7},{7,6},{8,9},{9,8},{10,11... | collective-permute-start | bytes 786440 | tf_op jit(solution)/shard_map/k_core/ppermute | solution.py:49
  68.0 4.8 %collective-permute-start.9 = (bf16[512,128]{1,0:T(8,128)(2,1)S(1)}, bf16[512,128]{1,0:T(8,128)(2,1)S(1)}, u32[]{:S(2)}, u32[]{:S(2)}) collective-permute-start(bf16[512,128]{1,0:T(8,128)(2,1)S(1)} %add_convert_fusion.3), channel_id=1, source_target_pairs={{0,8},{1,9},{2,10},{3,11},{4,12},{5,13},{6,14},{7,15},{8,0},{9,1},... | collective-permute-start | bytes 393224 | tf_op jit(solution)/shard_map/k_x/ppermute | solution.py:49
  68.1 15.9 %collective-permute-start.13 = (bf16[512,512]{1,0:T(8,128)(2,1)S(1)}, bf16[512,512]{1,0:T(8,128)(2,1)S(1)}, u32[]{:S(2)}, u32[]{:S(2)}) collective-permute-start(bf16[512,512]{1,0:T(8,128)(2,1)S(1)} %copy-done.11), channel_id=1, source_target_pairs={{0,8},{1,9},{2,10},{3,11},{4,12},{5,13},{6,14},{7,15},{8,0},{9,1},... | collective-permute-start | bytes 1572872 | tf_op jit(solution)/shard_map/r_12/ppermute | solution.py:49
  69.6 14.5 %collective-permute-start.14 = (bf16[512,512]{1,0:T(8,128)(2,1)}, bf16[512,512]{1,0:T(8,128)(2,1)S(1)}, u32[]{:S(2)}, u32[]{:S(2)}) collective-permute-start(bf16[512,512]{1,0:T(8,128)(2,1)} %collective-permute-done.6.refs_4_), channel_id=1, source_target_pairs={{0,2},{1,7},{2,4},{3,1},{4,6},{5,3},{6,0},{7,5},{8,10},{9,15},{10,... | collective-permute-start | bytes 1572872 | tf_op jit(solution)/shard_map/t_xff/ppermute | solution.py:49
  72.9 6.9 %collective-permute-start.12 = (bf16[512,128]{1,0:T(8,128)(2,1)S(1)}, bf16[512,128]{1,0:T(8,128)(2,1)S(1)}, u32[]{:S(2)}, u32[]{:S(2)}) collective-permute-start(bf16[512,128]{1,0:T(8,128)(2,1)S(1)} %add_convert_fusion.2), channel_id=1, source_target_pairs={{0,4},{1,5},{2,6},{3,7},{4,0},{5,1},{6,2},{7,3},{8,12},{9,13},{10,... | collective-permute-start | bytes 393224 | tf_op jit(solution)/shard_map/k_far/ppermute | solution.py:49
  73.0 8.3 %collective-permute-start.11 = (bf16[512,128]{1,0:T(8,128)(2,1)S(1)}, bf16[512,128]{1,0:T(8,128)(2,1)S(1)}, u32[]{:S(2)}, u32[]{:S(2)}) collective-permute-start(bf16[512,128]{1,0:T(8,128)(2,1)S(1)} %add_convert_fusion.2), channel_id=1, source_target_pairs={{0,6},{1,3},{2,0},{3,5},{4,2},{5,7},{6,4},{7,1},{8,14},{9,11},{10,... | collective-permute-start | bytes 393224 | tf_op jit(solution)/shard_map/k_b/ppermute | solution.py:49
  74.2 9.5 %collective-permute-start.10 = (bf16[512,128]{1,0:T(8,128)(2,1)S(1)}, bf16[512,128]{1,0:T(8,128)(2,1)S(1)}, u32[]{:S(2)}, u32[]{:S(2)}) collective-permute-start(bf16[512,128]{1,0:T(8,128)(2,1)S(1)} %add_convert_fusion.2), channel_id=1, source_target_pairs={{0,2},{1,7},{2,4},{3,1},{4,6},{5,3},{6,0},{7,5},{8,10},{9,15},{10,... | collective-permute-start | bytes 393224 | tf_op jit(solution)/shard_map/k_f/ppermute | solution.py:49
  79.7 19.2 %collective-permute-start.16 = (bf16[512,512]{1,0:T(8,128)(2,1)}, bf16[512,512]{1,0:T(8,128)(2,1)}, u32[]{:S(2)}, u32[]{:S(2)}) collective-permute-start(bf16[512,512]{1,0:T(8,128)(2,1)} %get-tuple-element.73), channel_id=1, source_target_pairs={{0,6},{1,3},{2,0},{3,5},{4,2},{5,7},{6,4},{7,1},{8,14},{9,11},{10,... | collective-permute-start | bytes 1572872 | tf_op jit(solution)/shard_map/r_1b/ppermute | solution.py:49
  81.2 17.7 %collective-permute-start.17 = (bf16[512,512]{1,0:T(8,128)(2,1)}, bf16[512,512]{1,0:T(8,128)(2,1)}, u32[]{:S(2)}, u32[]{:S(2)}) collective-permute-start(bf16[512,512]{1,0:T(8,128)(2,1)} %get-tuple-element.74), channel_id=1, source_target_pairs={{0,2},{1,7},{2,4},{3,1},{4,6},{5,3},{6,0},{7,5},{8,10},{9,15},{10,... | collective-permute-start | bytes 1572872 | tf_op jit(solution)/shard_map/r_1f/ppermute | solution.py:49
  83.9 21.8 %copy-start.3 = (bf16[512,128]{1,0:T(8,128)(2,1)}, bf16[512,128]{1,0:T(8,128)(2,1)S(1)}, u32[]{:S(2)}) copy-start(bf16[512,128]{1,0:T(8,128)(2,1)S(1)} %add_convert_fusion.1.ranks.refs_10_) | copy-start | bytes 393220
  84.1 0.8 copy-start.10
  84.8 4.5 %copy-start.9 = (bf16[512,512]{1,0:T(8,128)(2,1)}, bf16[512,512]{1,0:T(8,128)(2,1)S(1)}, u32[]{:S(2)}) copy-start(bf16[512,512]{1,0:T(8,128)(2,1)S(1)} %collective-permute-done.14.refs_7_) | copy-start | bytes 1572868
  87.0 16.0 %collective-permute-start.15 = (bf16[512,512]{1,0:T(8,128)(2,1)}, bf16[512,512]{1,0:T(8,128)(2,1)}, u32[]{:S(2)}, u32[]{:S(2)}) collective-permute-start(bf16[512,512]{1,0:T(8,128)(2,1)} %add.160), channel_id=1, source_target_pairs={{0,6},{1,3},{2,0},{3,5},{4,2},{5,7},{6,4},{7,1},{8,14},{9,11},{10,... | collective-permute-start | bytes 1572872 | tf_op jit(solution)/shard_map/r_02/ppermute | solution.py:49
  89.3 32.3 %all-to-all-start.2 = ((bf16[8,4,8,1408]{3,2,1,0:T(8,128)(2,1)}), bf16[8,4,8,1408]{3,2,1,0:T(8,128)(2,1)S(1)}, u32[]{:S(2)}, u32[]{:S(2)}) async-start(bf16[8,4,8,1408]{3,2,1,0:T(8,128)(2,1)} %grads.1), calls=%async_computation.2 | async-start | bytes 1441792 | tf_op jit(solution)/shard_map/all_to_all | solution.py:57
  96.3 25.4 %collective-permute-start.19 = (bf16[512,512]{1,0:T(8,128)(2,1)}, bf16[512,512]{1,0:T(8,128)(2,1)}, u32[]{:S(2)}, u32[]{:S(2)}) collective-permute-start(bf16[512,512]{1,0:T(8,128)(2,1)} %get-tuple-element.81), channel_id=1, source_target_pairs={{0,2},{1,7},{2,4},{3,1},{4,6},{5,3},{6,0},{7,5},{8,10},{9,15},{10,... | collective-permute-start | bytes 1572872 | tf_op jit(solution)/shard_map/r_0f/ppermute | solution.py:49
  105.5 16.1 %collective-permute-start.18 = (bf16[512,512]{1,0:T(8,128)(2,1)}, bf16[512,512]{1,0:T(8,128)(2,1)}, u32[]{:S(2)}, u32[]{:S(2)}) collective-permute-start(bf16[512,512]{1,0:T(8,128)(2,1)} %get-tuple-element.75), channel_id=1, source_target_pairs={{0,6},{1,3},{2,0},{3,5},{4,2},{5,7},{6,4},{7,1},{8,14},{9,11},{10,... | collective-permute-start | bytes 1572872 | tf_op jit(solution)/shard_map/r_0b/ppermute | solution.py:49
  105.5 16.1 %collective-permute-start.20 = (bf16[512,512]{1,0:T(8,128)(2,1)}, bf16[512,512]{1,0:T(8,128)(2,1)}, u32[]{:S(2)}, u32[]{:S(2)}) collective-permute-start(bf16[512,512]{1,0:T(8,128)(2,1)} %get-tuple-element.76), channel_id=1, source_target_pairs={{0,8},{1,9},{2,10},{3,11},{4,12},{5,13},{6,14},{7,15},{8,0},{9,1},... | collective-permute-start | bytes 1572872 | tf_op jit(solution)/shard_map/r_10/ppermute | solution.py:49
  119.4 1.3 copy-start.4
  120.7 0.9 copy-start.6
  121.7 18.5 %collective-permute-start.21 = (bf16[512,896]{1,0:T(8,128)(2,1)}, bf16[512,896]{1,0:T(8,128)(2,1)}, u32[]{:S(2)}, u32[]{:S(2)}) collective-permute-start(bf16[512,896]{1,0:T(8,128)(2,1)} %copy-done.6), channel_id=1, source_target_pairs={{0,1},{1,0},{2,3},{3,2},{4,5},{5,4},{6,7},{7,6},{8,9},{9,8},{10,11... | collective-permute-start | bytes 2752520 | tf_op jit(solution)/shard_map/c_sum/ppermute | solution.py:49
  128.2 19.3 %all-to-all-start.3 = ((bf16[8,4,8,1408]{3,2,1,0:T(8,128)(2,1)}), bf16[8,4,8,1408]{3,2,1,0:T(8,128)(2,1)S(1)}, u32[]{:S(2)}, u32[]{:S(2)}) async-start(bf16[8,4,8,1408]{3,2,1,0:T(8,128)(2,1)} %total.1), calls=%async_computation.3 | async-start | bytes 1441792 | tf_op jit(solution)/shard_map/all_to_all | solution.py:57
  135.9 4.3 %copy-start.5 = (f32[512,896]{1,0:T(8,128)S(1)}, f32[512,896]{1,0:T(8,128)}, u32[]{:S(2)}) copy-start(f32[512,896]{1,0:T(8,128)} %copy-done.4) | copy-start | bytes 5505028

commit v3 on v2

--- a/solution.py
+++ b/solution.py
@@ -63,8 +63,9 @@
 
 def cut_kernel(down, up, out):
     width = down.shape[-1]
-    out[:, 0, :, :width] = down[0]
-    out[:, 0, :, width:] = up[0]
+    for b in range(down.shape[0]):
+        out[:, b, :, :width] = down[b]
+        out[:, b, :, width:] = up[b]
 
 
 def pick_kernel(slots, got, out):
@@ -162,8 +163,7 @@
 
 
 def ahead_kernel(count, order, *refs):
-    pieces, (own, pair, ranks, adapters, out, out_pair) = refs[:count], refs[count : count + 6]
-    held, total, sems = refs[count + 6 :]
+    pieces, weight, (*start, out, held, total, sems) = refs[:count], refs[count], refs[count + 1 :]
     i = pl.program_id(0)
     copies = [pltpu.make_async_copy(s, held.at[k], sems.at[k]) for k, s in enumerate(pieces)]
 
@@ -171,13 +171,17 @@
     def _():
         for copy in copies:
             copy.start()
-        rank = adapters.shape[1]
-        rows = ranks.shape[0] // BLK
-        width = adapters.shape[2] - out.shape[1]
-        for b in range(BLK):
-            span = slice(b * rows, (b + 1) * rows)
-            out[span, :] = SCALE * jnp.dot(ranks[span, :rank], adapters[b, :, width:], preferred_element_type=F32)
-        total[...] = jnp.zeros_like(total)
+        if start:
+            ranks, adapters, other = start
+            rank = adapters.shape[1]
+            rows = ranks.shape[0] // BLK
+            width = adapters.shape[2] - out.shape[1]
+            for b in range(BLK):
+                span = slice(b * rows, (b + 1) * rows)
+                low = jnp.dot(ranks[span, :rank], adapters[b, :, width:], preferred_element_type=F32)
+                total[span, :] = SCALE * low + other[span, :].astype(F32)
+        else:
+            total[...] = jnp.zeros_like(total)
 
     for k in range(count):
 
@@ -185,52 +189,49 @@
         def _():
             copies[k].wait()
 
-    out[...] += jnp.dot(held[i], own[0], preferred_element_type=F32)
-    total[...] += jnp.dot(held[i], pair[0], preferred_element_type=F32)
+    total[...] += jnp.dot(held[i], weight[0], preferred_element_type=F32)
 
     @pl.when(i == count - 1)
     def _():
-        out_pair[...] = total[...].astype(BF16)
-
-
-def ahead(pieces, weight, pair, ranks, adapters, order):
+        out[...] = total[...].astype(BF16)
+
+
+def ahead(pieces, weight, order, start=()):
     count = len(pieces)
     rows, depth = pieces[0].shape
     wide = weight.shape[2]
-    block = pl.BlockSpec((1, depth, wide), lambda i, order: (order[i], 0, 0))
-    total = pl.BlockSpec((rows, wide), lambda i, order: (0, 0))
+    starts = [pl.BlockSpec(v.shape, lambda i, order, n=v.ndim: (0,) * n) for v in start]
     return pl.pallas_call(
         functools.partial(ahead_kernel, count),
         grid_spec=pltpu.PrefetchScalarGridSpec(
             num_scalar_prefetch=1,
             grid=(count,),
             in_specs=[HBM] * count
-            + [
-                block,
-                block,
-                pl.BlockSpec(ranks.shape, lambda i, order: (0, 0)),
-                pl.BlockSpec(adapters.shape, lambda i, order: (0, 0, 0)),
-            ],
-            out_specs=[total, total],
+            + [pl.BlockSpec((1, depth, wide), lambda i, order: (order[i], 0, 0))]
+            + starts,
+            out_specs=pl.BlockSpec((rows, wide), lambda i, order: (0, 0)),
             scratch_shapes=[
                 pltpu.VMEM((count, rows, depth), BF16),
                 pltpu.VMEM((rows, wide), F32),
                 pltpu.SemaphoreType.DMA((count,)),
             ],
         ),
-        out_shape=[jax.ShapeDtypeStruct((rows, wide), F32), jax.ShapeDtypeStruct((rows, wide), BF16)],
-        compiler_params=params(30),
-        cost_estimate=COST,
-        name="ahead",
-    )(order, *pieces, weight, pair, ranks, adapters)
+        out_shape=jax.ShapeDtypeStruct((rows, wide), BF16),
+        compiler_params=params(24),
+        cost_estimate=COST,
+        name="ahead_own" if start else "ahead_pair",
+    )(order, *pieces, weight, *start)
 
 
 def close_kernel(here, back, fwd, across, ranks, adapters, out):
     rank = adapters.shape[1]
-    width = out.shape[1]
+    rows, width = out.shape
+    each = rows // adapters.shape[0]
     value = here[...].astype(F32) + back[...].astype(F32) + fwd[...].astype(F32) + across[...].astype(F32)
-    low = jnp.dot(ranks[:, rank:], adapters[0, :, :width], preferred_element_type=F32)
-    out[...] = (value + SCALE * low).astype(BF16)
+    for b in range(adapters.shape[0]):
+        span = slice(b * each, (b + 1) * each)
+        low = jnp.dot(ranks[span, rank:], adapters[b, :, :width], preferred_element_type=F32)
+        out[span, :] = (value[span, :] + SCALE * low).astype(BF16)
 
 
 def add_kernel(a0, a1, b0, b1, b2, out_a, out_b):
@@ -309,12 +310,12 @@
     cot_pair = send(cotangent, "core", "c_cot")
     cut = pl.pallas_call(
         cut_kernel,
-        grid=(per_group,),
+        grid=(per_group // 2,),
         in_specs=[
-            pl.BlockSpec((1, GRP, piece, feats), lambda b: (b, 0, 0, 0)),
-            pl.BlockSpec((1, GRP, piece, hidden), lambda b: (b, 0, 0, 0)),
-        ],
-        out_specs=pl.BlockSpec((GRP, 1, piece, both), lambda b: (0, b, 0, 0)),
+            pl.BlockSpec((2, GRP, piece, feats), lambda b: (b, 0, 0, 0)),
+            pl.BlockSpec((2, GRP, piece, hidden), lambda b: (b, 0, 0, 0)),
+        ],
+        out_specs=pl.BlockSpec((GRP, 2, piece, both), lambda b: (0, b, 0, 0)),
         out_shape=piece_shape,
         compiler_params=params(WIDE),
         cost_estimate=COST,
@@ -395,8 +396,8 @@
     r_10 = send(sum_10, "x", "r_10")
     t_xff, sum_0b, sum_10 = lax.optimization_barrier((t_xff, sum_0b, sum_10))
     pieces = (tokens, t_x, t_f, t_b, t_xf, t_xb, t_ff, t_xff)
-    own_sum, pair_sum = ahead(pieces, weight, pair_w, ranks, adapters, order)
-    got, own_sum, pair_sum, r_0b, r_0f, r_10 = lax.optimization_barrier((got, own_sum, pair_sum, r_0b, r_0f, r_10))
+    pair_sum = ahead(pieces, pair_w, order)
+    got, pair_sum, r_0b, r_0f, r_10 = lax.optimization_barrier((got, pair_sum, r_0b, r_0f, r_10))
 
     totals = pl.pallas_call(
         total_kernel,
@@ -410,22 +411,22 @@
         name="total",
     )(slots, got)
     final = exchange(totals)
-    mixed = (own_sum + send(pair_sum, "core", "c_sum").astype(F32)).astype(BF16)
-    step = pl.BlockSpec((block_rows, feats), lambda b: (b, 0))
+    mixed = ahead(pieces, weight, order, (ranks, adapters, send(pair_sum, "core", "c_sum")))
+    step = pl.BlockSpec((2 * block_rows, feats), lambda b: (b, 0))
     token_gradient = pl.pallas_call(
         close_kernel,
-        grid=(BLK,),
+        grid=(BLK // 2,),
         in_specs=[
             step,
             step,
             step,
             step,
-            pl.BlockSpec((block_rows, 2 * rank), lambda b: (b, 0)),
-            pl.BlockSpec((1, rank, both), lambda b: (b, 0, 0)),
-        ],
-        out_specs=pl.BlockSpec((block_rows, feats), lambda b: (b, 0)),
+            pl.BlockSpec((2 * block_rows, 2 * rank), lambda b: (b, 0)),
+            pl.BlockSpec((2, rank, both), lambda b: (b, 0, 0)),
+        ],
+        out_specs=pl.BlockSpec((2 * block_rows, feats), lambda b: (b, 0)),
         out_shape=jax.ShapeDtypeStruct((rows, feats), BF16),
-        compiler_params=params(WIDE),
+        compiler_params=params(40),
         cost_estimate=COST,
         name="close",
     )(g00, r_0b, r_0f, r_10, ranks, adapters)

time: 150 us -> 146 us (0.973)
  starting transfers between devices: 59.1 us -> 54.3 us
  waiting for transfers between devices: 33.5 us -> 28.9 us
  Pallas kernels: 49.1 us -> 53.2 us
  local copies, waits for them, and re-layouts: 3.88 us -> 7.06 us
  other arithmetic: 2.58 us -> 0.99 us
    pallas_call x1 -> x2, Pallas kernels: 13.8 us -> 21.2 us  [ahead(): pl.pallas_call(functools.partial(ahead_kernel, count), grid_spec=pltpu.Pr...]
    all_to_all x4, waiting for transfers between devices: 5.06 us -> 0.01 us  [exchange(): return lax.all_to_all(pieces, 'grp', 0, 0, tiled=True)]
    ppermute x22, starting transfers between devices: 29.9 us -> 25.9 us  [send(): return lax.ppermute(value, 'mem', MOVES[move])]
    pallas_call x2, Pallas kernels: 7.53 us -> 4.33 us  [the longest x1 2.39 us: shards(): pl.pallas_call(close_kernel, grid=(BLK // 2,), in_specs=[step, step, step...]
    unnamed x28 -> x24, local copies, waits for them, and re-layouts: 3.79 us -> 6.98 us
    convert_element_type x1 -> x0, other arithmetic: 2.26 us -> none  [shards(): mixed = (own_sum + send(pair_sum, 'core', 'c_sum').astype(F32)).astype(BF16)]
  transfers between devices with their start and end apart: 26 -> 26, of which waited for: 12 -> 10; matrix products, arithmetic and copies ran while one was open for 2% -> 1% of each run, Pallas kernels for 31% -> 35%
where the time goes in v3:
time: 146 us; the launch traced here: 145 us
  starting transfers between devices  54.3 us (37%)
  Pallas kernels  53.2 us (36%)
  waiting for transfers between devices  28.9 us (20%)
  local copies, waits for them, and re-layouts  7.06 us (5%)
    ppermute x22, waiting for transfers between devices, send(): return lax.ppermute(value, 'mem', MOVES[move])  28.9 us
    all_to_all x4, starting transfers between devices, exchange(): return lax.all_to_all(pieces, 'grp', 0, 0, tiled=True)  28.4 us
    ppermute x22, starting transfers between devices, send(): return lax.ppermute(value, 'mem', MOVES[move])  25.9 us
    pallas_call x2, Pallas kernels, ahead(): pl.pallas_call(functools.partial(ahead_kernel, count), grid_spec=pltpu.Pr...  21.2 us
    pallas_call x1, Pallas kernels, backward(): pl.pallas_call(functools.partial(back_kernel, count), grid_spec=pltpu.Pre...  14.5 us
    unnamed x24, local copies, waits for them, and re-layouts  6.98 us
  transfers between devices with their start and end apart: 26, of which 10 were waited for; matrix products, arithmetic and copies ran while one was open for 1% of the time, Pallas kernels for 35%

profile of v3, /device:TPU:1, one launch (start us, length us, event | category | flops | bytes accessed | tf_op | source)
XLA Modules:
  0.0 145.2 jit_solution(5760390118125886036)
XLA Ops:
  0.6 1.5 %collective-permute-start.4 = (bf16[8192,896]{1,0:T(8,128)(2,1)}, bf16[8192,896]{1,0:T(8,128)(2,1)}, u32[]{:S(2)}, u32[]{:S(2)}) collective-permute-start(bf16[8192,896]{1,0:T(8,128)(2,1)} %param.8), channel_id=1, source_target_pairs={{0,1},{1,0},{2,3},{3,2},{4,5},{5,4},{6,7},{7,6},{8,9},{9,8},{10,11... | collective-permute-start | bytes 44040200 | tf_op jit(solution)/shard_map/w_all/ppermute | solution.py:49
  2.1 1.9 %cut.1 = bf16[8,4,8,1408]{3,2,1,0:T(8,128)(2,1)} custom-call(bf16[4,8,8,512]{3,2,1,0:T(8,128)(2,1)} %bitcast.21, bf16[4,8,8,896]{3,2,1,0:T(8,128)(2,1)} %bitcast.20), custom_call_target="tpu_custom_call" | custom-call | flops 1 | bytes 1 | tf_op jit(solution)/shard_map/cut/pallas_call | solution.py:311
  4.1 7.6 %all-to-all-start = ((bf16[8,4,8,1408]{3,2,1,0:T(8,128)(2,1)}), bf16[8,4,8,1408]{3,2,1,0:T(8,128)(2,1)S(1)}, u32[]{:S(2)}, u32[]{:S(2)}) async-start(bf16[8,4,8,1408]{3,2,1,0:T(8,128)(2,1)} %cut.1), calls=%async_computation | async-start | bytes 1441792 | tf_op jit(solution)/shard_map/all_to_all | solution.py:57
  11.6 1.3 collective-permute-start.2
  12.9 1.5 %collective-permute-start.1 = (bf16[512,512]{1,0:T(8,128)(2,1)}, bf16[512,512]{1,0:T(8,128)(2,1)S(1)}, u32[]{:S(2)}, u32[]{:S(2)}) collective-permute-start(bf16[512,512]{1,0:T(8,128)(2,1)} %refs_0_.3), channel_id=1, source_target_pairs={{0,2},{1,7},{2,4},{3,1},{4,6},{5,3},{6,0},{7,5},{8,10},{9,15},{10,... | collective-permute-start | bytes 1572872 | tf_op jit(solution)/shard_map/t_f/ppermute | solution.py:49
  14.5 0.3 collective-permute-start
  14.8 0.8 collective-permute-start.3
  15.6 0.8 select_reduce_fusion.slots
  16.4 6.9 %collective-permute-done.2.refs_3_ = bf16[512,512]{1,0:T(8,128)(2,1)S(1)} collective-permute-done((bf16[512,512]{1,0:T(8,128)(2,1)}, bf16[512,512]{1,0:T(8,128)(2,1)S(1)}, u32[]{:S(2)}, u32[]{:S(2)}) %collective-permute-start.2) | collective-permute-done | bytes 524320 | tf_op jit(solution)/shard_map/t_b/ppermute | solution.py:49
  23.3 3.4 %collective-permute-done.1.refs_2_ = bf16[512,512]{1,0:T(8,128)(2,1)S(1)} collective-permute-done((bf16[512,512]{1,0:T(8,128)(2,1)}, bf16[512,512]{1,0:T(8,128)(2,1)S(1)}, u32[]{:S(2)}, u32[]{:S(2)}) %collective-permute-start.1) | collective-permute-done | bytes 524320 | tf_op jit(solution)/shard_map/t_f/ppermute | solution.py:49
  26.7 5.4 %collective-permute-done.refs_1_ = bf16[512,512]{1,0:T(8,128)(2,1)} collective-permute-done((bf16[512,512]{1,0:T(8,128)(2,1)}, bf16[512,512]{1,0:T(8,128)(2,1)}, u32[]{:S(2)}, u32[]{:S(2)}) %collective-permute-start) | collective-permute-done | bytes 524320 | tf_op jit(solution)/shard_map/t_x/ppermute | solution.py:49
  32.1 1.6 %pick.1 = bf16[8,4,8,1408]{3,2,1,0:T(8,128)(2,1)} custom-call(s32[32]{0:T(128)S(1)} %select_reduce_fusion.slots, bf16[8,4,8,1408]{3,2,1,0:T(8,128)(2,1)S(1)} %all-to-all-done.got), custom_call_target="tpu_custom_call" | custom-call | flops 1 | bytes 1 | tf_op jit(solution)/shard_map/pick/pallas_call | solution.py:333
  33.7 6.9 %all-to-all-start.1 = ((bf16[8,4,8,1408]{3,2,1,0:T(8,128)(2,1)}), bf16[8,4,8,1408]{3,2,1,0:T(8,128)(2,1)S(1)}, u32[]{:S(2)}, u32[]{:S(2)}) async-start(bf16[8,4,8,1408]{3,2,1,0:T(8,128)(2,1)} %pick.1), calls=%async_computation.1 | async-start | bytes 1441792 | tf_op jit(solution)/shard_map/all_to_all | solution.py:57
  40.6 2.7 %collective-permute-start.5 = (bf16[512,512]{1,0:T(8,128)(2,1)S(1)}, bf16[512,512]{1,0:T(8,128)(2,1)}, u32[]{:S(2)}, u32[]{:S(2)}) collective-permute-start(bf16[512,512]{1,0:T(8,128)(2,1)S(1)} %collective-permute-done.1.refs_2_), channel_id=1, source_target_pairs={{0,2},{1,7},{2,4},{3,1},{4,6},{5,3},{6,0},{7,5},{8,10},{9,15},{10,... | collective-permute-start | bytes 1572872 | tf_op jit(solution)/shard_map/t_ff/ppermute | solution.py:49
  43.4 0.0 collective-permute-start.7
  43.4 2.7 %collective-permute-start.6 = (bf16[512,512]{1,0:T(8,128)(2,1)}, bf16[512,512]{1,0:T(8,128)(2,1)}, u32[]{:S(2)}, u32[]{:S(2)}) collective-permute-start(bf16[512,512]{1,0:T(8,128)(2,1)} %collective-permute-done.refs_1_), channel_id=1, source_target_pairs={{0,2},{1,7},{2,4},{3,1},{4,6},{5,3},{6,0},{7,5},{8,10},{9,15},{10,... | collective-permute-start | bytes 1572872 | tf_op jit(solution)/shard_map/t_xf/ppermute | solution.py:49
  46.0 0.1 stack.35.order
  46.1 0.0 copy-start.3
  46.1 0.9 copy-done.3
  47.1 1.2 copy-done.1
  48.2 1.2 copy-done.4
  49.4 14.5 %backward.1 = (bf16[512,512]{1,0:T(8,128)(2,1)}, bf16[512,512]{1,0:T(8,128)(2,1)}, bf16[512,512]{1,0:T(8,128)(2,1)}, bf16[512,512]{1,0:T(8,128)(2,1)}, bf16[512,...) custom-call(s32[8]{0:T(128)S(1)} %stack.35.order, ...), custom_call_target="tpu_custom_call" | custom-call | flops 1 | bytes 1 | tf_op jit(solution)/shard_map/backward/pallas_call | solution.py:149
  63.9 0.0 collective-permute-done.5.refs_6_
  63.9 0.0 collective-permute-done.6.refs_4_
  63.9 0.0 all-to-all-done.1.got
  64.0 1.4 rank.1
  65.4 0.1 collective-permute-start.8
  65.5 1.5 %collective-permute-done.8 = f32[512,128]{1,0:T(8,128)S(1)} collective-permute-done((f32[512,128]{1,0:T(8,128)S(1)}, f32[512,128]{1,0:T(8,128)S(1)}, u32[]{:S(2)}, u32[]{:S(2)}) %collective-permute-start.8) | collective-permute-done | bytes 262176 | tf_op jit(solution)/shard_map/k_core/ppermute | solution.py:49
  67.0 0.1 collective-permute-start.9
  67.1 1.5 %collective-permute-start.13 = (bf16[512,512]{1,0:T(8,128)(2,1)}, bf16[512,512]{1,0:T(8,128)(2,1)S(1)}, u32[]{:S(2)}, u32[]{:S(2)}) collective-permute-start(bf16[512,512]{1,0:T(8,128)(2,1)} %get-tuple-element.59), channel_id=1, source_target_pairs={{0,8},{1,9},{2,10},{3,11},{4,12},{5,13},{6,14},{7,15},{8,0},{9,1},... | collective-permute-start | bytes 1572872 | tf_op jit(solution)/shard_map/r_12/ppermute | solution.py:49
  68.6 1.8 %collective-permute-start.14 = (bf16[512,512]{1,0:T(8,128)(2,1)}, bf16[512,512]{1,0:T(8,128)(2,1)S(1)}, u32[]{:S(2)}, u32[]{:S(2)}) collective-permute-start(bf16[512,512]{1,0:T(8,128)(2,1)} %collective-permute-done.6.refs_4_), channel_id=1, source_target_pairs={{0,2},{1,7},{2,4},{3,1},{4,6},{5,3},{6,0},{7,5},{8,10},{9,15},{10,... | collective-permute-start | bytes 1572872 | tf_op jit(solution)/shard_map/t_xff/ppermute | solution.py:49
  70.4 1.7 %collective-permute-done.9 = bf16[512,128]{1,0:T(8,128)(2,1)S(1)} collective-permute-done((bf16[512,128]{1,0:T(8,128)(2,1)S(1)}, bf16[512,128]{1,0:T(8,128)(2,1)S(1)}, u32[]{:S(2)}, u32[]{:S(2)}) %collective-permute-start.9) | collective-permute-done | bytes 131104 | tf_op jit(solution)/shard_map/k_x/ppermute | solution.py:49
  72.1 1.7 %collective-permute-start.12 = (bf16[512,128]{1,0:T(8,128)(2,1)S(1)}, bf16[512,128]{1,0:T(8,128)(2,1)S(1)}, u32[]{:S(2)}, u32[]{:S(2)}) collective-permute-start(bf16[512,128]{1,0:T(8,128)(2,1)S(1)} %add_convert_fusion.1), channel_id=1, source_target_pairs={{0,4},{1,5},{2,6},{3,7},{4,0},{5,1},{6,2},{7,3},{8,12},{9,13},{10,... | collective-permute-start | bytes 393224 | tf_op jit(solution)/shard_map/k_far/ppermute | solution.py:49
  73.8 0.5 collective-permute-start.11
  74.4 2.1 %collective-permute-start.10 = (bf16[512,128]{1,0:T(8,128)(2,1)S(1)}, bf16[512,128]{1,0:T(8,128)(2,1)S(1)}, u32[]{:S(2)}, u32[]{:S(2)}) collective-permute-start(bf16[512,128]{1,0:T(8,128)(2,1)S(1)} %add_convert_fusion.1), channel_id=1, source_target_pairs={{0,2},{1,7},{2,4},{3,1},{4,6},{5,3},{6,0},{7,5},{8,10},{9,15},{10,... | collective-permute-start | bytes 393224 | tf_op jit(solution)/shard_map/k_f/ppermute | solution.py:49
  76.5 2.5 %collective-permute-done.12 = bf16[512,128]{1,0:T(8,128)(2,1)S(1)} collective-permute-done((bf16[512,128]{1,0:T(8,128)(2,1)S(1)}, bf16[512,128]{1,0:T(8,128)(2,1)S(1)}, u32[]{:S(2)}, u32[]{:S(2)}) %collective-permute-start.12) | collective-permute-done | bytes 131104 | tf_op jit(solution)/shard_map/k_far/ppermute | solution.py:49
  79.0 1.4 collective-permute-start.16
  80.4 1.0 collective-permute-done.11
  81.4 1.0 collective-permute-start.17
  82.4 0.0 collective-permute-done.10
  82.4 0.1 add_convert_fusion.ranks.refs_9_
  82.5 0.9 collective-permute-done.13.a1
  83.3 0.8 copy-done.11
  84.1 2.1 %add.155 = bf16[512,512]{1,0:T(8,128)(2,1)} custom-call(bf16[512,512]{1,0:T(8,128)(2,1)} %get-tuple-element.67.a0, bf16[512,512]{1,0:T(8,128)(2,1)} %copy-done.11), custom_call_target="tpu_custom_call" | custom-call | flops 1 | bytes 1 | tf_op jit(solution)/shard_map/add/pallas_call | solution.py:264
  86.3 0.3 collective-permute-start.15
  86.6 2.3 %grads.1 = bf16[8,4,8,1408]{3,2,1,0:T(8,128)(2,1)} custom-call(bf16[512,512]{1,0:T(8,128)(2,1)S(1)} %copy-done, bf16[512,896]{1,0:T(8,128)(2,1)S(1)} %copy-done.2, bf16[512,128]{1,0:T(8,128)(2,1)S(1)} %add_convert_fusion.ranks.refs_9_), custom_call_target="tpu_custom_call" | custom-call | flops 1 | bytes 1 | tf_op jit(solution)/shard_map/grads/pallas_call | solution.py:375
  88.8 6.9 %all-to-all-start.2 = ((bf16[8,4,8,1408]{3,2,1,0:T(8,128)(2,1)}), bf16[8,4,8,1408]{3,2,1,0:T(8,128)(2,1)S(1)}, u32[]{:S(2)}, u32[]{:S(2)}) async-start(bf16[8,4,8,1408]{3,2,1,0:T(8,128)(2,1)} %grads.1), calls=%async_computation.2 | async-start | bytes 1441792 | tf_op jit(solution)/shard_map/all_to_all | solution.py:57
  95.8 2.1 %collective-permute-start.19 = (bf16[512,512]{1,0:T(8,128)(2,1)}, bf16[512,512]{1,0:T(8,128)(2,1)S(1)}, u32[]{:S(2)}, u32[]{:S(2)}) collective-permute-start(bf16[512,512]{1,0:T(8,128)(2,1)} %get-tuple-element.75), channel_id=1, source_target_pairs={{0,2},{1,7},{2,4},{3,1},{4,6},{5,3},{6,0},{7,5},{8,10},{9,15},{10,... | collective-permute-start | bytes 1572872 | tf_op jit(solution)/shard_map/r_0f/ppermute | solution.py:49
  97.9 3.9 %collective-permute-done.15.a1 = bf16[512,512]{1,0:T(8,128)(2,1)} collective-permute-done((bf16[512,512]{1,0:T(8,128)(2,1)}, bf16[512,512]{1,0:T(8,128)(2,1)}, u32[]{:S(2)}, u32[]{:S(2)}) %collective-permute-start.15) | collective-permute-done | bytes 524320 | tf_op jit(solution)/shard_map/r_02/ppermute | solution.py:49
  101.8 2.5 %add_both.1 = (bf16[512,512]{1,0:T(8,128)(2,1)}, bf16[512,512]{1,0:T(8,128)(2,1)}) custom-call(bf16[512,512]{1,0:T(8,128)(2,1)} %get-tuple-element.66.a0, bf16[512,512]{1,0:T(8,128)(2,1)} %collective-permute-done.15.a1, bf16[512,512]{1,0:T(8,128)(2,1)} %get-tuple-element.69.b0, bf16[512,512]{1,0:T(8,128)(2,1)} %collective-permute-done.16.b1, ...), custom_call_target="tpu_custom_call" | custom-call | flops 1 | bytes 1 | tf_op jit(solution)/shard_map/add_both/pallas_call | solution.py:245
  104.3 0.1 collective-permute-start.20
  104.4 9.9 %ahead_pair.1 = bf16[512,896]{1,0:T(8,128)(2,1)S(1)} custom-call(s32[8]{0:T(128)S(1)} %stack.35.order, bf16[512,512]{1,0:T(8,128)(2,1)S(1)} %copy-done, bf16[512,512]{1,0:T(8,128)(2,1)} %collective-permute-done.refs_1_, bf16[512,512]{1,0:T(8,128)(2,1)} %copy-done.9, bf16[512,512]{1,0:T(8,128)(2,1)} %copy-done.8, ...), custom_call_target="tpu_custom_call" | custom-call | flops 1 | bytes 1 | tf_op jit(solution)/shard_map/ahead_pair/pallas_call | solution.py:204
  114.3 0.0 collective-permute-done.19.fwd
  114.4 0.8 copy-done.6
  115.1 1.8 %collective-permute-done.18.back = bf16[512,512]{1,0:T(8,128)(2,1)} collective-permute-done((bf16[512,512]{1,0:T(8,128)(2,1)}, bf16[512,512]{1,0:T(8,128)(2,1)}, u32[]{:S(2)}, u32[]{:S(2)}) %collective-permute-start.18) | collective-permute-done | bytes 524320 | tf_op jit(solution)/shard_map/r_0b/ppermute | solution.py:49
  116.9 0.0 collective-permute-done.20.across
  116.9 2.4 %collective-permute-start.21 = (bf16[512,896]{1,0:T(8,128)(2,1)S(1)}, bf16[512,896]{1,0:T(8,128)(2,1)}, u32[]{:S(2)}, u32[]{:S(2)}) collective-permute-start(bf16[512,896]{1,0:T(8,128)(2,1)S(1)} %ahead_pair.1), channel_id=1, source_target_pairs={{0,1},{1,0},{2,3},{3,2},{4,5},{5,4},{6,7},{7,6},{8,9},{9,8},{10,11... | collective-permute-start | bytes 2752520 | tf_op jit(solution)/shard_map/c_sum/ppermute | solution.py:49
  119.3 1.8 %total.1 = bf16[8,4,8,1408]{3,2,1,0:T(8,128)(2,1)} custom-call(s32[32]{0:T(128)S(1)} %select_reduce_fusion.slots, bf16[8,4,8,1408]{3,2,1,0:T(8,128)(2,1)S(1)} %all-to-all-done.2.got), custom_call_target="tpu_custom_call" | custom-call | flops 1 | bytes 1 | tf_op jit(solution)/shard_map/total/pallas_call | solution.py:402
  121.0 7.0 %all-to-all-start.3 = ((bf16[8,4,8,1408]{3,2,1,0:T(8,128)(2,1)}), bf16[8,4,8,1408]{3,2,1,0:T(8,128)(2,1)S(1)}, u32[]{:S(2)}, u32[]{:S(2)}) async-start(bf16[8,4,8,1408]{3,2,1,0:T(8,128)(2,1)} %total.1), calls=%async_computation.3 | async-start | bytes 1441792 | tf_op jit(solution)/shard_map/all_to_all | solution.py:57
  128.0 1.0 copy-done.5
  129.1 1.0 copy-done.7
  130.1 2.4 %close.1 = bf16[512,512]{1,0:T(8,128)(2,1)} custom-call(bf16[512,512]{1,0:T(8,128)(2,1)S(1)} %copy-done.5, bf16[512,512]{1,0:T(8,128)(2,1)} %collective-permute-done.18.back, bf16[512,512]{1,0:T(8,128)(2,1)S(1)} %copy-done.7, bf16[512,512]{1,0:T(8,128)(2,1)} %collective-permute-done.20.across, bf16[512,128]{1,0:T(8,128)(2,1)S(1)} %add_convert_fusion.ranks.refs_9_, ...), custom_call_target="tpu_custom_call" | custom-call | flops 1 | bytes 1 | tf_op jit(solution)/shard_map/close/pallas_call | solution.py:416
  132.5 11.2 %ahead_own.1 = bf16[512,896]{1,0:T(8,128)(2,1)} custom-call(s32[8]{0:T(128)S(1)} %stack.35.order, bf16[512,512]{1,0:T(8,128)(2,1)S(1)} %copy-done, bf16[512,512]{1,0:T(8,128)(2,1)} %collective-permute-done.refs_1_, bf16[512,512]{1,0:T(8,128)(2,1)} %copy-done.9, bf16[512,512]{1,0:T(8,128)(2,1)} %copy-done.8, bf16[512,512]{1,0:T(8,128)(2,1)} %collective-permute-done.6.refs_4_, ...), custom_call_target="tpu_custom_call" | custom-call | flops 1 | bytes 1 | tf_op jit(solution)/shard_map/ahead_own/pallas_call | solution.py:204
  143.7 1.5 %join.1 = (bf16[4,8,8,512]{3,2,1,0:T(8,128)(2,1)}, bf16[4,8,8,896]{3,2,1,0:T(8,128)(2,1)}) custom-call(bf16[8,4,8,1408]{3,2,1,0:T(8,128)(2,1)S(1)} %all-to-all-done.3.got), custom_call_target="tpu_custom_call" | custom-call | flops 1 | bytes 1 | tf_op jit(solution)/shard_map/join/pallas_call | solution.py:434
  (29 shorter events, 0.1 us)
Async XLA Ops:
  0.6 46.4 %collective-permute-start.4 = (bf16[8192,896]{1,0:T(8,128)(2,1)}, bf16[8192,896]{1,0:T(8,128)(2,1)}, u32[]{:S(2)}, u32[]{:S(2)}) collective-permute-start(bf16[8192,896]{1,0:T(8,128)(2,1)} %param.8), channel_id=1, source_target_pairs={{0,1},{1,0},{2,3},{3,2},{4,5},{5,4},{6,7},{7,6},{8,9},{9,8},{10,11... | collective-permute-start | bytes 44040200 | tf_op jit(solution)/shard_map/w_all/ppermute | solution.py:49
  4.1 28.0 %all-to-all-start = ((bf16[8,4,8,1408]{3,2,1,0:T(8,128)(2,1)}), bf16[8,4,8,1408]{3,2,1,0:T(8,128)(2,1)S(1)}, u32[]{:S(2)}, u32[]{:S(2)}) async-start(bf16[8,4,8,1408]{3,2,1,0:T(8,128)(2,1)} %cut.1), calls=%async_computation | async-start | bytes 1441792 | tf_op jit(solution)/shard_map/all_to_all | solution.py:57
  11.6 11.6 %collective-permute-start.2 = (bf16[512,512]{1,0:T(8,128)(2,1)}, bf16[512,512]{1,0:T(8,128)(2,1)S(1)}, u32[]{:S(2)}, u32[]{:S(2)}) collective-permute-start(bf16[512,512]{1,0:T(8,128)(2,1)} %refs_0_.3), channel_id=1, source_target_pairs={{0,6},{1,3},{2,0},{3,5},{4,2},{5,7},{6,4},{7,1},{8,14},{9,11},{10,... | collective-permute-start | bytes 1572872 | tf_op jit(solution)/shard_map/t_b/ppermute | solution.py:49
  12.9 13.7 %collective-permute-start.1 = (bf16[512,512]{1,0:T(8,128)(2,1)}, bf16[512,512]{1,0:T(8,128)(2,1)S(1)}, u32[]{:S(2)}, u32[]{:S(2)}) collective-permute-start(bf16[512,512]{1,0:T(8,128)(2,1)} %refs_0_.3), channel_id=1, source_target_pairs={{0,2},{1,7},{2,4},{3,1},{4,6},{5,3},{6,0},{7,5},{8,10},{9,15},{10,... | collective-permute-start | bytes 1572872 | tf_op jit(solution)/shard_map/t_f/ppermute | solution.py:49
  14.5 17.6 %collective-permute-start = (bf16[512,512]{1,0:T(8,128)(2,1)}, bf16[512,512]{1,0:T(8,128)(2,1)}, u32[]{:S(2)}, u32[]{:S(2)}) collective-permute-start(bf16[512,512]{1,0:T(8,128)(2,1)} %refs_0_.3), channel_id=1, source_target_pairs={{0,8},{1,9},{2,10},{3,11},{4,12},{5,13},{6,14},{7,15},{8,0},{9,1},... | collective-permute-start | bytes 1572872 | tf_op jit(solution)/shard_map/t_x/ppermute | solution.py:49
  14.8 31.4 %collective-permute-start.3 = (bf16[512,896]{1,0:T(8,128)(2,1)}, bf16[512,896]{1,0:T(8,128)(2,1)S(1)}, u32[]{:S(2)}, u32[]{:S(2)}) collective-permute-start(bf16[512,896]{1,0:T(8,128)(2,1)} %cot.5), channel_id=1, source_target_pairs={{0,1},{1,0},{2,3},{3,2},{4,5},{5,4},{6,7},{7,6},{8,9},{9,8},{10,11... | collective-permute-start | bytes 2752520 | tf_op jit(solution)/shard_map/c_cot/ppermute | solution.py:49
  23.3 3.4 %copy-start.8 = (bf16[512,512]{1,0:T(8,128)(2,1)}, bf16[512,512]{1,0:T(8,128)(2,1)S(1)}, u32[]{:S(2)}) copy-start(bf16[512,512]{1,0:T(8,128)(2,1)S(1)} %collective-permute-done.2.refs_3_) | copy-start | bytes 1572868
  26.7 37.2 %copy-start.9 = (bf16[512,512]{1,0:T(8,128)(2,1)}, bf16[512,512]{1,0:T(8,128)(2,1)S(1)}, u32[]{:S(2)}) copy-start(bf16[512,512]{1,0:T(8,128)(2,1)S(1)} %collective-permute-done.1.refs_2_) | copy-start | bytes 1572868
  33.7 30.3 %all-to-all-start.1 = ((bf16[8,4,8,1408]{3,2,1,0:T(8,128)(2,1)}), bf16[8,4,8,1408]{3,2,1,0:T(8,128)(2,1)S(1)}, u32[]{:S(2)}, u32[]{:S(2)}) async-start(bf16[8,4,8,1408]{3,2,1,0:T(8,128)(2,1)} %pick.1), calls=%async_computation.1 | async-start | bytes 1441792 | tf_op jit(solution)/shard_map/all_to_all | solution.py:57
  40.6 23.3 %collective-permute-start.5 = (bf16[512,512]{1,0:T(8,128)(2,1)S(1)}, bf16[512,512]{1,0:T(8,128)(2,1)}, u32[]{:S(2)}, u32[]{:S(2)}) collective-permute-start(bf16[512,512]{1,0:T(8,128)(2,1)S(1)} %collective-permute-done.1.refs_2_), channel_id=1, source_target_pairs={{0,2},{1,7},{2,4},{3,1},{4,6},{5,3},{6,0},{7,5},{8,10},{9,15},{10,... | collective-permute-start | bytes 1572872 | tf_op jit(solution)/shard_map/t_ff/ppermute | solution.py:49
  43.4 20.6 %collective-permute-start.7 = (bf16[512,512]{1,0:T(8,128)(2,1)}, bf16[512,512]{1,0:T(8,128)(2,1)}, u32[]{:S(2)}, u32[]{:S(2)}) collective-permute-start(bf16[512,512]{1,0:T(8,128)(2,1)} %collective-permute-done.refs_1_), channel_id=1, source_target_pairs={{0,6},{1,3},{2,0},{3,5},{4,2},{5,7},{6,4},{7,1},{8,14},{9,11},{10,... | collective-permute-start | bytes 1572872 | tf_op jit(solution)/shard_map/t_xb/ppermute | solution.py:49
  43.4 20.6 %collective-permute-start.6 = (bf16[512,512]{1,0:T(8,128)(2,1)}, bf16[512,512]{1,0:T(8,128)(2,1)}, u32[]{:S(2)}, u32[]{:S(2)}) collective-permute-start(bf16[512,512]{1,0:T(8,128)(2,1)} %collective-permute-done.refs_1_), channel_id=1, source_target_pairs={{0,2},{1,7},{2,4},{3,1},{4,6},{5,3},{6,0},{7,5},{8,10},{9,15},{10,... | collective-permute-start | bytes 1572872 | tf_op jit(solution)/shard_map/t_xf/ppermute | solution.py:49
  46.1 0.9 copy-start.3
  47.1 1.2 copy-start.1
  48.2 1.2 copy-start.4
  49.4 14.5 %copy-start = (bf16[512,512]{1,0:T(8,128)(2,1)S(1)}, bf16[512,512]{1,0:T(8,128)(2,1)}, u32[]{:S(2)}) copy-start(bf16[512,512]{1,0:T(8,128)(2,1)} %refs_0_.3) | copy-start | bytes 1572868
  49.4 14.5 %copy-start.2 = (bf16[512,896]{1,0:T(8,128)(2,1)S(1)}, bf16[512,896]{1,0:T(8,128)(2,1)}, u32[]{:S(2)}) copy-start(bf16[512,896]{1,0:T(8,128)(2,1)} %cot.5) | copy-start | bytes 2752516
  65.4 1.6 %collective-permute-start.8 = (f32[512,128]{1,0:T(8,128)S(1)}, f32[512,128]{1,0:T(8,128)S(1)}, u32[]{:S(2)}, u32[]{:S(2)}) collective-permute-start(f32[512,128]{1,0:T(8,128)S(1)} %get-tuple-element.58), channel_id=1, source_target_pairs={{0,1},{1,0},{2,3},{3,2},{4,5},{5,4},{6,7},{7,6},{8,9},{9,8},{10,11... | collective-permute-start | bytes 786440 | tf_op jit(solution)/shard_map/k_core/ppermute | solution.py:49
  67.0 5.0 %collective-permute-start.9 = (bf16[512,128]{1,0:T(8,128)(2,1)S(1)}, bf16[512,128]{1,0:T(8,128)(2,1)S(1)}, u32[]{:S(2)}, u32[]{:S(2)}) collective-permute-start(bf16[512,128]{1,0:T(8,128)(2,1)S(1)} %add_convert_fusion.2), channel_id=1, source_target_pairs={{0,8},{1,9},{2,10},{3,11},{4,12},{5,13},{6,14},{7,15},{8,0},{9,1},... | collective-permute-start | bytes 393224 | tf_op jit(solution)/shard_map/k_x/ppermute | solution.py:49
  67.1 16.2 %collective-permute-start.13 = (bf16[512,512]{1,0:T(8,128)(2,1)}, bf16[512,512]{1,0:T(8,128)(2,1)S(1)}, u32[]{:S(2)}, u32[]{:S(2)}) collective-permute-start(bf16[512,512]{1,0:T(8,128)(2,1)} %get-tuple-element.59), channel_id=1, source_target_pairs={{0,8},{1,9},{2,10},{3,11},{4,12},{5,13},{6,14},{7,15},{8,0},{9,1},... | collective-permute-start | bytes 1572872 | tf_op jit(solution)/shard_map/r_12/ppermute | solution.py:49
  68.6 14.7 %collective-permute-start.14 = (bf16[512,512]{1,0:T(8,128)(2,1)}, bf16[512,512]{1,0:T(8,128)(2,1)S(1)}, u32[]{:S(2)}, u32[]{:S(2)}) collective-permute-start(bf16[512,512]{1,0:T(8,128)(2,1)} %collective-permute-done.6.refs_4_), channel_id=1, source_target_pairs={{0,2},{1,7},{2,4},{3,1},{4,6},{5,3},{6,0},{7,5},{8,10},{9,15},{10,... | collective-permute-start | bytes 1572872 | tf_op jit(solution)/shard_map/t_xff/ppermute | solution.py:49
  72.1 6.9 %collective-permute-start.12 = (bf16[512,128]{1,0:T(8,128)(2,1)S(1)}, bf16[512,128]{1,0:T(8,128)(2,1)S(1)}, u32[]{:S(2)}, u32[]{:S(2)}) collective-permute-start(bf16[512,128]{1,0:T(8,128)(2,1)S(1)} %add_convert_fusion.1), channel_id=1, source_target_pairs={{0,4},{1,5},{2,6},{3,7},{4,0},{5,1},{6,2},{7,3},{8,12},{9,13},{10,... | collective-permute-start | bytes 393224 | tf_op jit(solution)/shard_map/k_far/ppermute | solution.py:49
  73.8 7.6 %collective-permute-start.11 = (bf16[512,128]{1,0:T(8,128)(2,1)S(1)}, bf16[512,128]{1,0:T(8,128)(2,1)S(1)}, u32[]{:S(2)}, u32[]{:S(2)}) collective-permute-start(bf16[512,128]{1,0:T(8,128)(2,1)S(1)} %add_convert_fusion.1), channel_id=1, source_target_pairs={{0,6},{1,3},{2,0},{3,5},{4,2},{5,7},{6,4},{7,1},{8,14},{9,11},{10,... | collective-permute-start | bytes 393224 | tf_op jit(solution)/shard_map/k_b/ppermute | solution.py:49
  74.4 8.0 %collective-permute-start.10 = (bf16[512,128]{1,0:T(8,128)(2,1)S(1)}, bf16[512,128]{1,0:T(8,128)(2,1)S(1)}, u32[]{:S(2)}, u32[]{:S(2)}) collective-permute-start(bf16[512,128]{1,0:T(8,128)(2,1)S(1)} %add_convert_fusion.1), channel_id=1, source_target_pairs={{0,2},{1,7},{2,4},{3,1},{4,6},{5,3},{6,0},{7,5},{8,10},{9,15},{10,... | collective-permute-start | bytes 393224 | tf_op jit(solution)/shard_map/k_f/ppermute | solution.py:49
  79.0 18.9 %collective-permute-start.16 = (bf16[512,512]{1,0:T(8,128)(2,1)}, bf16[512,512]{1,0:T(8,128)(2,1)}, u32[]{:S(2)}, u32[]{:S(2)}) collective-permute-start(bf16[512,512]{1,0:T(8,128)(2,1)} %get-tuple-element.70), channel_id=1, source_target_pairs={{0,6},{1,3},{2,0},{3,5},{4,2},{5,7},{6,4},{7,1},{8,14},{9,11},{10,... | collective-permute-start | bytes 1572872 | tf_op jit(solution)/shard_map/r_1b/ppermute | solution.py:49
  81.4 16.5 %collective-permute-start.17 = (bf16[512,512]{1,0:T(8,128)(2,1)}, bf16[512,512]{1,0:T(8,128)(2,1)}, u32[]{:S(2)}, u32[]{:S(2)}) collective-permute-start(bf16[512,512]{1,0:T(8,128)(2,1)} %get-tuple-element.71), channel_id=1, source_target_pairs={{0,2},{1,7},{2,4},{3,1},{4,6},{5,3},{6,0},{7,5},{8,10},{9,15},{10,... | collective-permute-start | bytes 1572872 | tf_op jit(solution)/shard_map/r_1f/ppermute | solution.py:49
  83.3 0.8 copy-start.11
  84.1 4.7 %copy-start.10 = (bf16[512,512]{1,0:T(8,128)(2,1)}, bf16[512,512]{1,0:T(8,128)(2,1)S(1)}, u32[]{:S(2)}) copy-start(bf16[512,512]{1,0:T(8,128)(2,1)S(1)} %collective-permute-done.14.refs_7_) | copy-start | bytes 1572868
  86.3 15.5 %collective-permute-start.15 = (bf16[512,512]{1,0:T(8,128)(2,1)}, bf16[512,512]{1,0:T(8,128)(2,1)}, u32[]{:S(2)}, u32[]{:S(2)}) collective-permute-start(bf16[512,512]{1,0:T(8,128)(2,1)} %add.155), channel_id=1, source_target_pairs={{0,6},{1,3},{2,0},{3,5},{4,2},{5,7},{6,4},{7,1},{8,14},{9,11},{10,... | collective-permute-start | bytes 1572872 | tf_op jit(solution)/shard_map/r_02/ppermute | solution.py:49
  88.8 26.3 %all-to-all-start.2 = ((bf16[8,4,8,1408]{3,2,1,0:T(8,128)(2,1)}), bf16[8,4,8,1408]{3,2,1,0:T(8,128)(2,1)S(1)}, u32[]{:S(2)}, u32[]{:S(2)}) async-start(bf16[8,4,8,1408]{3,2,1,0:T(8,128)(2,1)} %grads.1), calls=%async_computation.2 | async-start | bytes 1441792 | tf_op jit(solution)/shard_map/all_to_all | solution.py:57
  95.8 18.6 %collective-permute-start.19 = (bf16[512,512]{1,0:T(8,128)(2,1)}, bf16[512,512]{1,0:T(8,128)(2,1)S(1)}, u32[]{:S(2)}, u32[]{:S(2)}) collective-permute-start(bf16[512,512]{1,0:T(8,128)(2,1)} %get-tuple-element.75), channel_id=1, source_target_pairs={{0,2},{1,7},{2,4},{3,1},{4,6},{5,3},{6,0},{7,5},{8,10},{9,15},{10,... | collective-permute-start | bytes 1572872 | tf_op jit(solution)/shard_map/r_0f/ppermute | solution.py:49
  104.3 12.6 %collective-permute-start.18 = (bf16[512,512]{1,0:T(8,128)(2,1)}, bf16[512,512]{1,0:T(8,128)(2,1)}, u32[]{:S(2)}, u32[]{:S(2)}) collective-permute-start(bf16[512,512]{1,0:T(8,128)(2,1)} %get-tuple-element.72), channel_id=1, source_target_pairs={{0,6},{1,3},{2,0},{3,5},{4,2},{5,7},{6,4},{7,1},{8,14},{9,11},{10,... | collective-permute-start | bytes 1572872 | tf_op jit(solution)/shard_map/r_0b/ppermute | solution.py:49
  104.3 12.6 %collective-permute-start.20 = (bf16[512,512]{1,0:T(8,128)(2,1)}, bf16[512,512]{1,0:T(8,128)(2,1)}, u32[]{:S(2)}, u32[]{:S(2)}) collective-permute-start(bf16[512,512]{1,0:T(8,128)(2,1)} %get-tuple-element.73), channel_id=1, source_target_pairs={{0,8},{1,9},{2,10},{3,11},{4,12},{5,13},{6,14},{7,15},{8,0},{9,1},... | collective-permute-start | bytes 1572872 | tf_op jit(solution)/shard_map/r_10/ppermute | solution.py:49
  114.4 0.8 copy-start.6
  116.9 15.6 %collective-permute-start.21 = (bf16[512,896]{1,0:T(8,128)(2,1)S(1)}, bf16[512,896]{1,0:T(8,128)(2,1)}, u32[]{:S(2)}, u32[]{:S(2)}) collective-permute-start(bf16[512,896]{1,0:T(8,128)(2,1)S(1)} %ahead_pair.1), channel_id=1, source_target_pairs={{0,1},{1,0},{2,3},{3,2},{4,5},{5,4},{6,7},{7,6},{8,9},{9,8},{10,11... | collective-permute-start | bytes 2752520 | tf_op jit(solution)/shard_map/c_sum/ppermute | solution.py:49
  121.0 22.7 %all-to-all-start.3 = ((bf16[8,4,8,1408]{3,2,1,0:T(8,128)(2,1)}), bf16[8,4,8,1408]{3,2,1,0:T(8,128)(2,1)S(1)}, u32[]{:S(2)}, u32[]{:S(2)}) async-start(bf16[8,4,8,1408]{3,2,1,0:T(8,128)(2,1)} %total.1), calls=%async_computation.3 | async-start | bytes 1441792 | tf_op jit(solution)/shard_map/all_to_all | solution.py:57
  128.0 1.0 copy-start.5
  129.1 1.0 copy-start.7
